TPU v7x, 256 devices: a whole 4x4x8 slice. The times are simulated.
256 devices in a mesh: seq: 32 (over x, z_lo, core), head: 8 (over y, z_hi).
Axes of the slice: x: 4, y: 4, z: 8 (z_hi: 2, z_lo: 4; z = z_hi * 4 + z_lo), core: 2. Of those that a mesh axis runs over, the one named last changes fastest.
Arguments:
- tokens: bfloat16 [20480, 6144], P('seq'), may hold values from -6 to 6
- w_qkv: bfloat16 [3, 6144, 4096], P(None, 'seq', 'head'), may hold values from -0.07782233 to 0.07782233
- log_decay: float32 [32, 20480], P('head', 'seq'), may hold values from -0.7 to 0, as said below
- gain: float32 [4096], P('head'), may hold values from 0.5 to 1.5
Outputs:
- normed: bfloat16 [20480, 4096], P('seq', 'head')
Inputs may be any that keep to these rules, and one draw needn't show every extreme that they name: `log_decay`: every entry is negative.
All inputs are finite; a program needn't handle non-finite values.
Results may differ from a plain program's by a relative error of at most 0.0061.
Values may be sent and summed in bfloat16 or wider, within the bound.
No kernel may reach another device: no remote copies, remote signals or barrier semaphores. Data moves between devices by JAX's collectives and lax.ppermute only.
A program may use at most 128 MiB of HBM per device.

v0:
```python
import functools

import jax
import jax.numpy as jnp
from jax import lax
from jax.experimental import pallas as pl
from jax.experimental.pallas import tpu as pltpu
from jax.sharding import Mesh, PartitionSpec as P

HEAD_COUNT = 32
DH = 128
TAIL = 16
F32, BF16 = jnp.float32, jnp.bfloat16
NEXT = [(i, (i + 1) % 4) for i in range(4)]
LAST = [(i, (i - 1) % 4) for i in range(4)]
SWAP = [(0, 1), (1, 0)]
VMEM_LIMIT = 20 * 1024 * 1024
PROJECT_LIMIT = 54 * 1024 * 1024


ACROSS = (((1,), (1,)), ((), ()))


def tied(value, *others):
    return lax.optimization_barrier((value, others))[0]


def project_body(groups, chunks, has_acc, index_ref, *refs):
    mine, theirs, weights = refs[:chunks], refs[chunks : 2 * chunks], refs[2 * chunks : 3 * chunks]
    accs, outs = refs[3 * chunks : 3 * chunks + len(groups)], refs[-len(groups) :]
    tile, depth = mine[0].shape
    rows = jnp.concatenate(
        [jnp.concatenate([ref[...] for ref in mine], axis=1), jnp.concatenate([ref[...] for ref in theirs], axis=1)], axis=0
    )
    for g, members in enumerate(groups):
        for n, c in enumerate(members):
            w = jnp.concatenate([ref[c * depth : (c + 1) * depth, :] for ref in weights], axis=0)
            total = jnp.dot(rows, w, preferred_element_type=F32)
            for place in range(2):
                part = total[place * tile : (place + 1) * tile]
                outs[g][place, n] = part + accs[g][place, n] if has_acc else part


def project(index, mine, theirs, weights, accs):
    groups = ((0,), (1, 2))
    rows, width = mine.shape[0], weights[0].shape[1]
    depth = weights[0].shape[0] // 3
    tile, chunks = rows // 4, len(index)
    token_specs = [pl.BlockSpec((tile, depth), functools.partial(lambda n, i, ref: (i, ref[n]), n)) for n in range(chunks)]
    weight_specs = [pl.BlockSpec(part.shape, lambda i, ref: (0, 0)) for part in weights]
    out_specs = [pl.BlockSpec((2, len(g), tile, width), lambda i, ref: (0, 0, i, 0)) for g in groups]
    return pl.pallas_call(
        functools.partial(project_body, groups, chunks, accs is not None),
        out_shape=[jax.ShapeDtypeStruct((2, len(g), rows, width), F32) for g in groups],
        grid_spec=pltpu.PrefetchScalarGridSpec(
            num_scalar_prefetch=1,
            grid=(4,),
            in_specs=token_specs * 2 + weight_specs + (out_specs if accs else []),
            out_specs=out_specs,
        ),
        compiler_params=pltpu.CompilerParams(vmem_limit_bytes=PROJECT_LIMIT),
        cost_estimate=pl.CostEstimate(
            flops=12 * rows * depth * chunks * width, bytes_accessed=4 * rows * depth * chunks, transcendentals=0
        ),
    )(jnp.stack(index), *([mine] * chunks), *([theirs] * chunks), *weights, *(accs or []))


def join(earlier, later):
    return jnp.exp(later[1])[:, None, :] * earlier[0] + later[0], earlier[1] + later[1]


def split(value, count):
    parts = []
    for _ in range(count):
        parts.append(value.astype(BF16).astype(F32))
        value = value - parts[-1]
    return parts


def unpack(ref, mask=None):
    state, total = ref[:, :DH, :].astype(F32), jnp.sum(ref[:, DH:, :].astype(F32), axis=1)
    if mask is not None:
        state, total = state * mask, total * mask
    return state, total


def pack(ref, value):
    ref[:, :DH, :] = value[0].astype(ref.dtype)
    row = lax.broadcasted_iota(jnp.int32, (ref.shape[0], TAIL, DH), 1)
    tail = jnp.zeros(row.shape, F32)
    for n, part in enumerate(split(value[1], 3)):
        tail = jnp.where(row == n, part[:, None, :], tail)
    ref[:, DH:, :] = tail.astype(ref.dtype)


def close_body(place_ref, mine_ref, theirs_ref, b_ref, f_ref, g_ref, acc_ref, decay_ref, kv_ref, chip_ref, sent_ref, first_ref):
    group, rows, depth = chip_ref.shape[0], mine_ref.shape[0], b_ref.shape[0] // 3
    half = f_ref.shape[0]
    second_mine = place_ref[0].astype(F32)
    k_weights = jnp.concatenate([b_ref[depth : 2 * depth, :], f_ref[depth:, :], g_ref[: 2 * depth - half, :]], axis=0)
    v_weights = jnp.concatenate([b_ref[2 * depth :, :], g_ref[2 * depth - half :, :]], axis=0)
    states, totals = [], []
    for place, ref in enumerate((mine_ref, theirs_ref)):
        k = (acc_ref[place, 0] + jnp.dot(ref[...], k_weights, preferred_element_type=F32)).astype(BF16)
        v = (acc_ref[place, 1] + jnp.dot(ref[...], v_weights, preferred_element_type=F32)).astype(BF16)
        kv_ref[place, 0] = k
        kv_ref[place, 1] = v
        total = decay_ref[place, :, rows - 1 :]
        tail = jnp.transpose(jnp.exp(total - decay_ref[place]))
        local = []
        for h in range(group):
            cut = slice(h * DH, (h + 1) * DH)
            keys = (k[:, cut].astype(F32) * tail[:, h : h + 1]).astype(BF16)
            local.append(lax.dot_general(keys, v[:, cut], (((0,), (0,)), ((), ())), preferred_element_type=F32))
        states.append(jnp.stack(local))
        totals.append(jnp.broadcast_to(total[:group], (group, DH)))
    first = [jnp.where(second_mine > 0, v[1], v[0]) for v in (states, totals)]
    second = [jnp.where(second_mine > 0, v[0], v[1]) for v in (states, totals)]
    pack(first_ref, first)
    both = join(first, second)
    pack(chip_ref, both)
    pack(sent_ref, both)


def row_body(z_ref, own_ref, back1, back2, back3, before_ref, row_ref):
    z = z_ref[0]
    backs = [back1, back2, back3]
    before = [unpack(ref, (j + 1 <= z).astype(F32)) for j, ref in enumerate(backs)]
    after = [unpack(ref, (j + 1 > z).astype(F32)) for j, ref in enumerate(backs)]
    prefix = join(join(before[2], before[1]), before[0])
    suffix = join(join(after[2], after[1]), after[0])
    pack(before_ref, prefix)
    pack(row_ref, join(join(prefix, unpack(own_ref)), suffix))


def incoming_body(place_ref, before_ref, first_ref, back1, back2, back3, out_ref):
    rows = join(join(unpack(back3), unpack(back2)), unpack(back1))
    state = join(rows, unpack(before_ref))[0]
    first = unpack(first_ref)
    later = jnp.exp(first[1])[:, None, :] * state + first[0]
    mine_second = place_ref[0].astype(F32)
    for place, value in enumerate(
        (jnp.where(mine_second > 0, later, state), jnp.where(mine_second > 0, state, later))
    ):
        for n, part in enumerate(split(value, 3)):
            out_ref[place, :, n * DH : (n + 1) * DH, :] = part.astype(BF16)


def small_kernel(body, outs, scalar, *args):
    return pl.pallas_call(
        body,
        out_shape=[jax.ShapeDtypeStruct(*out) for out in outs],
        in_specs=[pl.BlockSpec(memory_space=pltpu.SMEM)] + [pl.BlockSpec(memory_space=pltpu.VMEM)] * len(args),
        out_specs=[pl.BlockSpec(memory_space=pltpu.VMEM)] * len(outs),
        compiler_params=pltpu.CompilerParams(vmem_limit_bytes=VMEM_LIMIT),
    )(scalar, *args)


def intra_body(scale, place_ref, mine_ref, theirs_ref, b_ref, f_ref, acc_ref, kv_ref, decay_ref, q_ref, out_ref):
    rows, width, depth = mine_ref.shape[0], b_ref.shape[1], b_ref.shape[0] // 3
    i, j = (lax.broadcasted_iota(jnp.int32, (DH, DH), axis) for axis in range(2))
    weights = jnp.concatenate([b_ref[:depth, :], f_ref[:depth, :]], axis=0)
    for place, ref in enumerate((mine_ref, theirs_ref)):
        whole = (acc_ref[place, 0] + jnp.dot(ref[...], weights, preferred_element_type=F32)).astype(BF16)
        q_ref[place] = whole
        columns = jnp.transpose(decay_ref[place])
        for start in range(0, rows, DH):
            stop = start + DH
            for h in range(width // DH):
                cut = slice(h * DH, (h + 1) * DH)
                q = whole[start:stop, cut]
                column, row = columns[start:stop, h : h + 1], decay_ref[place, h : h + 1, :stop]
                raw = lax.dot_general(q, kv_ref[place, 0, :stop, cut], ACROSS, preferred_element_type=F32) * scale
                gap = jnp.where(i >= j, column - row[:, start:], -1e30)
                scores = (raw[:, start:] * jnp.exp(gap)).astype(BF16)
                if start:
                    border = row[:, start - 1 : start]
                    faded = raw[:, :start] * jnp.exp(column - border) * jnp.exp(border - row[:, :start])
                    scores = jnp.concatenate([faded.astype(BF16), scores], axis=1)
                out_ref[place, start:stop, cut] = jnp.dot(
                    scores, kv_ref[place, 1, :stop, cut], preferred_element_type=F32
                )


def inter_body(scale, q_ref, decay_ref, intra_ref, state_ref, out_ref, square_ref):
    rows, width = q_ref.shape[1:]
    squares = jnp.zeros((8, rows), F32)
    grown = jnp.transpose(jnp.exp(decay_ref[0]) * scale)
    for h in range(width // DH):
        cut = slice(h * DH, (h + 1) * DH)
        q = q_ref[0, :, cut]
        inter = jnp.dot(jnp.concatenate([q] * 3, axis=1), state_ref[0, h], preferred_element_type=F32)
        attended = intra_ref[0, :, cut] + inter * grown[:, h : h + 1]
        out_ref[0, :, cut] = attended
        for part in split(attended * attended, 2):
            squares += lax.dot_general(jnp.ones((8, DH), BF16), part.astype(BF16), ACROSS, preferred_element_type=F32)
    square_ref[0] = squares


def by_place(body, outs, flops, *args):
    def whole(shape):
        return pl.BlockSpec((1,) + shape[1:], lambda a: (a,) + (0,) * (len(shape) - 1))

    return pl.pallas_call(
        functools.partial(body, DH**-0.5),
        out_shape=[jax.ShapeDtypeStruct(shape, F32) for shape in outs],
        grid=(2,),
        in_specs=[whole(arg.shape) for arg in args],
        out_specs=[whole(shape) for shape in outs],
        compiler_params=pltpu.CompilerParams(vmem_limit_bytes=VMEM_LIMIT),
        cost_estimate=pl.CostEstimate(flops=flops, bytes_accessed=4 * 10**6, transcendentals=10**6),
    )(*args)


def on_device(tokens, w_qkv, log_decay, gain):
    rows = tokens.shape[0]
    width = w_qkv.shape[2] // 2
    group = width // DH
    x, z, core = lax.axis_index("x"), lax.axis_index("zl"), lax.axis_index("core")
    place = core.reshape(1)

    def halves(array, axis):
        size = array.shape[axis] // 2
        mine = lax.dynamic_slice_in_dim(array, core * size, size, axis)
        theirs = lax.dynamic_slice_in_dim(array, (1 - core) * size, size, axis)
        return mine, theirs

    kept, sent = halves(w_qkv, 2)
    got = lax.ppermute(sent, "core", SWAP)
    own = jnp.where(core == 0, jnp.concatenate([kept, got], 1), jnp.concatenate([got, kept], 1))
    kept, sent = halves(log_decay, 0)
    decay = jnp.stack([kept, lax.ppermute(tied(sent, own), "core", SWAP)])
    other_tokens = lax.ppermute(tied(tokens, own), "core", SWAP)

    fades = jnp.pad(jnp.cumsum(decay, axis=2), ((0, 0), (0, 8 - group), (0, 0)))

    columns = [x, (x + 3) % 4, (x + 1) % 4, (x + 2) % 4]
    index = [[(4 * c + (z + 4 - d) % 4).astype(jnp.int32) for d in range(4)] for c in columns]
    own_x, right_x, left_x, far_x = index

    def along_z(part):
        return lax.ppermute(part, "zl", NEXT)

    def to_right(part):
        return lax.ppermute(part, "x", NEXT)

    def to_left(part):
        return lax.ppermute(part, "x", LAST)

    def tokens_at(array, chunks):
        return jnp.concatenate([lax.dynamic_slice_in_dim(array, c * depth, depth, 1) for c in chunks], axis=1)

    step = lax.optimization_barrier
    depth = own.shape[1]
    own = own.reshape(-1, width)
    half = own.shape[0] // 2
    a1, r0, l0 = along_z(own), to_right(own), to_left(own)

    a2, r1, l1, f0, g0 = along_z(a1), to_right(a1), to_left(a1), to_right(r0[:half]), to_left(l0[half:])

    held = tied(a2, a1, r0, l0)
    a3, r2, l2 = along_z(held), to_right(held), to_left(held)

    far0 = jnp.concatenate([f0, g0])
    sent_z, sent_x = tied((far0, a3), a2, r1, l1, f0, g0)
    b1, r3, l3 = along_z(sent_z), to_right(sent_x), to_left(sent_x)
    chunks = [own_x[0], own_x[1], right_x[0], left_x[0], own_x[2], right_x[1], left_x[1], far_x[0]]
    acc = project(chunks, tokens, other_tokens, [own, a1, r0, l0, a2, r1, l1, far0], None)
    last = [tokens_at(array, (far_x[2], far_x[3])) for array in (tokens, other_tokens)]

    sent_z, sent_r, sent_l, last = tied((b1, r3, l3, last), a3, r2, l2, acc, fades)
    b2, f3, g3 = along_z(sent_z), to_right(sent_r[:half]), to_left(sent_l[half:])
    chunks = [own_x[3], right_x[2], left_x[2], far_x[1], right_x[3], left_x[3]]
    q_acc, kv_acc = project(chunks, tokens, other_tokens, [a3, r2, l2, b1, r3, l3], acc)
    b2, f3, g3, q_acc, kv_acc = step((b2, f3, g3, q_acc, kv_acc))

    shape = (group, DH + TAIL, DH)
    outs = [((2, 2, rows, width), BF16), (shape, F32), (shape, BF16), (shape, F32)]
    kv, chip, sent, first = small_kernel(close_body, outs, place, *last, b2, f3, g3, kv_acc, fades)
    backs = [lax.ppermute(sent, "zl", [(i, (i + j) % 4) for i in range(4)]) for j in (1, 2, 3)]
    outs = [((2, rows, width), BF16), ((2, rows, width), F32)]
    q, intra = small_kernel(functools.partial(intra_body, DH**-0.5), outs, place, *last, b2, f3, q_acc, kv, fades)
    backs, intra = step((backs, intra))
    before, row = small_kernel(row_body, [(shape, F32), (shape, BF16)], z.reshape(1), chip, *backs)
    backs = [lax.ppermute(row, "x", [(i, i + j) for i in range(4 - j)]) for j in (1, 2, 3)]
    (state,) = small_kernel(incoming_body, [((2, group, 3 * DH, DH), BF16)], place, before, first, *backs)

    attended, squares = by_place(inter_body, [(2, rows, width), (2, 8, rows)], 10**9, q, fades, intra, state)
    squares = squares[:, 0, :]
    got = lax.ppermute(attended[1], "core", SWAP)
    squares = squares + sum(lax.ppermute(squares, "y", [(i, (i + j) % 4) for i in range(4)]) for j in (1, 2, 3))
    summed = squares[0] + lax.ppermute(squares[0], "zh", SWAP) + lax.ppermute(squares[1], "core", SWAP)
    summed = summed + lax.ppermute(squares[1], ("core", "zh"), [(i, 3 - i) for i in range(4)])
    scale = lax.rsqrt(summed / (HEAD_COUNT * DH) + 1e-6)[:, None]
    mine = attended[0]
    whole = jnp.where(core == 0, jnp.concatenate([mine, got], 1), jnp.concatenate([got, mine], 1))
    return (whole * scale * gain[None, :]).astype(BF16)


def solution(mesh):
    fine = Mesh(mesh.devices.reshape(4, 4, 2, 4, 2), ("x", "zl", "core", "y", "zh"))
    seq, head = ("x", "zl", "core"), ("y", "zh")
    return jax.shard_map(
        on_device,
        mesh=fine,
        in_specs=(P(seq, None), P(None, seq, head), P(head, seq), P(head)),
        out_specs=P(seq, head),
        check_vma=False,
    )
```

profile of v0, /device:TPU:24, one launch (start us, length us, event | category | flops | bytes accessed | tf_op | source)
XLA Modules:
  0.0 144.1 jit_solution(3110146245934873803)
XLA Ops:
  0.0 1.1 constant_dynamic-slice_fusion.7
  1.1 0.1 collective-permute-start
  1.2 1.6 %collective-permute-done = bf16[3,192,256]{2,1,0:T(8,128)(2,1)S(1)} collective-permute-done((bf16[3,192,256]{2,1,0:T(8,128)(2,1)S(1)}, bf16[3,192,256]{2,1,0:T(8,128)(2,1)S(1)}, u32[]{:S(2)}, u32[]{:S(2)}) %collective-permute-start) | collective-permute-done | bytes 294944 | tf_op jit(solution)/shard_map/ppermute | solution.py:229
  2.8 0.3 maximum_select_fusion.1
  3.1 0.2 collective-permute-start.13
  3.3 1.9 %collective-permute-start.5 = (bf16[1152,256]{1,0:T(8,128)(2,1)S(1)}, bf16[1152,256]{1,0:T(8,128)(2,1)}, u32[]{:S(2)}, u32[]{:S(2)}) collective-permute-start(bf16[1152,256]{1,0:T(8,128)(2,1)S(1)} %bitcast.27), channel_id=1, source_target_pairs={{0,16},{16,32},{32,48},{48,0},{1,17},{17,33},{33,49},{49,1},{2,18}... | collective-permute-start | bytes 1769480 | tf_op jit(solution)/shard_map/ppermute | solution.py:242
  5.2 1.5 %collective-permute-start.1 = (bf16[1152,256]{1,0:T(8,128)(2,1)S(1)}, bf16[1152,256]{1,0:T(8,128)(2,1)S(1)}, u32[]{:S(2)}, u32[]{:S(2)}) collective-permute-start(bf16[1152,256]{1,0:T(8,128)(2,1)S(1)} %bitcast.28), channel_id=1, source_target_pairs={{0,64},{64,128},{128,192},{192,0},{1,65},{65,129},{129,193},{193,1... | collective-permute-start | bytes 1769480 | tf_op jit(solution)/shard_map/ppermute | solution.py:245
  6.7 1.7 %collective-permute-start.3 = (bf16[1152,256]{1,0:T(8,128)(2,1)S(1)}, bf16[1152,256]{1,0:T(8,128)(2,1)}, u32[]{:S(2)}, u32[]{:S(2)}) collective-permute-start(bf16[1152,256]{1,0:T(8,128)(2,1)S(1)} %bitcast.29), channel_id=1, source_target_pairs={{0,192},{64,0},{128,64},{192,128},{1,193},{65,1},{129,65},{193,129... | collective-permute-start | bytes 1769480 | tf_op jit(solution)/shard_map/ppermute | solution.py:248
  8.4 13.4 %collective-permute-done.5.refs_17_ = bf16[1152,256]{1,0:T(8,128)(2,1)} collective-permute-done((bf16[1152,256]{1,0:T(8,128)(2,1)S(1)}, bf16[1152,256]{1,0:T(8,128)(2,1)}, u32[]{:S(2)}, u32[]{:S(2)}) %collective-permute-start.5) | collective-permute-done | bytes 589856 | tf_op jit(solution)/shard_map/ppermute | solution.py:242
  21.9 1.3 constant_dynamic-slice_fusion.5
  23.2 0.1 collective-permute-start.16
  23.3 0.8 slice.46
  24.1 1.5 %collective-permute-start.2 = (bf16[576,256]{1,0:T(8,128)(2,1)}, bf16[576,256]{1,0:T(8,128)(2,1)S(1)}, u32[]{:S(2)}, u32[]{:S(2)}) collective-permute-start(bf16[576,256]{1,0:T(8,128)(2,1)} %slice.46), channel_id=1, source_target_pairs={{0,64},{64,128},{128,192},{192,0},{1,65},{65,129},{129,193},{193,1... | collective-permute-start | bytes 884744 | tf_op jit(solution)/shard_map/ppermute | solution.py:245
  25.7 0.6 stack.65.index_ref
  26.3 1.6 %collective-permute-start.8 = (bf16[1152,256]{1,0:T(8,128)(2,1)}, bf16[1152,256]{1,0:T(8,128)(2,1)S(1)}, u32[]{:S(2)}, u32[]{:S(2)}) collective-permute-start(bf16[1152,256]{1,0:T(8,128)(2,1)} %collective-permute-done.5.refs_17_), channel_id=1, source_target_pairs={{0,64},{64,128},{128,192},{192,0},{1,65},{65,129},{129,193},{193,1... | collective-permute-start | bytes 1769480 | tf_op jit(solution)/shard_map/ppermute | solution.py:245
  27.9 1.7 %collective-permute-start.9 = (bf16[1152,256]{1,0:T(8,128)(2,1)}, bf16[1152,256]{1,0:T(8,128)(2,1)S(1)}, u32[]{:S(2)}, u32[]{:S(2)}) collective-permute-start(bf16[1152,256]{1,0:T(8,128)(2,1)} %collective-permute-done.5.refs_17_), channel_id=1, source_target_pairs={{0,192},{64,0},{128,64},{192,128},{1,193},{65,1},{129,65},{193,129... | collective-permute-start | bytes 1769480 | tf_op jit(solution)/shard_map/ppermute | solution.py:248
  29.6 9.4 %collective-permute-done.6.refs_20_ = bf16[1152,256]{1,0:T(8,128)(2,1)} collective-permute-done((bf16[1152,256]{1,0:T(8,128)(2,1)}, bf16[1152,256]{1,0:T(8,128)(2,1)}, u32[]{:S(2)}, u32[]{:S(2)}) %collective-permute-start.6) | collective-permute-done | bytes 589856 | tf_op jit(solution)/shard_map/ppermute | solution.py:242
  39.0 1.2 reduce-window.6
  40.2 0.2 slice_reduce_fusion
  40.3 0.3 reduce-window.9
  40.7 1.0 slice.47
  41.7 2.8 %collective-permute-start.4 = (bf16[576,256]{1,0:T(8,128)(2,1)S(1)}, bf16[576,256]{1,0:T(8,128)(2,1)S(1)}, u32[]{:S(2)}, u32[]{:S(2)}) collective-permute-start(bf16[576,256]{1,0:T(8,128)(2,1)S(1)} %slice.47), channel_id=1, source_target_pairs={{0,192},{64,0},{128,64},{192,128},{1,193},{65,1},{129,65},{193,129... | collective-permute-start | bytes 884744 | tf_op jit(solution)/shard_map/ppermute | solution.py:248
  44.6 5.2 %collective-permute-done.4 = bf16[576,256]{1,0:T(8,128)(2,1)S(1)} collective-permute-done((bf16[576,256]{1,0:T(8,128)(2,1)S(1)}, bf16[576,256]{1,0:T(8,128)(2,1)S(1)}, u32[]{:S(2)}, u32[]{:S(2)}) %collective-permute-start.4) | collective-permute-done | bytes 294944 | tf_op jit(solution)/shard_map/ppermute | solution.py:248
  49.9 1.3 collective-permute-start.14
  51.2 2.6 %collective-permute-start.15 = (bf16[1152,256]{1,0:T(8,128)(2,1)}, bf16[1152,256]{1,0:T(8,128)(2,1)S(1)}, u32[]{:S(2)}, u32[]{:S(2)}) collective-permute-start(bf16[1152,256]{1,0:T(8,128)(2,1)} %collective-permute-done.6.refs_20_), channel_id=1, source_target_pairs={{0,192},{64,0},{128,64},{192,128},{1,193},{65,1},{129,65},{193,129... | collective-permute-start | bytes 1769480 | tf_op jit(solution)/shard_map/ppermute | solution.py:248
  53.8 1.5 %collective-permute-done.7.refs_12_ = bf16[1152,256]{1,0:T(8,128)(2,1)} collective-permute-done((bf16[1152,256]{1,0:T(8,128)(2,1)}, bf16[1152,256]{1,0:T(8,128)(2,1)}, u32[]{:S(2)}, u32[]{:S(2)}) %collective-permute-start.7) | collective-permute-done | bytes 589856 | tf_op jit(solution)/shard_map/ppermute | solution.py:242
  55.3 1.5 %collective-permute-start.11 = (bf16[1152,256]{1,0:T(8,128)(2,1)}, bf16[1152,256]{1,0:T(8,128)(2,1)S(1)}, u32[]{:S(2)}, u32[]{:S(2)}) collective-permute-start(bf16[1152,256]{1,0:T(8,128)(2,1)} %collective-permute-done.7.refs_12_), channel_id=1, source_target_pairs={{0,64},{64,128},{128,192},{192,0},{1,65},{65,129},{129,193},{193,1... | collective-permute-start | bytes 1769480 | tf_op jit(solution)/shard_map/ppermute | solution.py:245
  56.8 1.7 %collective-permute-start.12 = (bf16[1152,256]{1,0:T(8,128)(2,1)}, bf16[1152,256]{1,0:T(8,128)(2,1)}, u32[]{:S(2)}, u32[]{:S(2)}) collective-permute-start(bf16[1152,256]{1,0:T(8,128)(2,1)} %collective-permute-done.7.refs_12_), channel_id=1, source_target_pairs={{0,192},{64,0},{128,64},{192,128},{1,193},{65,1},{129,65},{193,129... | collective-permute-start | bytes 1769480 | tf_op jit(solution)/shard_map/ppermute | solution.py:248
  58.5 1.3 constant_dynamic-slice_fusion.3
  59.9 12.5 %shard_map.46 = (f32[2,1,640,256]{3,2,1,0:T(8,128)}, f32[2,2,640,256]{3,2,1,0:T(8,128)}) custom-call(s32[8]{0:T(128)} %stack.65.index_ref, bf16[640,6144]{1,0:T(8,128)(2,1)} %refs_5_.3, bf16[640,6144]{1,0:T(8,128)(2,1)} %refs_5_.3, bf16[640,6144]{1,0:T(8,128)(2,1)} %refs_5_.3, bf16[640,6144]{1,0:T(8,128)(2,1)} %refs_5_.3, bf16[640,6144]{1,0:T(8,128)(2,1)} %refs_5_.3, ...), custom_call_target="tpu_custom_call" | custom-call | flops 6039797760 | bytes 7864320 | tf_op jit(solution)/shard_map/pallas_call | solution.py:52
  72.5 0.6 collective-permute-done.10.refs_15_
  73.1 5.0 %collective-permute-done.11.refs_16_ = bf16[1152,256]{1,0:T(8,128)(2,1)S(1)} collective-permute-done((bf16[1152,256]{1,0:T(8,128)(2,1)}, bf16[1152,256]{1,0:T(8,128)(2,1)S(1)}, u32[]{:S(2)}, u32[]{:S(2)}) %collective-permute-start.11) | collective-permute-done | bytes 589856 | tf_op jit(solution)/shard_map/ppermute | solution.py:245
  78.1 1.0 collective-permute-start.17
  79.2 0.6 stack.75.index_ref
  79.8 1.2 collective-permute-start.18
  80.9 1.0 slice.40
  81.9 2.2 %collective-permute-start.19 = (bf16[576,256]{1,0:T(8,128)(2,1)S(1)}, bf16[576,256]{1,0:T(8,128)(2,1)S(1)}, u32[]{:S(2)}, u32[]{:S(2)}) collective-permute-start(bf16[576,256]{1,0:T(8,128)(2,1)S(1)} %slice.40), channel_id=1, source_target_pairs={{0,192},{64,0},{128,64},{192,128},{1,193},{65,1},{129,65},{193,129... | collective-permute-start | bytes 884744 | tf_op jit(solution)/shard_map/ppermute | solution.py:248
  84.2 11.0 %shard_map.47 = (f32[2,1,640,256]{3,2,1,0:T(8,128)}, f32[2,2,640,256]{3,2,1,0:T(8,128)}) custom-call(s32[6]{0:T(128)} %stack.75.index_ref, bf16[640,6144]{1,0:T(8,128)(2,1)} %refs_5_.3, bf16[640,6144]{1,0:T(8,128)(2,1)} %refs_5_.3, bf16[640,6144]{1,0:T(8,128)(2,1)} %refs_5_.3, bf16[640,6144]{1,0:T(8,128)(2,1)} %refs_5_.3, bf16[640,6144]{1,0:T(8,128)(2,1)} %refs_5_.3, ...), custom_call_target="tpu_custom_call" | custom-call | flops 4529848320 | bytes 5898240 | tf_op jit(solution)/shard_map/pallas_call | solution.py:52
  95.2 1.7 %copy-done = f32[2,2,640,256]{3,2,1,0:T(8,128)S(1)} copy-done((f32[2,2,640,256]{3,2,1,0:T(8,128)S(1)}, f32[2,2,640,256]{3,2,1,0:T(8,128)}, u32[]{:S(2)}) %copy-start) | copy-done | bytes 2621464
  96.9 1.8 %shard_map.48 = (bf16[2,2,640,256]{3,2,1,0:T(8,128)(2,1)S(1)}, f32[2,144,128]{2,1,0:T(8,128)S(1)}, bf16[2,144,128]{2,1,0:T(8,128)(2,1)S(1)}, f32[2,144,128]{2,1,0:T(8,128)S(1)}) custom-call(s32[1]{0:T(128)} %bitcast.place_ref, bf16[640,768]{1,0:T(8,128)(2,1)S(1)} %pad_maximum_fusion.mine_ref, bf16[640,768]{1,0:T(8,128)(2,1)S(1)} %pad_maximum_fusion.1.theirs_ref, ...), custom_call_target="tpu_custom_call" | custom-call | tf_op jit(solution)/shard_map/pallas_call | solution.py:150
  98.7 2.0 %collective-permute-start.20 = (bf16[2,144,128]{2,1,0:T(8,128)(2,1)S(1)}, bf16[2,144,128]{2,1,0:T(8,128)(2,1)S(1)}, u32[]{:S(2)}, u32[]{:S(2)}) collective-permute-start(bf16[2,144,128]{2,1,0:T(8,128)(2,1)S(1)} %get-tuple-element.59), channel_id=1, source_target_pairs={{0,16},{16,32},{32,48},{48,0},{1,17},{17,33},{33,49},{49,1},{2,18}... | collective-permute-start | bytes 221192 | tf_op jit(solution)/shard_map/ppermute | solution.py:280
  100.7 1.5 %collective-permute-start.21 = (bf16[2,144,128]{2,1,0:T(8,128)(2,1)S(1)}, bf16[2,144,128]{2,1,0:T(8,128)(2,1)S(1)}, u32[]{:S(2)}, u32[]{:S(2)}) collective-permute-start(bf16[2,144,128]{2,1,0:T(8,128)(2,1)S(1)} %get-tuple-element.59), channel_id=1, source_target_pairs={{0,32},{16,48},{32,0},{48,16},{1,33},{17,49},{33,1},{49,17},{2,34}... | collective-permute-start | bytes 221192 | tf_op jit(solution)/shard_map/ppermute | solution.py:280
  102.2 2.2 %collective-permute-start.22 = (bf16[2,144,128]{2,1,0:T(8,128)(2,1)S(1)}, bf16[2,144,128]{2,1,0:T(8,128)(2,1)S(1)}, u32[]{:S(2)}, u32[]{:S(2)}) collective-permute-start(bf16[2,144,128]{2,1,0:T(8,128)(2,1)S(1)} %get-tuple-element.59), channel_id=1, source_target_pairs={{0,48},{16,0},{32,16},{48,32},{1,49},{17,1},{33,17},{49,33},{2,50}... | collective-permute-start | bytes 221192 | tf_op jit(solution)/shard_map/ppermute | solution.py:280
  104.5 4.7 %shard_map.49 = (bf16[2,640,256]{2,1,0:T(8,128)(2,1)S(1)}, f32[2,640,256]{2,1,0:T(8,128)S(1)}) custom-call(s32[1]{0:T(128)} %bitcast.place_ref, bf16[640,768]{1,0:T(8,128)(2,1)S(1)} %pad_maximum_fusion.mine_ref, bf16[640,768]{1,0:T(8,128)(2,1)S(1)} %pad_maximum_fusion.1.theirs_ref, bf16[1152,256]{1,0:T(8,128)(2,1)S(1)} %collective-permute-done.17.b_ref, ...), custom_call_target="tpu_custom_call" | custom-call | tf_op jit(solution)/shard_map/pallas_call | solution.py:150
  109.2 0.1 shard_map.50
  109.4 1.9 %collective-permute-start.23 = (bf16[2,144,128]{2,1,0:T(8,128)(2,1)S(1)}, bf16[2,144,128]{2,1,0:T(8,128)(2,1)S(1)}, u32[]{:S(2)}, u32[]{:S(2)}) collective-permute-start(bf16[2,144,128]{2,1,0:T(8,128)(2,1)S(1)} %get-tuple-element.68), channel_id=1, source_target_pairs={{0,64},{64,128},{128,192},{1,65},{65,129},{129,193},{2,66},{66,130... | collective-permute-start | bytes 221192 | tf_op jit(solution)/shard_map/ppermute | solution.py:285
  111.3 5.3 %collective-permute-start.24 = (bf16[2,144,128]{2,1,0:T(8,128)(2,1)S(1)}, bf16[2,144,128]{2,1,0:T(8,128)(2,1)S(1)}, u32[]{:S(2)}, u32[]{:S(2)}) collective-permute-start(bf16[2,144,128]{2,1,0:T(8,128)(2,1)S(1)} %get-tuple-element.68), channel_id=1, source_target_pairs={{0,128},{64,192},{1,129},{65,193},{2,130},{66,194},{3,131},{67,195... | collective-permute-start | bytes 221192 | tf_op jit(solution)/shard_map/ppermute | solution.py:285
  116.5 1.3 collective-permute-start.25
  117.9 0.6 collective-permute-done.24.back2
  118.5 1.3 collective-permute-done.25.back3
  119.8 0.1 shard_map.51.state_ref
  119.9 2.2 %shard_map.52 = (f32[2,640,256]{2,1,0:T(8,128)S(1)}, f32[2,8,640]{2,1,0:T(8,128)S(1)}) custom-call(bf16[2,640,256]{2,1,0:T(8,128)(2,1)S(1)} %get-tuple-element.58.q_ref, f32[2,8,640]{2,1,0:T(8,128)S(1)} %pad.4.decay_ref, f32[2,640,256]{2,1,0:T(8,128)S(1)} %get-tuple-element.61.intra_ref, bf16[2,2,384,128]{3,2,1,0:T(8,128)(2,1)S(1)} %shard_map.51.state_ref), custom_call_target="tpu_custom_call" | custom-call | flops 1000000000 | bytes 4000000 | tf_op jit(solution)/shard_map/pallas_call | solution.py:204
  122.1 0.1 slice_bitcast_fusion.1
  122.2 0.1 collective-permute-start.26
  122.4 0.3 collective-permute-start.27
  122.7 2.6 %collective-permute-start.28 = (f32[2,640]{1,0:T(2,128)S(1)}, f32[2,640]{1,0:T(2,128)S(1)}, u32[]{:S(2)}, u32[]{:S(2)}) collective-permute-start(f32[2,640]{1,0:T(2,128)S(1)} %bitcast.33), channel_id=1, source_target_pairs={{0,4},{2,6},{4,0},{6,2},{1,5},{3,7},{5,1},{7,3},{8,12},{10,14},{12... | collective-permute-start | bytes 15368 | tf_op jit(solution)/shard_map/ppermute | solution.py:291
  125.3 0.8 collective-permute-done.27
  126.1 1.7 %collective-permute-done.28 = f32[2,640]{1,0:T(2,128)S(1)} collective-permute-done((f32[2,640]{1,0:T(2,128)S(1)}, f32[2,640]{1,0:T(2,128)S(1)}, u32[]{:S(2)}, u32[]{:S(2)}) %collective-permute-start.28) | collective-permute-done | bytes 5152 | tf_op jit(solution)/shard_map/ppermute | solution.py:291
  127.8 2.3 %collective-permute-done.29 = f32[2,640]{1,0:T(2,128)S(1)} collective-permute-done((f32[2,640]{1,0:T(2,128)S(1)}, f32[2,640]{1,0:T(2,128)S(1)}, u32[]{:S(2)}, u32[]{:S(2)}) %collective-permute-start.29) | collective-permute-done | bytes 5152 | tf_op jit(solution)/shard_map/ppermute | solution.py:291
  130.1 6.0 %collective-permute-start.30 = (f32[640]{0:T(1024)S(1)}, f32[640]{0:T(1024)S(1)}, u32[]{:S(2)}, u32[]{:S(2)}) collective-permute-start(f32[640]{0:T(1024)S(1)} %get-tuple-element.71), channel_id=1, source_target_pairs={{0,1},{1,0},{2,3},{3,2},{4,5},{5,4},{6,7},{7,6},{8,9},{9,8},{10,11... | collective-permute-start | bytes 7688 | tf_op jit(solution)/shard_map/ppermute | solution.py:292
  136.1 0.2 collective-permute-start.32
  136.3 1.4 collective-permute-done.30
  137.7 5.3 %collective-permute-done.32 = f32[640]{0:T(1024)S(1)} collective-permute-done((f32[640]{0:T(1024)S(1)}, f32[640]{0:T(1024)S(1)}, u32[]{:S(2)}, u32[]{:S(2)}) %collective-permute-start.32) | collective-permute-done | bytes 2592 | tf_op jit(solution)/shard_map/ppermute | solution.py:293
  143.0 1.0 fusion.2
  (64 shorter events, 0.5 us)
Async XLA Ops:
  0.0 21.9 %copy-start.10 = (f32[4,640]{1,0:T(4,128)S(1)}, f32[4,640]{1,0:T(4,128)}, u32[]{:S(2)}) copy-start(f32[4,640]{1,0:T(4,128)} %param.6) | copy-start | bytes 30724
  1.1 1.7 %collective-permute-start = (bf16[3,192,256]{2,1,0:T(8,128)(2,1)S(1)}, bf16[3,192,256]{2,1,0:T(8,128)(2,1)S(1)}, u32[]{:S(2)}, u32[]{:S(2)}) collective-permute-start(bf16[3,192,256]{2,1,0:T(8,128)(2,1)S(1)} %get-tuple-element.80), channel_id=1, source_target_pairs={{0,8},{8,0},{1,9},{9,1},{2,10},{10,2},{3,11},{11,3},{4,12},{12,4},... | collective-permute-start | bytes 884744 | tf_op jit(solution)/shard_map/ppermute | solution.py:229
  3.0 21.0 %copy-start.2 = (bf16[3,384,256]{2,1,0:T(8,128)(2,1)}, bf16[3,384,256]{2,1,0:T(8,128)(2,1)S(1)}, u32[]{:S(2)}) copy-start(bf16[3,384,256]{2,1,0:T(8,128)(2,1)S(1)} %maximum_select_fusion.1) | copy-start | bytes 1769476
  3.1 55.5 %collective-permute-start.13 = (bf16[640,6144]{1,0:T(8,128)(2,1)}, bf16[640,6144]{1,0:T(8,128)(2,1)}, u32[]{:S(2)}, u32[]{:S(2)}) collective-permute-start(bf16[640,6144]{1,0:T(8,128)(2,1)} %refs_5_.3), channel_id=1, source_target_pairs={{0,8},{8,0},{1,9},{9,1},{2,10},{10,2},{3,11},{11,3},{4,12},{12,4},... | collective-permute-start | bytes 23592968 | tf_op jit(solution)/shard_map/ppermute | solution.py:233
  3.3 18.6 %collective-permute-start.5 = (bf16[1152,256]{1,0:T(8,128)(2,1)S(1)}, bf16[1152,256]{1,0:T(8,128)(2,1)}, u32[]{:S(2)}, u32[]{:S(2)}) collective-permute-start(bf16[1152,256]{1,0:T(8,128)(2,1)S(1)} %bitcast.27), channel_id=1, source_target_pairs={{0,16},{16,32},{32,48},{48,0},{1,17},{17,33},{33,49},{49,1},{2,18}... | collective-permute-start | bytes 1769480 | tf_op jit(solution)/shard_map/ppermute | solution.py:242
  5.2 18.1 %collective-permute-start.1 = (bf16[1152,256]{1,0:T(8,128)(2,1)S(1)}, bf16[1152,256]{1,0:T(8,128)(2,1)S(1)}, u32[]{:S(2)}, u32[]{:S(2)}) collective-permute-start(bf16[1152,256]{1,0:T(8,128)(2,1)S(1)} %bitcast.28), channel_id=1, source_target_pairs={{0,64},{64,128},{128,192},{192,0},{1,65},{65,129},{129,193},{193,1... | collective-permute-start | bytes 1769480 | tf_op jit(solution)/shard_map/ppermute | solution.py:245
  6.7 21.2 %collective-permute-start.3 = (bf16[1152,256]{1,0:T(8,128)(2,1)S(1)}, bf16[1152,256]{1,0:T(8,128)(2,1)}, u32[]{:S(2)}, u32[]{:S(2)}) collective-permute-start(bf16[1152,256]{1,0:T(8,128)(2,1)S(1)} %bitcast.29), channel_id=1, source_target_pairs={{0,192},{64,0},{128,64},{192,128},{1,193},{65,1},{129,65},{193,129... | collective-permute-start | bytes 1769480 | tf_op jit(solution)/shard_map/ppermute | solution.py:248
  21.9 17.1 %collective-permute-start.6 = (bf16[1152,256]{1,0:T(8,128)(2,1)}, bf16[1152,256]{1,0:T(8,128)(2,1)}, u32[]{:S(2)}, u32[]{:S(2)}) collective-permute-start(bf16[1152,256]{1,0:T(8,128)(2,1)} %collective-permute-done.5.refs_17_), channel_id=1, source_target_pairs={{0,16},{16,32},{32,48},{48,0},{1,17},{17,33},{33,49},{49,1},{2,18}... | collective-permute-start | bytes 1769480 | tf_op jit(solution)/shard_map/ppermute | solution.py:242
  23.2 3.1 %collective-permute-start.16 = (f32[2,640]{1,0:T(2,128)S(1)}, f32[2,640]{1,0:T(2,128)S(1)}, u32[]{:S(2)}, u32[]{:S(2)}) collective-permute-start(f32[2,640]{1,0:T(2,128)S(1)} %get-tuple-element.44), channel_id=1, source_target_pairs={{0,8},{8,0},{1,9},{9,1},{2,10},{10,2},{3,11},{11,3},{4,12},{12,4},... | collective-permute-start | bytes 15368 | tf_op jit(solution)/shard_map/ppermute | solution.py:232
  23.3 2.4 %copy-start.3 = (bf16[1152,256]{1,0:T(8,128)(2,1)}, bf16[1152,256]{1,0:T(8,128)(2,1)S(1)}, u32[]{:S(2)}) copy-start(bf16[1152,256]{1,0:T(8,128)(2,1)S(1)} %collective-permute-done.1.refs_18_) | copy-start | bytes 1769476
  24.1 17.6 %collective-permute-start.2 = (bf16[576,256]{1,0:T(8,128)(2,1)}, bf16[576,256]{1,0:T(8,128)(2,1)S(1)}, u32[]{:S(2)}, u32[]{:S(2)}) collective-permute-start(bf16[576,256]{1,0:T(8,128)(2,1)} %slice.46), channel_id=1, source_target_pairs={{0,64},{64,128},{128,192},{192,0},{1,65},{65,129},{129,193},{193,1... | collective-permute-start | bytes 884744 | tf_op jit(solution)/shard_map/ppermute | solution.py:245
  26.3 24.9 %collective-permute-start.8 = (bf16[1152,256]{1,0:T(8,128)(2,1)}, bf16[1152,256]{1,0:T(8,128)(2,1)S(1)}, u32[]{:S(2)}, u32[]{:S(2)}) collective-permute-start(bf16[1152,256]{1,0:T(8,128)(2,1)} %collective-permute-done.5.refs_17_), channel_id=1, source_target_pairs={{0,64},{64,128},{128,192},{192,0},{1,65},{65,129},{129,193},{193,1... | collective-permute-start | bytes 1769480 | tf_op jit(solution)/shard_map/ppermute | solution.py:245
  27.9 25.9 %collective-permute-start.9 = (bf16[1152,256]{1,0:T(8,128)(2,1)}, bf16[1152,256]{1,0:T(8,128)(2,1)S(1)}, u32[]{:S(2)}, u32[]{:S(2)}) collective-permute-start(bf16[1152,256]{1,0:T(8,128)(2,1)} %collective-permute-done.5.refs_17_), channel_id=1, source_target_pairs={{0,192},{64,0},{128,64},{192,128},{1,193},{65,1},{129,65},{193,129... | collective-permute-start | bytes 1769480 | tf_op jit(solution)/shard_map/ppermute | solution.py:248
  39.0 16.3 %collective-permute-start.7 = (bf16[1152,256]{1,0:T(8,128)(2,1)}, bf16[1152,256]{1,0:T(8,128)(2,1)}, u32[]{:S(2)}, u32[]{:S(2)}) collective-permute-start(bf16[1152,256]{1,0:T(8,128)(2,1)} %collective-permute-done.6.refs_20_), channel_id=1, source_target_pairs={{0,16},{16,32},{32,48},{48,0},{1,17},{17,33},{33,49},{49,1},{2,18}... | collective-permute-start | bytes 1769480 | tf_op jit(solution)/shard_map/ppermute | solution.py:242
  41.7 8.2 %collective-permute-start.4 = (bf16[576,256]{1,0:T(8,128)(2,1)S(1)}, bf16[576,256]{1,0:T(8,128)(2,1)S(1)}, u32[]{:S(2)}, u32[]{:S(2)}) collective-permute-start(bf16[576,256]{1,0:T(8,128)(2,1)S(1)} %slice.47), channel_id=1, source_target_pairs={{0,192},{64,0},{128,64},{192,128},{1,193},{65,1},{129,65},{193,129... | collective-permute-start | bytes 884744 | tf_op jit(solution)/shard_map/ppermute | solution.py:248
  49.9 10.0 %copy-start.4 = (bf16[1152,256]{1,0:T(8,128)(2,1)}, bf16[1152,256]{1,0:T(8,128)(2,1)S(1)}, u32[]{:S(2)}) copy-start(bf16[1152,256]{1,0:T(8,128)(2,1)S(1)} %constant_dynamic-update-slice_fusion.refs_23_) | copy-start | bytes 1769476
  49.9 22.6 %collective-permute-start.14 = (bf16[1152,256]{1,0:T(8,128)(2,1)}, bf16[1152,256]{1,0:T(8,128)(2,1)S(1)}, u32[]{:S(2)}, u32[]{:S(2)}) collective-permute-start(bf16[1152,256]{1,0:T(8,128)(2,1)} %collective-permute-done.6.refs_20_), channel_id=1, source_target_pairs={{0,64},{64,128},{128,192},{192,0},{1,65},{65,129},{129,193},{193,1... | collective-permute-start | bytes 1769480 | tf_op jit(solution)/shard_map/ppermute | solution.py:245
  51.2 8.6 %copy-start.6 = (bf16[1152,256]{1,0:T(8,128)(2,1)}, bf16[1152,256]{1,0:T(8,128)(2,1)S(1)}, u32[]{:S(2)}) copy-start(bf16[1152,256]{1,0:T(8,128)(2,1)S(1)} %collective-permute-done.8.refs_21_) | copy-start | bytes 1769476
  51.2 21.3 %collective-permute-start.15 = (bf16[1152,256]{1,0:T(8,128)(2,1)}, bf16[1152,256]{1,0:T(8,128)(2,1)S(1)}, u32[]{:S(2)}, u32[]{:S(2)}) collective-permute-start(bf16[1152,256]{1,0:T(8,128)(2,1)} %collective-permute-done.6.refs_20_), channel_id=1, source_target_pairs={{0,192},{64,0},{128,64},{192,128},{1,193},{65,1},{129,65},{193,129... | collective-permute-start | bytes 1769480 | tf_op jit(solution)/shard_map/ppermute | solution.py:248
  53.8 6.1 %copy-start.7 = (bf16[1152,256]{1,0:T(8,128)(2,1)}, bf16[1152,256]{1,0:T(8,128)(2,1)S(1)}, u32[]{:S(2)}) copy-start(bf16[1152,256]{1,0:T(8,128)(2,1)S(1)} %collective-permute-done.9.refs_22_) | copy-start | bytes 1769476
  55.3 22.8 %collective-permute-start.11 = (bf16[1152,256]{1,0:T(8,128)(2,1)}, bf16[1152,256]{1,0:T(8,128)(2,1)S(1)}, u32[]{:S(2)}, u32[]{:S(2)}) collective-permute-start(bf16[1152,256]{1,0:T(8,128)(2,1)} %collective-permute-done.7.refs_12_), channel_id=1, source_target_pairs={{0,64},{64,128},{128,192},{192,0},{1,65},{65,129},{129,193},{193,1... | collective-permute-start | bytes 1769480 | tf_op jit(solution)/shard_map/ppermute | solution.py:245
  56.8 21.4 %collective-permute-start.12 = (bf16[1152,256]{1,0:T(8,128)(2,1)}, bf16[1152,256]{1,0:T(8,128)(2,1)}, u32[]{:S(2)}, u32[]{:S(2)}) collective-permute-start(bf16[1152,256]{1,0:T(8,128)(2,1)} %collective-permute-done.7.refs_12_), channel_id=1, source_target_pairs={{0,192},{64,0},{128,64},{192,128},{1,193},{65,1},{129,65},{193,129... | collective-permute-start | bytes 1769480 | tf_op jit(solution)/shard_map/ppermute | solution.py:248
  58.5 14.6 %collective-permute-start.10 = (bf16[1152,256]{1,0:T(8,128)(2,1)S(1)}, bf16[1152,256]{1,0:T(8,128)(2,1)}, u32[]{:S(2)}, u32[]{:S(2)}) collective-permute-start(bf16[1152,256]{1,0:T(8,128)(2,1)S(1)} %constant_dynamic-update-slice_fusion.refs_23_), channel_id=1, source_target_pairs={{0,16},{16,32},{32,48},{48,0},{1,17},{17,33},{33,49},{49,1},{2,18}... | collective-permute-start | bytes 1769480 | tf_op jit(solution)/shard_map/ppermute | solution.py:242
  72.5 5.6 %copy-start.8 = (bf16[1152,256]{1,0:T(8,128)(2,1)}, bf16[1152,256]{1,0:T(8,128)(2,1)S(1)}, u32[]{:S(2)}) copy-start(bf16[1152,256]{1,0:T(8,128)(2,1)S(1)} %collective-permute-done.14.refs_13_) | copy-start | bytes 1769476
  72.5 5.6 %copy-start.9 = (bf16[1152,256]{1,0:T(8,128)(2,1)}, bf16[1152,256]{1,0:T(8,128)(2,1)S(1)}, u32[]{:S(2)}) copy-start(bf16[1152,256]{1,0:T(8,128)(2,1)S(1)} %collective-permute-done.15.refs_14_) | copy-start | bytes 1769476
  78.1 6.0 %copy-start.5 = (bf16[1152,256]{1,0:T(8,128)(2,1)}, bf16[1152,256]{1,0:T(8,128)(2,1)S(1)}, u32[]{:S(2)}) copy-start(bf16[1152,256]{1,0:T(8,128)(2,1)S(1)} %collective-permute-done.11.refs_16_) | copy-start | bytes 1769476
  78.1 17.0 %collective-permute-start.17 = (bf16[1152,256]{1,0:T(8,128)(2,1)}, bf16[1152,256]{1,0:T(8,128)(2,1)S(1)}, u32[]{:S(2)}, u32[]{:S(2)}) collective-permute-start(bf16[1152,256]{1,0:T(8,128)(2,1)} %collective-permute-done.10.refs_15_), channel_id=1, source_target_pairs={{0,16},{16,32},{32,48},{48,0},{1,17},{17,33},{33,49},{49,1},{2,18}... | collective-permute-start | bytes 1769480 | tf_op jit(solution)/shard_map/ppermute | solution.py:242
  79.8 15.3 %collective-permute-start.18 = (bf16[576,256]{1,0:T(8,128)(2,1)S(1)}, bf16[576,256]{1,0:T(8,128)(2,1)S(1)}, u32[]{:S(2)}, u32[]{:S(2)}) collective-permute-start(bf16[576,256]{1,0:T(8,128)(2,1)S(1)} %slice.39), channel_id=1, source_target_pairs={{0,64},{64,128},{128,192},{192,0},{1,65},{65,129},{129,193},{193,1... | collective-permute-start | bytes 884744 | tf_op jit(solution)/shard_map/ppermute | solution.py:245
  81.9 13.2 %collective-permute-start.19 = (bf16[576,256]{1,0:T(8,128)(2,1)S(1)}, bf16[576,256]{1,0:T(8,128)(2,1)S(1)}, u32[]{:S(2)}, u32[]{:S(2)}) collective-permute-start(bf16[576,256]{1,0:T(8,128)(2,1)S(1)} %slice.40), channel_id=1, source_target_pairs={{0,192},{64,0},{128,64},{192,128},{1,193},{65,1},{129,65},{193,129... | collective-permute-start | bytes 884744 | tf_op jit(solution)/shard_map/ppermute | solution.py:248
  95.2 1.7 %copy-start = (f32[2,2,640,256]{3,2,1,0:T(8,128)S(1)}, f32[2,2,640,256]{3,2,1,0:T(8,128)}, u32[]{:S(2)}) copy-start(f32[2,2,640,256]{3,2,1,0:T(8,128)} %get-tuple-element.56.acc_ref) | copy-start | bytes 7864324
  96.9 7.6 %copy-start.1 = (f32[2,1,640,256]{3,2,1,0:T(8,128)S(1)}, f32[2,1,640,256]{3,2,1,0:T(8,128)}, u32[]{:S(2)}) copy-start(f32[2,1,640,256]{3,2,1,0:T(8,128)} %get-tuple-element.54.acc_ref) | copy-start | bytes 3932164
  98.7 10.5 %collective-permute-start.20 = (bf16[2,144,128]{2,1,0:T(8,128)(2,1)S(1)}, bf16[2,144,128]{2,1,0:T(8,128)(2,1)S(1)}, u32[]{:S(2)}, u32[]{:S(2)}) collective-permute-start(bf16[2,144,128]{2,1,0:T(8,128)(2,1)S(1)} %get-tuple-element.59), channel_id=1, source_target_pairs={{0,16},{16,32},{32,48},{48,0},{1,17},{17,33},{33,49},{49,1},{2,18}... | collective-permute-start | bytes 221192 | tf_op jit(solution)/shard_map/ppermute | solution.py:280
  100.7 8.5 %collective-permute-start.21 = (bf16[2,144,128]{2,1,0:T(8,128)(2,1)S(1)}, bf16[2,144,128]{2,1,0:T(8,128)(2,1)S(1)}, u32[]{:S(2)}, u32[]{:S(2)}) collective-permute-start(bf16[2,144,128]{2,1,0:T(8,128)(2,1)S(1)} %get-tuple-element.59), channel_id=1, source_target_pairs={{0,32},{16,48},{32,0},{48,16},{1,33},{17,49},{33,1},{49,17},{2,34}... | collective-permute-start | bytes 221192 | tf_op jit(solution)/shard_map/ppermute | solution.py:280
  102.2 7.0 %collective-permute-start.22 = (bf16[2,144,128]{2,1,0:T(8,128)(2,1)S(1)}, bf16[2,144,128]{2,1,0:T(8,128)(2,1)S(1)}, u32[]{:S(2)}, u32[]{:S(2)}) collective-permute-start(bf16[2,144,128]{2,1,0:T(8,128)(2,1)S(1)} %get-tuple-element.59), channel_id=1, source_target_pairs={{0,48},{16,0},{32,16},{48,32},{1,49},{17,1},{33,17},{49,33},{2,50}... | collective-permute-start | bytes 221192 | tf_op jit(solution)/shard_map/ppermute | solution.py:280
  109.4 8.5 %collective-permute-start.23 = (bf16[2,144,128]{2,1,0:T(8,128)(2,1)S(1)}, bf16[2,144,128]{2,1,0:T(8,128)(2,1)S(1)}, u32[]{:S(2)}, u32[]{:S(2)}) collective-permute-start(bf16[2,144,128]{2,1,0:T(8,128)(2,1)S(1)} %get-tuple-element.68), channel_id=1, source_target_pairs={{0,64},{64,128},{128,192},{1,65},{65,129},{129,193},{2,66},{66,130... | collective-permute-start | bytes 221192 | tf_op jit(solution)/shard_map/ppermute | solution.py:285
  111.3 7.2 %collective-permute-start.24 = (bf16[2,144,128]{2,1,0:T(8,128)(2,1)S(1)}, bf16[2,144,128]{2,1,0:T(8,128)(2,1)S(1)}, u32[]{:S(2)}, u32[]{:S(2)}) collective-permute-start(bf16[2,144,128]{2,1,0:T(8,128)(2,1)S(1)} %get-tuple-element.68), channel_id=1, source_target_pairs={{0,128},{64,192},{1,129},{65,193},{2,130},{66,194},{3,131},{67,195... | collective-permute-start | bytes 221192 | tf_op jit(solution)/shard_map/ppermute | solution.py:285
  116.5 3.3 %collective-permute-start.25 = (bf16[2,144,128]{2,1,0:T(8,128)(2,1)S(1)}, bf16[2,144,128]{2,1,0:T(8,128)(2,1)S(1)}, u32[]{:S(2)}, u32[]{:S(2)}) collective-permute-start(bf16[2,144,128]{2,1,0:T(8,128)(2,1)S(1)} %get-tuple-element.68), channel_id=1, source_target_pairs={{0,192},{1,193},{2,194},{3,195},{4,196},{5,197},{6,198},{7,199},{8... | collective-permute-start | bytes 221192 | tf_op jit(solution)/shard_map/ppermute | solution.py:285
  122.1 20.9 %copy-start.11 = (f32[512]{0:T(512)S(1)}, f32[512]{0:T(512)}, u32[]{:S(2)}) copy-start(f32[512]{0:T(512)} %param.7) | copy-start | bytes 6148
  122.2 20.8 %collective-permute-start.26 = (f32[640,256]{1,0:T(8,128)S(1)}, f32[640,256]{1,0:T(8,128)S(1)}, u32[]{:S(2)}, u32[]{:S(2)}) collective-permute-start(f32[640,256]{1,0:T(8,128)S(1)} %get-tuple-element.78), channel_id=1, source_target_pairs={{0,8},{8,0},{1,9},{9,1},{2,10},{10,2},{3,11},{11,3},{4,12},{12,4},... | collective-permute-start | bytes 1966088 | tf_op jit(solution)/shard_map/ppermute | solution.py:290
  122.4 3.7 %collective-permute-start.27 = (f32[2,640]{1,0:T(2,128)S(1)}, f32[2,640]{1,0:T(2,128)S(1)}, u32[]{:S(2)}, u32[]{:S(2)}) collective-permute-start(f32[2,640]{1,0:T(2,128)S(1)} %bitcast.32), channel_id=1, source_target_pairs={{0,2},{2,4},{4,6},{6,0},{1,3},{3,5},{5,7},{7,1},{8,10},{10,12},{12... | collective-permute-start | bytes 15368 | tf_op jit(solution)/shard_map/ppermute | solution.py:291
  122.7 5.1 %collective-permute-start.28 = (f32[2,640]{1,0:T(2,128)S(1)}, f32[2,640]{1,0:T(2,128)S(1)}, u32[]{:S(2)}, u32[]{:S(2)}) collective-permute-start(f32[2,640]{1,0:T(2,128)S(1)} %bitcast.33), channel_id=1, source_target_pairs={{0,4},{2,6},{4,0},{6,2},{1,5},{3,7},{5,1},{7,3},{8,12},{10,14},{12... | collective-permute-start | bytes 15368 | tf_op jit(solution)/shard_map/ppermute | solution.py:291
  125.3 4.8 %collective-permute-start.29 = (f32[2,640]{1,0:T(2,128)S(1)}, f32[2,640]{1,0:T(2,128)S(1)}, u32[]{:S(2)}, u32[]{:S(2)}) collective-permute-start(f32[2,640]{1,0:T(2,128)S(1)} %bitcast.34), channel_id=1, source_target_pairs={{0,6},{2,0},{4,2},{6,4},{1,7},{3,1},{5,3},{7,5},{8,14},{10,8},{12,... | collective-permute-start | bytes 15368 | tf_op jit(solution)/shard_map/ppermute | solution.py:291
  130.1 7.6 %collective-permute-start.30 = (f32[640]{0:T(1024)S(1)}, f32[640]{0:T(1024)S(1)}, u32[]{:S(2)}, u32[]{:S(2)}) collective-permute-start(f32[640]{0:T(1024)S(1)} %get-tuple-element.71), channel_id=1, source_target_pairs={{0,1},{1,0},{2,3},{3,2},{4,5},{5,4},{6,7},{7,6},{8,9},{9,8},{10,11... | collective-permute-start | bytes 7688 | tf_op jit(solution)/shard_map/ppermute | solution.py:292
  136.1 1.7 %collective-permute-start.31 = (f32[640]{0:T(1024)S(1)}, f32[640]{0:T(1024)S(1)}, u32[]{:S(2)}, u32[]{:S(2)}) collective-permute-start(f32[640]{0:T(1024)S(1)} %get-tuple-element.72), channel_id=1, source_target_pairs={{0,8},{8,0},{1,9},{9,1},{2,10},{10,2},{3,11},{11,3},{4,12},{12,4},... | collective-permute-start | bytes 7688 | tf_op jit(solution)/shard_map/ppermute | solution.py:292
  136.1 6.9 %collective-permute-start.32 = (f32[640]{0:T(1024)S(1)}, f32[640]{0:T(1024)S(1)}, u32[]{:S(2)}, u32[]{:S(2)}) collective-permute-start(f32[640]{0:T(1024)S(1)} %get-tuple-element.72), channel_id=1, source_target_pairs={{0,9},{1,8},{8,1},{9,0},{2,11},{3,10},{10,3},{11,2},{4,13},{5,12},... | collective-permute-start | bytes 7688 | tf_op jit(solution)/shard_map/ppermute | solution.py:293
where the time goes:
time: 146 us; the launch traced here: 144 us
  waiting for transfers between devices  50.2 us (34%)
  starting transfers between devices  48.1 us (33%)
  Pallas kernels  32.5 us (22%)
  local copies, waits for them, and re-layouts  9.81 us (7%)
  other arithmetic  3.06 us (2%)
    ppermute x5, waiting for transfers between devices, along_z(): return lax.ppermute(part, 'zl', NEXT)  24.9 us
    pallas_call x2, Pallas kernels, project(): pl.pallas_call(functools.partial(project_body, groups, chunks, accs is no...  23.5 us
    ppermute x6, starting transfers between devices, to_left(): return lax.ppermute(part, 'x', LAST)  12.9 us
    ppermute x6, starting transfers between devices, to_right(): return lax.ppermute(part, 'x', NEXT)  8.49 us
    ppermute x3, starting transfers between devices, on_device(): lax.ppermute(row, 'x', [(i, i + j) for i in range(4 - j)])  8.44 us
    pallas_call x4, Pallas kernels, small_kernel(): pl.pallas_call(body, out_shape=[jax.ShapeDtypeStruct(*out) for out in out...  6.79 us
    ppermute x1, starting transfers between devices, on_device(): lax.ppermute(squares[0], 'zh', SWAP)  5.95 us
    ppermute x3, starting transfers between devices, on_device(): lax.ppermute(sent, 'zl', [(i, (i + j) % 4) for i in range(4)])  5.76 us
  transfers between devices with their start and end apart: 33, of which 14 were waited for; matrix products, arithmetic and copies ran while one was open for 6% of the time, Pallas kernels for 20%

commit v1 on v0

--- a/solution.py
+++ b/solution.py
@@ -287,10 +287,10 @@
 
     attended, squares = by_place(inter_body, [(2, rows, width), (2, 8, rows)], 10**9, q, fades, intra, state)
     squares = squares[:, 0, :]
-    got = lax.ppermute(attended[1], "core", SWAP)
-    squares = squares + sum(lax.ppermute(squares, "y", [(i, (i + j) % 4) for i in range(4)]) for j in (1, 2, 3))
-    summed = squares[0] + lax.ppermute(squares[0], "zh", SWAP) + lax.ppermute(squares[1], "core", SWAP)
-    summed = summed + lax.ppermute(squares[1], ("core", "zh"), [(i, 3 - i) for i in range(4)])
+    summed = squares[0] + lax.ppermute(squares[1], "core", SWAP)
+    got = lax.ppermute(tied(attended[1], summed), "core", SWAP)
+    summed = summed + sum(lax.ppermute(summed, "y", [(i, (i + j) % 4) for i in range(4)]) for j in (1, 2, 3))
+    summed = summed + lax.ppermute(summed, "zh", SWAP)
     scale = lax.rsqrt(summed / (HEAD_COUNT * DH) + 1e-6)[:, None]
     mine = attended[0]
     whole = jnp.where(core == 0, jnp.concatenate([mine, got], 1), jnp.concatenate([got, mine], 1))

time: 146 us -> 142 us (0.973)
  waiting for transfers between devices: 50.2 us -> 46.1 us
    ppermute x7 -> x6, waiting for transfers between devices: 11.5 us -> 7.45 us  [the longest x3 4.81 us: on_device(): lax.ppermute(summed, 'y', [(i, (i + j) % 4) for i in range(4)])]
    ppermute x7 -> x6, starting transfers between devices: 9.17 us -> 9.01 us  [the longest x1 5.93 us: on_device(): summed = summed + lax.ppermute(summed, 'zh', SWAP)]
  transfers between devices with their start and end apart: 33 -> 32, of which waited for: 14 -> 14; matrix products, arithmetic and copies ran while one was open for 6% -> 6% of each run, Pallas kernels for 20% -> 20%
where the time goes in v1:
time: 142 us; the launch traced here: 140 us
  starting transfers between devices  47.9 us (34%)
  waiting for transfers between devices  46.1 us (32%)
  Pallas kernels  32.5 us (23%)
  local copies, waits for them, and re-layouts  9.9 us (7%)
  other arithmetic  3.06 us (2%)
    ppermute x5, waiting for transfers between devices, along_z(): return lax.ppermute(part, 'zl', NEXT)  24.8 us
    pallas_call x2, Pallas kernels, project(): pl.pallas_call(functools.partial(project_body, groups, chunks, accs is no...  23.5 us
    ppermute x6, starting transfers between devices, to_left(): return lax.ppermute(part, 'x', LAST)  12.9 us
    ppermute x6, starting transfers between devices, to_right(): return lax.ppermute(part, 'x', NEXT)  8.49 us
    ppermute x3, starting transfers between devices, on_device(): lax.ppermute(row, 'x', [(i, i + j) for i in range(4 - j)])  8.44 us
    pallas_call x4, Pallas kernels, small_kernel(): pl.pallas_call(body, out_shape=[jax.ShapeDtypeStruct(*out) for out in out...  6.79 us
    ppermute x1, starting transfers between devices, on_device(): summed = summed + lax.ppermute(summed, 'zh', SWAP)  5.93 us
    ppermute x3, starting transfers between devices, on_device(): lax.ppermute(sent, 'zl', [(i, (i + j) % 4) for i in range(4)])  5.74 us
  transfers between devices with their start and end apart: 32, of which 14 were waited for; matrix products, arithmetic and copies ran while one was open for 6% of the time, Pallas kernels for 20%

profile of v1, /device:TPU:24, one launch (start us, length us, event | category | flops | bytes accessed | tf_op | source)
XLA Modules:
  0.0 139.9 jit_solution(5826045685870619489)
XLA Ops:
  0.0 1.1 constant_dynamic-slice_fusion.7
  1.1 0.1 collective-permute-start
  1.2 1.6 %collective-permute-done = bf16[3,192,256]{2,1,0:T(8,128)(2,1)S(1)} collective-permute-done((bf16[3,192,256]{2,1,0:T(8,128)(2,1)S(1)}, bf16[3,192,256]{2,1,0:T(8,128)(2,1)S(1)}, u32[]{:S(2)}, u32[]{:S(2)}) %collective-permute-start) | collective-permute-done | bytes 294944 | tf_op jit(solution)/shard_map/ppermute | solution.py:229
  2.8 0.3 maximum_select_fusion.1
  3.1 0.2 collective-permute-start.13
  3.3 1.9 %collective-permute-start.5 = (bf16[1152,256]{1,0:T(8,128)(2,1)S(1)}, bf16[1152,256]{1,0:T(8,128)(2,1)}, u32[]{:S(2)}, u32[]{:S(2)}) collective-permute-start(bf16[1152,256]{1,0:T(8,128)(2,1)S(1)} %bitcast.22), channel_id=1, source_target_pairs={{0,16},{16,32},{32,48},{48,0},{1,17},{17,33},{33,49},{49,1},{2,18}... | collective-permute-start | bytes 1769480 | tf_op jit(solution)/shard_map/ppermute | solution.py:242
  5.2 1.5 %collective-permute-start.1 = (bf16[1152,256]{1,0:T(8,128)(2,1)S(1)}, bf16[1152,256]{1,0:T(8,128)(2,1)S(1)}, u32[]{:S(2)}, u32[]{:S(2)}) collective-permute-start(bf16[1152,256]{1,0:T(8,128)(2,1)S(1)} %bitcast.23), channel_id=1, source_target_pairs={{0,64},{64,128},{128,192},{192,0},{1,65},{65,129},{129,193},{193,1... | collective-permute-start | bytes 1769480 | tf_op jit(solution)/shard_map/ppermute | solution.py:245
  6.7 1.7 %collective-permute-start.3 = (bf16[1152,256]{1,0:T(8,128)(2,1)S(1)}, bf16[1152,256]{1,0:T(8,128)(2,1)}, u32[]{:S(2)}, u32[]{:S(2)}) collective-permute-start(bf16[1152,256]{1,0:T(8,128)(2,1)S(1)} %bitcast.24), channel_id=1, source_target_pairs={{0,192},{64,0},{128,64},{192,128},{1,193},{65,1},{129,65},{193,129... | collective-permute-start | bytes 1769480 | tf_op jit(solution)/shard_map/ppermute | solution.py:248
  8.4 13.4 %collective-permute-done.5.refs_17_ = bf16[1152,256]{1,0:T(8,128)(2,1)} collective-permute-done((bf16[1152,256]{1,0:T(8,128)(2,1)S(1)}, bf16[1152,256]{1,0:T(8,128)(2,1)}, u32[]{:S(2)}, u32[]{:S(2)}) %collective-permute-start.5) | collective-permute-done | bytes 589856 | tf_op jit(solution)/shard_map/ppermute | solution.py:242
  21.9 1.3 constant_dynamic-slice_fusion.5
  23.2 0.1 collective-permute-start.16
  23.3 0.8 slice.45
  24.1 1.5 %collective-permute-start.2 = (bf16[576,256]{1,0:T(8,128)(2,1)}, bf16[576,256]{1,0:T(8,128)(2,1)S(1)}, u32[]{:S(2)}, u32[]{:S(2)}) collective-permute-start(bf16[576,256]{1,0:T(8,128)(2,1)} %slice.45), channel_id=1, source_target_pairs={{0,64},{64,128},{128,192},{192,0},{1,65},{65,129},{129,193},{193,1... | collective-permute-start | bytes 884744 | tf_op jit(solution)/shard_map/ppermute | solution.py:245
  25.7 0.6 stack.65.index_ref
  26.4 1.6 %collective-permute-start.8 = (bf16[1152,256]{1,0:T(8,128)(2,1)}, bf16[1152,256]{1,0:T(8,128)(2,1)S(1)}, u32[]{:S(2)}, u32[]{:S(2)}) collective-permute-start(bf16[1152,256]{1,0:T(8,128)(2,1)} %collective-permute-done.5.refs_17_), channel_id=1, source_target_pairs={{0,64},{64,128},{128,192},{192,0},{1,65},{65,129},{129,193},{193,1... | collective-permute-start | bytes 1769480 | tf_op jit(solution)/shard_map/ppermute | solution.py:245
  27.9 1.7 %collective-permute-start.9 = (bf16[1152,256]{1,0:T(8,128)(2,1)}, bf16[1152,256]{1,0:T(8,128)(2,1)S(1)}, u32[]{:S(2)}, u32[]{:S(2)}) collective-permute-start(bf16[1152,256]{1,0:T(8,128)(2,1)} %collective-permute-done.5.refs_17_), channel_id=1, source_target_pairs={{0,192},{64,0},{128,64},{192,128},{1,193},{65,1},{129,65},{193,129... | collective-permute-start | bytes 1769480 | tf_op jit(solution)/shard_map/ppermute | solution.py:248
  29.7 9.3 %collective-permute-done.6.refs_20_ = bf16[1152,256]{1,0:T(8,128)(2,1)} collective-permute-done((bf16[1152,256]{1,0:T(8,128)(2,1)}, bf16[1152,256]{1,0:T(8,128)(2,1)}, u32[]{:S(2)}, u32[]{:S(2)}) %collective-permute-start.6) | collective-permute-done | bytes 589856 | tf_op jit(solution)/shard_map/ppermute | solution.py:242
  39.0 1.2 reduce-window.6
  40.2 0.2 slice_reduce_fusion
  40.3 0.3 reduce-window.9
  40.7 1.0 slice.46
  41.7 2.8 %collective-permute-start.4 = (bf16[576,256]{1,0:T(8,128)(2,1)S(1)}, bf16[576,256]{1,0:T(8,128)(2,1)S(1)}, u32[]{:S(2)}, u32[]{:S(2)}) collective-permute-start(bf16[576,256]{1,0:T(8,128)(2,1)S(1)} %slice.46), channel_id=1, source_target_pairs={{0,192},{64,0},{128,64},{192,128},{1,193},{65,1},{129,65},{193,129... | collective-permute-start | bytes 884744 | tf_op jit(solution)/shard_map/ppermute | solution.py:248
  44.6 5.2 %collective-permute-done.4 = bf16[576,256]{1,0:T(8,128)(2,1)S(1)} collective-permute-done((bf16[576,256]{1,0:T(8,128)(2,1)S(1)}, bf16[576,256]{1,0:T(8,128)(2,1)S(1)}, u32[]{:S(2)}, u32[]{:S(2)}) %collective-permute-start.4) | collective-permute-done | bytes 294944 | tf_op jit(solution)/shard_map/ppermute | solution.py:248
  49.9 1.3 collective-permute-start.14
  51.2 2.6 %collective-permute-start.15 = (bf16[1152,256]{1,0:T(8,128)(2,1)}, bf16[1152,256]{1,0:T(8,128)(2,1)S(1)}, u32[]{:S(2)}, u32[]{:S(2)}) collective-permute-start(bf16[1152,256]{1,0:T(8,128)(2,1)} %collective-permute-done.6.refs_20_), channel_id=1, source_target_pairs={{0,192},{64,0},{128,64},{192,128},{1,193},{65,1},{129,65},{193,129... | collective-permute-start | bytes 1769480 | tf_op jit(solution)/shard_map/ppermute | solution.py:248
  53.8 1.5 %collective-permute-done.7.refs_12_ = bf16[1152,256]{1,0:T(8,128)(2,1)} collective-permute-done((bf16[1152,256]{1,0:T(8,128)(2,1)}, bf16[1152,256]{1,0:T(8,128)(2,1)}, u32[]{:S(2)}, u32[]{:S(2)}) %collective-permute-start.7) | collective-permute-done | bytes 589856 | tf_op jit(solution)/shard_map/ppermute | solution.py:242
  55.3 1.5 %collective-permute-start.11 = (bf16[1152,256]{1,0:T(8,128)(2,1)}, bf16[1152,256]{1,0:T(8,128)(2,1)S(1)}, u32[]{:S(2)}, u32[]{:S(2)}) collective-permute-start(bf16[1152,256]{1,0:T(8,128)(2,1)} %collective-permute-done.7.refs_12_), channel_id=1, source_target_pairs={{0,64},{64,128},{128,192},{192,0},{1,65},{65,129},{129,193},{193,1... | collective-permute-start | bytes 1769480 | tf_op jit(solution)/shard_map/ppermute | solution.py:245
  56.8 1.7 %collective-permute-start.12 = (bf16[1152,256]{1,0:T(8,128)(2,1)}, bf16[1152,256]{1,0:T(8,128)(2,1)}, u32[]{:S(2)}, u32[]{:S(2)}) collective-permute-start(bf16[1152,256]{1,0:T(8,128)(2,1)} %collective-permute-done.7.refs_12_), channel_id=1, source_target_pairs={{0,192},{64,0},{128,64},{192,128},{1,193},{65,1},{129,65},{193,129... | collective-permute-start | bytes 1769480 | tf_op jit(solution)/shard_map/ppermute | solution.py:248
  58.5 1.3 constant_dynamic-slice_fusion.3
  59.9 12.5 %shard_map.46 = (f32[2,1,640,256]{3,2,1,0:T(8,128)}, f32[2,2,640,256]{3,2,1,0:T(8,128)}) custom-call(s32[8]{0:T(128)} %stack.65.index_ref, bf16[640,6144]{1,0:T(8,128)(2,1)} %refs_5_.3, bf16[640,6144]{1,0:T(8,128)(2,1)} %refs_5_.3, bf16[640,6144]{1,0:T(8,128)(2,1)} %refs_5_.3, bf16[640,6144]{1,0:T(8,128)(2,1)} %refs_5_.3, bf16[640,6144]{1,0:T(8,128)(2,1)} %refs_5_.3, ...), custom_call_target="tpu_custom_call" | custom-call | flops 6039797760 | bytes 7864320 | tf_op jit(solution)/shard_map/pallas_call | solution.py:52
  72.5 0.6 collective-permute-done.10.refs_15_
  73.1 5.0 %collective-permute-done.11.refs_16_ = bf16[1152,256]{1,0:T(8,128)(2,1)S(1)} collective-permute-done((bf16[1152,256]{1,0:T(8,128)(2,1)}, bf16[1152,256]{1,0:T(8,128)(2,1)S(1)}, u32[]{:S(2)}, u32[]{:S(2)}) %collective-permute-start.11) | collective-permute-done | bytes 589856 | tf_op jit(solution)/shard_map/ppermute | solution.py:245
  78.1 1.0 collective-permute-start.17
  79.2 0.7 stack.75.index_ref
  79.9 1.2 collective-permute-start.18
  81.0 1.0 slice.40
  82.0 2.2 %collective-permute-start.19 = (bf16[576,256]{1,0:T(8,128)(2,1)S(1)}, bf16[576,256]{1,0:T(8,128)(2,1)S(1)}, u32[]{:S(2)}, u32[]{:S(2)}) collective-permute-start(bf16[576,256]{1,0:T(8,128)(2,1)S(1)} %slice.40), channel_id=1, source_target_pairs={{0,192},{64,0},{128,64},{192,128},{1,193},{65,1},{129,65},{193,129... | collective-permute-start | bytes 884744 | tf_op jit(solution)/shard_map/ppermute | solution.py:248
  84.2 11.0 %shard_map.47 = (f32[2,1,640,256]{3,2,1,0:T(8,128)}, f32[2,2,640,256]{3,2,1,0:T(8,128)}) custom-call(s32[6]{0:T(128)} %stack.75.index_ref, bf16[640,6144]{1,0:T(8,128)(2,1)} %refs_5_.3, bf16[640,6144]{1,0:T(8,128)(2,1)} %refs_5_.3, bf16[640,6144]{1,0:T(8,128)(2,1)} %refs_5_.3, bf16[640,6144]{1,0:T(8,128)(2,1)} %refs_5_.3, bf16[640,6144]{1,0:T(8,128)(2,1)} %refs_5_.3, ...), custom_call_target="tpu_custom_call" | custom-call | flops 4529848320 | bytes 5898240 | tf_op jit(solution)/shard_map/pallas_call | solution.py:52
  95.2 1.7 %copy-done = f32[2,2,640,256]{3,2,1,0:T(8,128)S(1)} copy-done((f32[2,2,640,256]{3,2,1,0:T(8,128)S(1)}, f32[2,2,640,256]{3,2,1,0:T(8,128)}, u32[]{:S(2)}) %copy-start) | copy-done | bytes 2621464
  97.0 1.8 %shard_map.48 = (bf16[2,2,640,256]{3,2,1,0:T(8,128)(2,1)S(1)}, f32[2,144,128]{2,1,0:T(8,128)S(1)}, bf16[2,144,128]{2,1,0:T(8,128)(2,1)S(1)}, f32[2,144,128]{2,1,0:T(8,128)S(1)}) custom-call(s32[1]{0:T(128)} %bitcast.place_ref, bf16[640,768]{1,0:T(8,128)(2,1)S(1)} %pad_maximum_fusion.mine_ref, bf16[640,768]{1,0:T(8,128)(2,1)S(1)} %pad_maximum_fusion.1.theirs_ref, ...), custom_call_target="tpu_custom_call" | custom-call | tf_op jit(solution)/shard_map/pallas_call | solution.py:150
  98.8 2.0 %collective-permute-start.20 = (bf16[2,144,128]{2,1,0:T(8,128)(2,1)S(1)}, bf16[2,144,128]{2,1,0:T(8,128)(2,1)S(1)}, u32[]{:S(2)}, u32[]{:S(2)}) collective-permute-start(bf16[2,144,128]{2,1,0:T(8,128)(2,1)S(1)} %get-tuple-element.60), channel_id=1, source_target_pairs={{0,16},{16,32},{32,48},{48,0},{1,17},{17,33},{33,49},{49,1},{2,18}... | collective-permute-start | bytes 221192 | tf_op jit(solution)/shard_map/ppermute | solution.py:280
  100.8 1.5 %collective-permute-start.21 = (bf16[2,144,128]{2,1,0:T(8,128)(2,1)S(1)}, bf16[2,144,128]{2,1,0:T(8,128)(2,1)S(1)}, u32[]{:S(2)}, u32[]{:S(2)}) collective-permute-start(bf16[2,144,128]{2,1,0:T(8,128)(2,1)S(1)} %get-tuple-element.60), channel_id=1, source_target_pairs={{0,32},{16,48},{32,0},{48,16},{1,33},{17,49},{33,1},{49,17},{2,34}... | collective-permute-start | bytes 221192 | tf_op jit(solution)/shard_map/ppermute | solution.py:280
  102.3 2.2 %collective-permute-start.22 = (bf16[2,144,128]{2,1,0:T(8,128)(2,1)S(1)}, bf16[2,144,128]{2,1,0:T(8,128)(2,1)S(1)}, u32[]{:S(2)}, u32[]{:S(2)}) collective-permute-start(bf16[2,144,128]{2,1,0:T(8,128)(2,1)S(1)} %get-tuple-element.60), channel_id=1, source_target_pairs={{0,48},{16,0},{32,16},{48,32},{1,49},{17,1},{33,17},{49,33},{2,50}... | collective-permute-start | bytes 221192 | tf_op jit(solution)/shard_map/ppermute | solution.py:280
  104.5 4.7 %shard_map.49 = (bf16[2,640,256]{2,1,0:T(8,128)(2,1)S(1)}, f32[2,640,256]{2,1,0:T(8,128)S(1)}) custom-call(s32[1]{0:T(128)} %bitcast.place_ref, bf16[640,768]{1,0:T(8,128)(2,1)S(1)} %pad_maximum_fusion.mine_ref, bf16[640,768]{1,0:T(8,128)(2,1)S(1)} %pad_maximum_fusion.1.theirs_ref, bf16[1152,256]{1,0:T(8,128)(2,1)S(1)} %collective-permute-done.17.b_ref, ...), custom_call_target="tpu_custom_call" | custom-call | tf_op jit(solution)/shard_map/pallas_call | solution.py:150
  109.3 0.1 shard_map.50
  109.4 1.9 %collective-permute-start.23 = (bf16[2,144,128]{2,1,0:T(8,128)(2,1)S(1)}, bf16[2,144,128]{2,1,0:T(8,128)(2,1)S(1)}, u32[]{:S(2)}, u32[]{:S(2)}) collective-permute-start(bf16[2,144,128]{2,1,0:T(8,128)(2,1)S(1)} %get-tuple-element.69), channel_id=1, source_target_pairs={{0,64},{64,128},{128,192},{1,65},{65,129},{129,193},{2,66},{66,130... | collective-permute-start | bytes 221192 | tf_op jit(solution)/shard_map/ppermute | solution.py:285
  111.3 5.3 %collective-permute-start.24 = (bf16[2,144,128]{2,1,0:T(8,128)(2,1)S(1)}, bf16[2,144,128]{2,1,0:T(8,128)(2,1)S(1)}, u32[]{:S(2)}, u32[]{:S(2)}) collective-permute-start(bf16[2,144,128]{2,1,0:T(8,128)(2,1)S(1)} %get-tuple-element.69), channel_id=1, source_target_pairs={{0,128},{64,192},{1,129},{65,193},{2,130},{66,194},{3,131},{67,195... | collective-permute-start | bytes 221192 | tf_op jit(solution)/shard_map/ppermute | solution.py:285
  116.6 1.3 collective-permute-start.25
  117.9 0.6 collective-permute-done.24.back2
  118.6 1.3 collective-permute-done.25.back3
  119.9 0.1 shard_map.51.state_ref
  120.0 2.2 %shard_map.52 = (f32[2,640,256]{2,1,0:T(8,128)S(1)}, f32[2,8,640]{2,1,0:T(8,128)S(1)}) custom-call(bf16[2,640,256]{2,1,0:T(8,128)(2,1)S(1)} %get-tuple-element.59.q_ref, f32[2,8,640]{2,1,0:T(8,128)S(1)} %pad.4.decay_ref, f32[2,640,256]{2,1,0:T(8,128)S(1)} %get-tuple-element.62.intra_ref, bf16[2,2,384,128]{3,2,1,0:T(8,128)(2,1)S(1)} %shard_map.51.state_ref), custom_call_target="tpu_custom_call" | custom-call | flops 1000000000 | bytes 4000000 | tf_op jit(solution)/shard_map/pallas_call | solution.py:204
  122.2 0.1 collective-permute-start.26
  122.4 0.1 slice_bitcast_fusion.1
  122.4 1.0 collective-permute-done.26
  123.5 0.2 collective-permute-start.27
  123.7 0.2 collective-permute-start.28
  123.9 2.6 %collective-permute-start.29 = (f32[640]{0:T(1024)S(1)}, f32[640]{0:T(1024)S(1)}, u32[]{:S(2)}, u32[]{:S(2)}) collective-permute-start(f32[640]{0:T(1024)S(1)} %add.194), channel_id=1, source_target_pairs={{0,4},{2,6},{4,0},{6,2},{1,5},{3,7},{5,1},{7,3},{8,12},{10,14},{12... | collective-permute-start | bytes 7688 | tf_op jit(solution)/shard_map/ppermute | solution.py:292
  126.5 0.8 collective-permute-done.28
  127.3 1.7 %collective-permute-done.29 = f32[640]{0:T(1024)S(1)} collective-permute-done((f32[640]{0:T(1024)S(1)}, f32[640]{0:T(1024)S(1)}, u32[]{:S(2)}, u32[]{:S(2)}) %collective-permute-start.29) | collective-permute-done | bytes 2592 | tf_op jit(solution)/shard_map/ppermute | solution.py:292
  129.0 2.3 %collective-permute-done.30 = f32[640]{0:T(1024)S(1)} collective-permute-done((f32[640]{0:T(1024)S(1)}, f32[640]{0:T(1024)S(1)}, u32[]{:S(2)}, u32[]{:S(2)}) %collective-permute-start.30) | collective-permute-done | bytes 2592 | tf_op jit(solution)/shard_map/ppermute | solution.py:292
  131.3 5.9 %collective-permute-start.31 = (f32[640]{0:T(1024)S(1)}, f32[640]{0:T(1024)S(1)}, u32[]{:S(2)}, u32[]{:S(2)}) collective-permute-start(f32[640]{0:T(1024)S(1)} %add_add_fusion), channel_id=1, source_target_pairs={{0,1},{1,0},{2,3},{3,2},{4,5},{5,4},{6,7},{7,6},{8,9},{9,8},{10,11... | collective-permute-start | bytes 7688 | tf_op jit(solution)/shard_map/ppermute | solution.py:293
  137.2 1.6 %collective-permute-done.31 = f32[640]{0:T(1024)S(1)} collective-permute-done((f32[640]{0:T(1024)S(1)}, f32[640]{0:T(1024)S(1)}, u32[]{:S(2)}, u32[]{:S(2)}) %collective-permute-start.31) | collective-permute-done | bytes 2592 | tf_op jit(solution)/shard_map/ppermute | solution.py:293
  138.8 1.0 fusion.2
  (61 shorter events, 0.5 us)
Async XLA Ops:
  0.0 21.9 %copy-start.10 = (f32[4,640]{1,0:T(4,128)S(1)}, f32[4,640]{1,0:T(4,128)}, u32[]{:S(2)}) copy-start(f32[4,640]{1,0:T(4,128)} %param.6) | copy-start | bytes 30724
  1.1 1.7 %collective-permute-start = (bf16[3,192,256]{2,1,0:T(8,128)(2,1)S(1)}, bf16[3,192,256]{2,1,0:T(8,128)(2,1)S(1)}, u32[]{:S(2)}, u32[]{:S(2)}) collective-permute-start(bf16[3,192,256]{2,1,0:T(8,128)(2,1)S(1)} %get-tuple-element.82), channel_id=1, source_target_pairs={{0,8},{8,0},{1,9},{9,1},{2,10},{10,2},{3,11},{11,3},{4,12},{12,4},... | collective-permute-start | bytes 884744 | tf_op jit(solution)/shard_map/ppermute | solution.py:229
  3.0 21.0 %copy-start.2 = (bf16[3,384,256]{2,1,0:T(8,128)(2,1)}, bf16[3,384,256]{2,1,0:T(8,128)(2,1)S(1)}, u32[]{:S(2)}) copy-start(bf16[3,384,256]{2,1,0:T(8,128)(2,1)S(1)} %maximum_select_fusion.1) | copy-start | bytes 1769476
  3.1 55.5 %collective-permute-start.13 = (bf16[640,6144]{1,0:T(8,128)(2,1)}, bf16[640,6144]{1,0:T(8,128)(2,1)}, u32[]{:S(2)}, u32[]{:S(2)}) collective-permute-start(bf16[640,6144]{1,0:T(8,128)(2,1)} %refs_5_.3), channel_id=1, source_target_pairs={{0,8},{8,0},{1,9},{9,1},{2,10},{10,2},{3,11},{11,3},{4,12},{12,4},... | collective-permute-start | bytes 23592968 | tf_op jit(solution)/shard_map/ppermute | solution.py:233
  3.3 18.6 %collective-permute-start.5 = (bf16[1152,256]{1,0:T(8,128)(2,1)S(1)}, bf16[1152,256]{1,0:T(8,128)(2,1)}, u32[]{:S(2)}, u32[]{:S(2)}) collective-permute-start(bf16[1152,256]{1,0:T(8,128)(2,1)S(1)} %bitcast.22), channel_id=1, source_target_pairs={{0,16},{16,32},{32,48},{48,0},{1,17},{17,33},{33,49},{49,1},{2,18}... | collective-permute-start | bytes 1769480 | tf_op jit(solution)/shard_map/ppermute | solution.py:242
  5.2 18.1 %collective-permute-start.1 = (bf16[1152,256]{1,0:T(8,128)(2,1)S(1)}, bf16[1152,256]{1,0:T(8,128)(2,1)S(1)}, u32[]{:S(2)}, u32[]{:S(2)}) collective-permute-start(bf16[1152,256]{1,0:T(8,128)(2,1)S(1)} %bitcast.23), channel_id=1, source_target_pairs={{0,64},{64,128},{128,192},{192,0},{1,65},{65,129},{129,193},{193,1... | collective-permute-start | bytes 1769480 | tf_op jit(solution)/shard_map/ppermute | solution.py:245
  6.7 21.2 %collective-permute-start.3 = (bf16[1152,256]{1,0:T(8,128)(2,1)S(1)}, bf16[1152,256]{1,0:T(8,128)(2,1)}, u32[]{:S(2)}, u32[]{:S(2)}) collective-permute-start(bf16[1152,256]{1,0:T(8,128)(2,1)S(1)} %bitcast.24), channel_id=1, source_target_pairs={{0,192},{64,0},{128,64},{192,128},{1,193},{65,1},{129,65},{193,129... | collective-permute-start | bytes 1769480 | tf_op jit(solution)/shard_map/ppermute | solution.py:248
  21.9 17.1 %collective-permute-start.6 = (bf16[1152,256]{1,0:T(8,128)(2,1)}, bf16[1152,256]{1,0:T(8,128)(2,1)}, u32[]{:S(2)}, u32[]{:S(2)}) collective-permute-start(bf16[1152,256]{1,0:T(8,128)(2,1)} %collective-permute-done.5.refs_17_), channel_id=1, source_target_pairs={{0,16},{16,32},{32,48},{48,0},{1,17},{17,33},{33,49},{49,1},{2,18}... | collective-permute-start | bytes 1769480 | tf_op jit(solution)/shard_map/ppermute | solution.py:242
  23.2 3.2 %collective-permute-start.16 = (f32[2,640]{1,0:T(2,128)S(1)}, f32[2,640]{1,0:T(2,128)S(1)}, u32[]{:S(2)}, u32[]{:S(2)}) collective-permute-start(f32[2,640]{1,0:T(2,128)S(1)} %get-tuple-element.45), channel_id=1, source_target_pairs={{0,8},{8,0},{1,9},{9,1},{2,10},{10,2},{3,11},{11,3},{4,12},{12,4},... | collective-permute-start | bytes 15368 | tf_op jit(solution)/shard_map/ppermute | solution.py:232
  23.3 2.4 %copy-start.3 = (bf16[1152,256]{1,0:T(8,128)(2,1)}, bf16[1152,256]{1,0:T(8,128)(2,1)S(1)}, u32[]{:S(2)}) copy-start(bf16[1152,256]{1,0:T(8,128)(2,1)S(1)} %collective-permute-done.1.refs_18_) | copy-start | bytes 1769476
  24.1 17.6 %collective-permute-start.2 = (bf16[576,256]{1,0:T(8,128)(2,1)}, bf16[576,256]{1,0:T(8,128)(2,1)S(1)}, u32[]{:S(2)}, u32[]{:S(2)}) collective-permute-start(bf16[576,256]{1,0:T(8,128)(2,1)} %slice.45), channel_id=1, source_target_pairs={{0,64},{64,128},{128,192},{192,0},{1,65},{65,129},{129,193},{193,1... | collective-permute-start | bytes 884744 | tf_op jit(solution)/shard_map/ppermute | solution.py:245
  26.4 24.8 %collective-permute-start.8 = (bf16[1152,256]{1,0:T(8,128)(2,1)}, bf16[1152,256]{1,0:T(8,128)(2,1)S(1)}, u32[]{:S(2)}, u32[]{:S(2)}) collective-permute-start(bf16[1152,256]{1,0:T(8,128)(2,1)} %collective-permute-done.5.refs_17_), channel_id=1, source_target_pairs={{0,64},{64,128},{128,192},{192,0},{1,65},{65,129},{129,193},{193,1... | collective-permute-start | bytes 1769480 | tf_op jit(solution)/shard_map/ppermute | solution.py:245
  27.9 25.9 %collective-permute-start.9 = (bf16[1152,256]{1,0:T(8,128)(2,1)}, bf16[1152,256]{1,0:T(8,128)(2,1)S(1)}, u32[]{:S(2)}, u32[]{:S(2)}) collective-permute-start(bf16[1152,256]{1,0:T(8,128)(2,1)} %collective-permute-done.5.refs_17_), channel_id=1, source_target_pairs={{0,192},{64,0},{128,64},{192,128},{1,193},{65,1},{129,65},{193,129... | collective-permute-start | bytes 1769480 | tf_op jit(solution)/shard_map/ppermute | solution.py:248
  39.0 16.3 %collective-permute-start.7 = (bf16[1152,256]{1,0:T(8,128)(2,1)}, bf16[1152,256]{1,0:T(8,128)(2,1)}, u32[]{:S(2)}, u32[]{:S(2)}) collective-permute-start(bf16[1152,256]{1,0:T(8,128)(2,1)} %collective-permute-done.6.refs_20_), channel_id=1, source_target_pairs={{0,16},{16,32},{32,48},{48,0},{1,17},{17,33},{33,49},{49,1},{2,18}... | collective-permute-start | bytes 1769480 | tf_op jit(solution)/shard_map/ppermute | solution.py:242
  41.7 8.2 %collective-permute-start.4 = (bf16[576,256]{1,0:T(8,128)(2,1)S(1)}, bf16[576,256]{1,0:T(8,128)(2,1)S(1)}, u32[]{:S(2)}, u32[]{:S(2)}) collective-permute-start(bf16[576,256]{1,0:T(8,128)(2,1)S(1)} %slice.46), channel_id=1, source_target_pairs={{0,192},{64,0},{128,64},{192,128},{1,193},{65,1},{129,65},{193,129... | collective-permute-start | bytes 884744 | tf_op jit(solution)/shard_map/ppermute | solution.py:248
  49.9 10.0 %copy-start.4 = (bf16[1152,256]{1,0:T(8,128)(2,1)}, bf16[1152,256]{1,0:T(8,128)(2,1)S(1)}, u32[]{:S(2)}) copy-start(bf16[1152,256]{1,0:T(8,128)(2,1)S(1)} %constant_dynamic-update-slice_fusion.refs_23_) | copy-start | bytes 1769476
  49.9 22.6 %collective-permute-start.14 = (bf16[1152,256]{1,0:T(8,128)(2,1)}, bf16[1152,256]{1,0:T(8,128)(2,1)S(1)}, u32[]{:S(2)}, u32[]{:S(2)}) collective-permute-start(bf16[1152,256]{1,0:T(8,128)(2,1)} %collective-permute-done.6.refs_20_), channel_id=1, source_target_pairs={{0,64},{64,128},{128,192},{192,0},{1,65},{65,129},{129,193},{193,1... | collective-permute-start | bytes 1769480 | tf_op jit(solution)/shard_map/ppermute | solution.py:245
  51.2 8.6 %copy-start.6 = (bf16[1152,256]{1,0:T(8,128)(2,1)}, bf16[1152,256]{1,0:T(8,128)(2,1)S(1)}, u32[]{:S(2)}) copy-start(bf16[1152,256]{1,0:T(8,128)(2,1)S(1)} %collective-permute-done.8.refs_21_) | copy-start | bytes 1769476
  51.2 21.3 %collective-permute-start.15 = (bf16[1152,256]{1,0:T(8,128)(2,1)}, bf16[1152,256]{1,0:T(8,128)(2,1)S(1)}, u32[]{:S(2)}, u32[]{:S(2)}) collective-permute-start(bf16[1152,256]{1,0:T(8,128)(2,1)} %collective-permute-done.6.refs_20_), channel_id=1, source_target_pairs={{0,192},{64,0},{128,64},{192,128},{1,193},{65,1},{129,65},{193,129... | collective-permute-start | bytes 1769480 | tf_op jit(solution)/shard_map/ppermute | solution.py:248
  53.8 6.1 %copy-start.7 = (bf16[1152,256]{1,0:T(8,128)(2,1)}, bf16[1152,256]{1,0:T(8,128)(2,1)S(1)}, u32[]{:S(2)}) copy-start(bf16[1152,256]{1,0:T(8,128)(2,1)S(1)} %collective-permute-done.9.refs_22_) | copy-start | bytes 1769476
  55.3 22.8 %collective-permute-start.11 = (bf16[1152,256]{1,0:T(8,128)(2,1)}, bf16[1152,256]{1,0:T(8,128)(2,1)S(1)}, u32[]{:S(2)}, u32[]{:S(2)}) collective-permute-start(bf16[1152,256]{1,0:T(8,128)(2,1)} %collective-permute-done.7.refs_12_), channel_id=1, source_target_pairs={{0,64},{64,128},{128,192},{192,0},{1,65},{65,129},{129,193},{193,1... | collective-permute-start | bytes 1769480 | tf_op jit(solution)/shard_map/ppermute | solution.py:245
  56.8 21.4 %collective-permute-start.12 = (bf16[1152,256]{1,0:T(8,128)(2,1)}, bf16[1152,256]{1,0:T(8,128)(2,1)}, u32[]{:S(2)}, u32[]{:S(2)}) collective-permute-start(bf16[1152,256]{1,0:T(8,128)(2,1)} %collective-permute-done.7.refs_12_), channel_id=1, source_target_pairs={{0,192},{64,0},{128,64},{192,128},{1,193},{65,1},{129,65},{193,129... | collective-permute-start | bytes 1769480 | tf_op jit(solution)/shard_map/ppermute | solution.py:248
  58.5 14.6 %collective-permute-start.10 = (bf16[1152,256]{1,0:T(8,128)(2,1)S(1)}, bf16[1152,256]{1,0:T(8,128)(2,1)}, u32[]{:S(2)}, u32[]{:S(2)}) collective-permute-start(bf16[1152,256]{1,0:T(8,128)(2,1)S(1)} %constant_dynamic-update-slice_fusion.refs_23_), channel_id=1, source_target_pairs={{0,16},{16,32},{32,48},{48,0},{1,17},{17,33},{33,49},{49,1},{2,18}... | collective-permute-start | bytes 1769480 | tf_op jit(solution)/shard_map/ppermute | solution.py:242
  72.5 5.7 %copy-start.8 = (bf16[1152,256]{1,0:T(8,128)(2,1)}, bf16[1152,256]{1,0:T(8,128)(2,1)S(1)}, u32[]{:S(2)}) copy-start(bf16[1152,256]{1,0:T(8,128)(2,1)S(1)} %collective-permute-done.14.refs_13_) | copy-start | bytes 1769476
  72.5 5.6 %copy-start.9 = (bf16[1152,256]{1,0:T(8,128)(2,1)}, bf16[1152,256]{1,0:T(8,128)(2,1)S(1)}, u32[]{:S(2)}) copy-start(bf16[1152,256]{1,0:T(8,128)(2,1)S(1)} %collective-permute-done.15.refs_14_) | copy-start | bytes 1769476
  78.1 6.1 %copy-start.5 = (bf16[1152,256]{1,0:T(8,128)(2,1)}, bf16[1152,256]{1,0:T(8,128)(2,1)S(1)}, u32[]{:S(2)}) copy-start(bf16[1152,256]{1,0:T(8,128)(2,1)S(1)} %collective-permute-done.11.refs_16_) | copy-start | bytes 1769476
  78.1 17.1 %collective-permute-start.17 = (bf16[1152,256]{1,0:T(8,128)(2,1)}, bf16[1152,256]{1,0:T(8,128)(2,1)S(1)}, u32[]{:S(2)}, u32[]{:S(2)}) collective-permute-start(bf16[1152,256]{1,0:T(8,128)(2,1)} %collective-permute-done.10.refs_15_), channel_id=1, source_target_pairs={{0,16},{16,32},{32,48},{48,0},{1,17},{17,33},{33,49},{49,1},{2,18}... | collective-permute-start | bytes 1769480 | tf_op jit(solution)/shard_map/ppermute | solution.py:242
  79.9 15.3 %collective-permute-start.18 = (bf16[576,256]{1,0:T(8,128)(2,1)S(1)}, bf16[576,256]{1,0:T(8,128)(2,1)S(1)}, u32[]{:S(2)}, u32[]{:S(2)}) collective-permute-start(bf16[576,256]{1,0:T(8,128)(2,1)S(1)} %slice.39), channel_id=1, source_target_pairs={{0,64},{64,128},{128,192},{192,0},{1,65},{65,129},{129,193},{193,1... | collective-permute-start | bytes 884744 | tf_op jit(solution)/shard_map/ppermute | solution.py:245
  82.0 13.2 %collective-permute-start.19 = (bf16[576,256]{1,0:T(8,128)(2,1)S(1)}, bf16[576,256]{1,0:T(8,128)(2,1)S(1)}, u32[]{:S(2)}, u32[]{:S(2)}) collective-permute-start(bf16[576,256]{1,0:T(8,128)(2,1)S(1)} %slice.40), channel_id=1, source_target_pairs={{0,192},{64,0},{128,64},{192,128},{1,193},{65,1},{129,65},{193,129... | collective-permute-start | bytes 884744 | tf_op jit(solution)/shard_map/ppermute | solution.py:248
  95.2 1.7 %copy-start = (f32[2,2,640,256]{3,2,1,0:T(8,128)S(1)}, f32[2,2,640,256]{3,2,1,0:T(8,128)}, u32[]{:S(2)}) copy-start(f32[2,2,640,256]{3,2,1,0:T(8,128)} %get-tuple-element.57.acc_ref) | copy-start | bytes 7864324
  97.0 7.6 %copy-start.1 = (f32[2,1,640,256]{3,2,1,0:T(8,128)S(1)}, f32[2,1,640,256]{3,2,1,0:T(8,128)}, u32[]{:S(2)}) copy-start(f32[2,1,640,256]{3,2,1,0:T(8,128)} %get-tuple-element.55.acc_ref) | copy-start | bytes 3932164
  98.8 10.5 %collective-permute-start.20 = (bf16[2,144,128]{2,1,0:T(8,128)(2,1)S(1)}, bf16[2,144,128]{2,1,0:T(8,128)(2,1)S(1)}, u32[]{:S(2)}, u32[]{:S(2)}) collective-permute-start(bf16[2,144,128]{2,1,0:T(8,128)(2,1)S(1)} %get-tuple-element.60), channel_id=1, source_target_pairs={{0,16},{16,32},{32,48},{48,0},{1,17},{17,33},{33,49},{49,1},{2,18}... | collective-permute-start | bytes 221192 | tf_op jit(solution)/shard_map/ppermute | solution.py:280
  100.8 8.5 %collective-permute-start.21 = (bf16[2,144,128]{2,1,0:T(8,128)(2,1)S(1)}, bf16[2,144,128]{2,1,0:T(8,128)(2,1)S(1)}, u32[]{:S(2)}, u32[]{:S(2)}) collective-permute-start(bf16[2,144,128]{2,1,0:T(8,128)(2,1)S(1)} %get-tuple-element.60), channel_id=1, source_target_pairs={{0,32},{16,48},{32,0},{48,16},{1,33},{17,49},{33,1},{49,17},{2,34}... | collective-permute-start | bytes 221192 | tf_op jit(solution)/shard_map/ppermute | solution.py:280
  102.3 7.0 %collective-permute-start.22 = (bf16[2,144,128]{2,1,0:T(8,128)(2,1)S(1)}, bf16[2,144,128]{2,1,0:T(8,128)(2,1)S(1)}, u32[]{:S(2)}, u32[]{:S(2)}) collective-permute-start(bf16[2,144,128]{2,1,0:T(8,128)(2,1)S(1)} %get-tuple-element.60), channel_id=1, source_target_pairs={{0,48},{16,0},{32,16},{48,32},{1,49},{17,1},{33,17},{49,33},{2,50}... | collective-permute-start | bytes 221192 | tf_op jit(solution)/shard_map/ppermute | solution.py:280
  109.4 8.5 %collective-permute-start.23 = (bf16[2,144,128]{2,1,0:T(8,128)(2,1)S(1)}, bf16[2,144,128]{2,1,0:T(8,128)(2,1)S(1)}, u32[]{:S(2)}, u32[]{:S(2)}) collective-permute-start(bf16[2,144,128]{2,1,0:T(8,128)(2,1)S(1)} %get-tuple-element.69), channel_id=1, source_target_pairs={{0,64},{64,128},{128,192},{1,65},{65,129},{129,193},{2,66},{66,130... | collective-permute-start | bytes 221192 | tf_op jit(solution)/shard_map/ppermute | solution.py:285
  111.3 7.2 %collective-permute-start.24 = (bf16[2,144,128]{2,1,0:T(8,128)(2,1)S(1)}, bf16[2,144,128]{2,1,0:T(8,128)(2,1)S(1)}, u32[]{:S(2)}, u32[]{:S(2)}) collective-permute-start(bf16[2,144,128]{2,1,0:T(8,128)(2,1)S(1)} %get-tuple-element.69), channel_id=1, source_target_pairs={{0,128},{64,192},{1,129},{65,193},{2,130},{66,194},{3,131},{67,195... | collective-permute-start | bytes 221192 | tf_op jit(solution)/shard_map/ppermute | solution.py:285
  116.6 3.3 %collective-permute-start.25 = (bf16[2,144,128]{2,1,0:T(8,128)(2,1)S(1)}, bf16[2,144,128]{2,1,0:T(8,128)(2,1)S(1)}, u32[]{:S(2)}, u32[]{:S(2)}) collective-permute-start(bf16[2,144,128]{2,1,0:T(8,128)(2,1)S(1)} %get-tuple-element.69), channel_id=1, source_target_pairs={{0,192},{1,193},{2,194},{3,195},{4,196},{5,197},{6,198},{7,199},{8... | collective-permute-start | bytes 221192 | tf_op jit(solution)/shard_map/ppermute | solution.py:285
  122.2 1.3 collective-permute-start.26
  122.3 16.5 %copy-start.11 = (f32[512]{0:T(512)S(1)}, f32[512]{0:T(512)}, u32[]{:S(2)}) copy-start(f32[512]{0:T(512)} %param.7) | copy-start | bytes 6148
  123.5 15.3 %collective-permute-start.27 = (f32[640,256]{1,0:T(8,128)S(1)}, f32[640,256]{1,0:T(8,128)S(1)}, u32[]{:S(2)}, u32[]{:S(2)}) collective-permute-start(f32[640,256]{1,0:T(8,128)S(1)} %get-tuple-element.72), channel_id=1, source_target_pairs={{0,8},{8,0},{1,9},{9,1},{2,10},{10,2},{3,11},{11,3},{4,12},{12,4},... | collective-permute-start | bytes 1966088 | tf_op jit(solution)/shard_map/ppermute | solution.py:291
  123.7 3.6 %collective-permute-start.28 = (f32[640]{0:T(1024)S(1)}, f32[640]{0:T(1024)S(1)}, u32[]{:S(2)}, u32[]{:S(2)}) collective-permute-start(f32[640]{0:T(1024)S(1)} %add.194), channel_id=1, source_target_pairs={{0,2},{2,4},{4,6},{6,0},{1,3},{3,5},{5,7},{7,1},{8,10},{10,12},{12... | collective-permute-start | bytes 7688 | tf_op jit(solution)/shard_map/ppermute | solution.py:292
  123.9 5.1 %collective-permute-start.29 = (f32[640]{0:T(1024)S(1)}, f32[640]{0:T(1024)S(1)}, u32[]{:S(2)}, u32[]{:S(2)}) collective-permute-start(f32[640]{0:T(1024)S(1)} %add.194), channel_id=1, source_target_pairs={{0,4},{2,6},{4,0},{6,2},{1,5},{3,7},{5,1},{7,3},{8,12},{10,14},{12... | collective-permute-start | bytes 7688 | tf_op jit(solution)/shard_map/ppermute | solution.py:292
  126.5 4.8 %collective-permute-start.30 = (f32[640]{0:T(1024)S(1)}, f32[640]{0:T(1024)S(1)}, u32[]{:S(2)}, u32[]{:S(2)}) collective-permute-start(f32[640]{0:T(1024)S(1)} %add.194), channel_id=1, source_target_pairs={{0,6},{2,0},{4,2},{6,4},{1,7},{3,1},{5,3},{7,5},{8,14},{10,8},{12,... | collective-permute-start | bytes 7688 | tf_op jit(solution)/shard_map/ppermute | solution.py:292
  131.3 7.5 %collective-permute-start.31 = (f32[640]{0:T(1024)S(1)}, f32[640]{0:T(1024)S(1)}, u32[]{:S(2)}, u32[]{:S(2)}) collective-permute-start(f32[640]{0:T(1024)S(1)} %add_add_fusion), channel_id=1, source_target_pairs={{0,1},{1,0},{2,3},{3,2},{4,5},{5,4},{6,7},{7,6},{8,9},{9,8},{10,11... | collective-permute-start | bytes 7688 | tf_op jit(solution)/shard_map/ppermute | solution.py:293

commit v2 on v1

--- a/solution.py
+++ b/solution.py
@@ -134,7 +134,9 @@
 
 
 def incoming_body(place_ref, before_ref, first_ref, back1, back2, back3, out_ref):
-    rows = join(join(unpack(back3), unpack(back2)), unpack(back1))
+    x = place_ref[1]
+    back = [unpack(ref, (j + 1 <= x).astype(F32)) for j, ref in enumerate((back1, back2, back3))]
+    rows = join(join(back[2], back[1]), back[0])
     state = join(rows, unpack(before_ref))[0]
     first = unpack(first_ref)
     later = jnp.exp(first[1])[:, None, :] * state + first[0]
@@ -282,8 +284,8 @@
     q, intra = small_kernel(functools.partial(intra_body, DH**-0.5), outs, place, *last, b2, f3, q_acc, kv, fades)
     backs, intra = step((backs, intra))
     before, row = small_kernel(row_body, [(shape, F32), (shape, BF16)], z.reshape(1), chip, *backs)
-    backs = [lax.ppermute(row, "x", [(i, i + j) for i in range(4 - j)]) for j in (1, 2, 3)]
-    (state,) = small_kernel(incoming_body, [((2, group, 3 * DH, DH), BF16)], place, before, first, *backs)
+    backs = [lax.ppermute(row, "x", [(i, (i + j) % 4) for i in range(4)]) for j in (1, 2, 3)]
+    (state,) = small_kernel(incoming_body, [((2, group, 3 * DH, DH), BF16)], jnp.stack([core, x]), before, first, *backs)
 
     attended, squares = by_place(inter_body, [(2, rows, width), (2, 8, rows)], 10**9, q, fades, intra, state)
     squares = squares[:, 0, :]

time: 142 us -> 138 us (0.972); the launches traced: 140 us -> 138 us
  starting transfers between devices: 47.9 us -> 43.9 us
    ppermute x3, starting transfers between devices: 8.44 us -> 4.42 us  [on_device(): lax.ppermute(row, 'x', [(i, (i + j) % 4) for i in range(4)])]
  transfers between devices with their start and end apart: 32 -> 32, of which waited for: 14 -> 15; matrix products, arithmetic and copies ran while one was open for 6% -> 6% of each run, Pallas kernels for 20% -> 20%
where the time goes in v2:
time: 138 us
  waiting for transfers between devices  47.4 us (34%)
  starting transfers between devices  43.9 us (32%)
  Pallas kernels  33.1 us (24%)
  local copies, waits for them, and re-layouts  9.84 us (7%)
  other arithmetic  3.13 us (2%)
    ppermute x5, waiting for transfers between devices, along_z(): return lax.ppermute(part, 'zl', NEXT)  24.8 us
    pallas_call x2, Pallas kernels, project(): pl.pallas_call(functools.partial(project_body, groups, chunks, accs is no...  23.5 us
    ppermute x6, starting transfers between devices, to_left(): return lax.ppermute(part, 'x', LAST)  12.9 us
    ppermute x6, starting transfers between devices, to_right(): return lax.ppermute(part, 'x', NEXT)  8.49 us
    pallas_call x4, Pallas kernels, small_kernel(): pl.pallas_call(body, out_shape=[jax.ShapeDtypeStruct(*out) for out in out...  7.4 us
    ppermute x1, starting transfers between devices, on_device(): summed = summed + lax.ppermute(summed, 'zh', SWAP)  5.93 us
    ppermute x3, starting transfers between devices, on_device(): lax.ppermute(sent, 'zl', [(i, (i + j) % 4) for i in range(4)])  5.74 us
    ppermute x6, waiting for transfers between devices, to_left(): return lax.ppermute(part, 'x', LAST)  5.24 us
  transfers between devices with their start and end apart: 32, of which 15 were waited for; matrix products, arithmetic and copies ran while one was open for 6% of the time, Pallas kernels for 20%

profile of v2, /device:TPU:24, one launch (start us, length us, event | category | flops | bytes accessed | tf_op | source)
XLA Modules:
  0.0 137.8 jit_solution(2654580623226755929)
XLA Ops:
  0.0 1.1 constant_dynamic-slice_fusion.7
  1.1 0.1 collective-permute-start
  1.2 1.6 %collective-permute-done = bf16[3,192,256]{2,1,0:T(8,128)(2,1)S(1)} collective-permute-done((bf16[3,192,256]{2,1,0:T(8,128)(2,1)S(1)}, bf16[3,192,256]{2,1,0:T(8,128)(2,1)S(1)}, u32[]{:S(2)}, u32[]{:S(2)}) %collective-permute-start) | collective-permute-done | bytes 294944 | tf_op jit(solution)/shard_map/ppermute | solution.py:231
  2.8 0.3 maximum_select_fusion.1
  3.1 0.2 collective-permute-start.13
  3.3 1.9 %collective-permute-start.5 = (bf16[1152,256]{1,0:T(8,128)(2,1)S(1)}, bf16[1152,256]{1,0:T(8,128)(2,1)}, u32[]{:S(2)}, u32[]{:S(2)}) collective-permute-start(bf16[1152,256]{1,0:T(8,128)(2,1)S(1)} %bitcast.23), channel_id=1, source_target_pairs={{0,16},{16,32},{32,48},{48,0},{1,17},{17,33},{33,49},{49,1},{2,18}... | collective-permute-start | bytes 1769480 | tf_op jit(solution)/shard_map/ppermute | solution.py:244
  5.2 1.5 %collective-permute-start.1 = (bf16[1152,256]{1,0:T(8,128)(2,1)S(1)}, bf16[1152,256]{1,0:T(8,128)(2,1)S(1)}, u32[]{:S(2)}, u32[]{:S(2)}) collective-permute-start(bf16[1152,256]{1,0:T(8,128)(2,1)S(1)} %bitcast.24), channel_id=1, source_target_pairs={{0,64},{64,128},{128,192},{192,0},{1,65},{65,129},{129,193},{193,1... | collective-permute-start | bytes 1769480 | tf_op jit(solution)/shard_map/ppermute | solution.py:247
  6.7 1.7 %collective-permute-start.3 = (bf16[1152,256]{1,0:T(8,128)(2,1)S(1)}, bf16[1152,256]{1,0:T(8,128)(2,1)}, u32[]{:S(2)}, u32[]{:S(2)}) collective-permute-start(bf16[1152,256]{1,0:T(8,128)(2,1)S(1)} %bitcast.25), channel_id=1, source_target_pairs={{0,192},{64,0},{128,64},{192,128},{1,193},{65,1},{129,65},{193,129... | collective-permute-start | bytes 1769480 | tf_op jit(solution)/shard_map/ppermute | solution.py:250
  8.4 13.4 %collective-permute-done.5.refs_17_ = bf16[1152,256]{1,0:T(8,128)(2,1)} collective-permute-done((bf16[1152,256]{1,0:T(8,128)(2,1)S(1)}, bf16[1152,256]{1,0:T(8,128)(2,1)}, u32[]{:S(2)}, u32[]{:S(2)}) %collective-permute-start.5) | collective-permute-done | bytes 589856 | tf_op jit(solution)/shard_map/ppermute | solution.py:244
  21.9 1.3 constant_dynamic-slice_fusion.5
  23.2 0.1 collective-permute-start.16
  23.3 0.8 slice.45
  24.1 1.5 %collective-permute-start.2 = (bf16[576,256]{1,0:T(8,128)(2,1)}, bf16[576,256]{1,0:T(8,128)(2,1)S(1)}, u32[]{:S(2)}, u32[]{:S(2)}) collective-permute-start(bf16[576,256]{1,0:T(8,128)(2,1)} %slice.45), channel_id=1, source_target_pairs={{0,64},{64,128},{128,192},{192,0},{1,65},{65,129},{129,193},{193,1... | collective-permute-start | bytes 884744 | tf_op jit(solution)/shard_map/ppermute | solution.py:247
  25.7 0.6 stack.72.index_ref
  26.4 1.6 %collective-permute-start.8 = (bf16[1152,256]{1,0:T(8,128)(2,1)}, bf16[1152,256]{1,0:T(8,128)(2,1)S(1)}, u32[]{:S(2)}, u32[]{:S(2)}) collective-permute-start(bf16[1152,256]{1,0:T(8,128)(2,1)} %collective-permute-done.5.refs_17_), channel_id=1, source_target_pairs={{0,64},{64,128},{128,192},{192,0},{1,65},{65,129},{129,193},{193,1... | collective-permute-start | bytes 1769480 | tf_op jit(solution)/shard_map/ppermute | solution.py:247
  27.9 1.7 %collective-permute-start.9 = (bf16[1152,256]{1,0:T(8,128)(2,1)}, bf16[1152,256]{1,0:T(8,128)(2,1)S(1)}, u32[]{:S(2)}, u32[]{:S(2)}) collective-permute-start(bf16[1152,256]{1,0:T(8,128)(2,1)} %collective-permute-done.5.refs_17_), channel_id=1, source_target_pairs={{0,192},{64,0},{128,64},{192,128},{1,193},{65,1},{129,65},{193,129... | collective-permute-start | bytes 1769480 | tf_op jit(solution)/shard_map/ppermute | solution.py:250
  29.7 9.3 %collective-permute-done.6.refs_20_ = bf16[1152,256]{1,0:T(8,128)(2,1)} collective-permute-done((bf16[1152,256]{1,0:T(8,128)(2,1)}, bf16[1152,256]{1,0:T(8,128)(2,1)}, u32[]{:S(2)}, u32[]{:S(2)}) %collective-permute-start.6) | collective-permute-done | bytes 589856 | tf_op jit(solution)/shard_map/ppermute | solution.py:244
  39.0 1.2 reduce-window.6
  40.2 0.2 slice_reduce_fusion
  40.3 0.3 reduce-window.9
  40.7 1.0 slice.46
  41.7 2.8 %collective-permute-start.4 = (bf16[576,256]{1,0:T(8,128)(2,1)S(1)}, bf16[576,256]{1,0:T(8,128)(2,1)S(1)}, u32[]{:S(2)}, u32[]{:S(2)}) collective-permute-start(bf16[576,256]{1,0:T(8,128)(2,1)S(1)} %slice.46), channel_id=1, source_target_pairs={{0,192},{64,0},{128,64},{192,128},{1,193},{65,1},{129,65},{193,129... | collective-permute-start | bytes 884744 | tf_op jit(solution)/shard_map/ppermute | solution.py:250
  44.6 5.2 %collective-permute-done.4 = bf16[576,256]{1,0:T(8,128)(2,1)S(1)} collective-permute-done((bf16[576,256]{1,0:T(8,128)(2,1)S(1)}, bf16[576,256]{1,0:T(8,128)(2,1)S(1)}, u32[]{:S(2)}, u32[]{:S(2)}) %collective-permute-start.4) | collective-permute-done | bytes 294944 | tf_op jit(solution)/shard_map/ppermute | solution.py:250
  49.9 1.3 collective-permute-start.14
  51.2 2.6 %collective-permute-start.15 = (bf16[1152,256]{1,0:T(8,128)(2,1)}, bf16[1152,256]{1,0:T(8,128)(2,1)S(1)}, u32[]{:S(2)}, u32[]{:S(2)}) collective-permute-start(bf16[1152,256]{1,0:T(8,128)(2,1)} %collective-permute-done.6.refs_20_), channel_id=1, source_target_pairs={{0,192},{64,0},{128,64},{192,128},{1,193},{65,1},{129,65},{193,129... | collective-permute-start | bytes 1769480 | tf_op jit(solution)/shard_map/ppermute | solution.py:250
  53.8 1.5 %collective-permute-done.7.refs_12_ = bf16[1152,256]{1,0:T(8,128)(2,1)} collective-permute-done((bf16[1152,256]{1,0:T(8,128)(2,1)}, bf16[1152,256]{1,0:T(8,128)(2,1)}, u32[]{:S(2)}, u32[]{:S(2)}) %collective-permute-start.7) | collective-permute-done | bytes 589856 | tf_op jit(solution)/shard_map/ppermute | solution.py:244
  55.3 1.5 %collective-permute-start.11 = (bf16[1152,256]{1,0:T(8,128)(2,1)}, bf16[1152,256]{1,0:T(8,128)(2,1)S(1)}, u32[]{:S(2)}, u32[]{:S(2)}) collective-permute-start(bf16[1152,256]{1,0:T(8,128)(2,1)} %collective-permute-done.7.refs_12_), channel_id=1, source_target_pairs={{0,64},{64,128},{128,192},{192,0},{1,65},{65,129},{129,193},{193,1... | collective-permute-start | bytes 1769480 | tf_op jit(solution)/shard_map/ppermute | solution.py:247
  56.8 1.7 %collective-permute-start.12 = (bf16[1152,256]{1,0:T(8,128)(2,1)}, bf16[1152,256]{1,0:T(8,128)(2,1)}, u32[]{:S(2)}, u32[]{:S(2)}) collective-permute-start(bf16[1152,256]{1,0:T(8,128)(2,1)} %collective-permute-done.7.refs_12_), channel_id=1, source_target_pairs={{0,192},{64,0},{128,64},{192,128},{1,193},{65,1},{129,65},{193,129... | collective-permute-start | bytes 1769480 | tf_op jit(solution)/shard_map/ppermute | solution.py:250
  58.5 1.3 constant_dynamic-slice_fusion.3
  59.9 12.5 %shard_map.46 = (f32[2,1,640,256]{3,2,1,0:T(8,128)}, f32[2,2,640,256]{3,2,1,0:T(8,128)}) custom-call(s32[8]{0:T(128)} %stack.72.index_ref, bf16[640,6144]{1,0:T(8,128)(2,1)} %refs_5_.3, bf16[640,6144]{1,0:T(8,128)(2,1)} %refs_5_.3, bf16[640,6144]{1,0:T(8,128)(2,1)} %refs_5_.3, bf16[640,6144]{1,0:T(8,128)(2,1)} %refs_5_.3, bf16[640,6144]{1,0:T(8,128)(2,1)} %refs_5_.3, ...), custom_call_target="tpu_custom_call" | custom-call | flops 6039797760 | bytes 7864320 | tf_op jit(solution)/shard_map/pallas_call | solution.py:52
  72.5 0.6 collective-permute-done.10.refs_15_
  73.1 5.0 %collective-permute-done.11.refs_16_ = bf16[1152,256]{1,0:T(8,128)(2,1)S(1)} collective-permute-done((bf16[1152,256]{1,0:T(8,128)(2,1)}, bf16[1152,256]{1,0:T(8,128)(2,1)S(1)}, u32[]{:S(2)}, u32[]{:S(2)}) %collective-permute-start.11) | collective-permute-done | bytes 589856 | tf_op jit(solution)/shard_map/ppermute | solution.py:247
  78.1 1.0 collective-permute-start.17
  79.2 0.6 stack.82.index_ref
  79.8 1.2 collective-permute-start.18
  81.0 1.0 slice.40
  81.9 2.2 %collective-permute-start.19 = (bf16[576,256]{1,0:T(8,128)(2,1)S(1)}, bf16[576,256]{1,0:T(8,128)(2,1)S(1)}, u32[]{:S(2)}, u32[]{:S(2)}) collective-permute-start(bf16[576,256]{1,0:T(8,128)(2,1)S(1)} %slice.40), channel_id=1, source_target_pairs={{0,192},{64,0},{128,64},{192,128},{1,193},{65,1},{129,65},{193,129... | collective-permute-start | bytes 884744 | tf_op jit(solution)/shard_map/ppermute | solution.py:250
  84.2 11.0 %shard_map.47 = (f32[2,1,640,256]{3,2,1,0:T(8,128)}, f32[2,2,640,256]{3,2,1,0:T(8,128)}) custom-call(s32[6]{0:T(128)} %stack.82.index_ref, bf16[640,6144]{1,0:T(8,128)(2,1)} %refs_5_.3, bf16[640,6144]{1,0:T(8,128)(2,1)} %refs_5_.3, bf16[640,6144]{1,0:T(8,128)(2,1)} %refs_5_.3, bf16[640,6144]{1,0:T(8,128)(2,1)} %refs_5_.3, bf16[640,6144]{1,0:T(8,128)(2,1)} %refs_5_.3, ...), custom_call_target="tpu_custom_call" | custom-call | flops 4529848320 | bytes 5898240 | tf_op jit(solution)/shard_map/pallas_call | solution.py:52
  95.2 1.7 %copy-done = f32[2,2,640,256]{3,2,1,0:T(8,128)S(1)} copy-done((f32[2,2,640,256]{3,2,1,0:T(8,128)S(1)}, f32[2,2,640,256]{3,2,1,0:T(8,128)}, u32[]{:S(2)}) %copy-start) | copy-done | bytes 2621464
  96.9 1.8 %shard_map.48 = (bf16[2,2,640,256]{3,2,1,0:T(8,128)(2,1)S(1)}, f32[2,144,128]{2,1,0:T(8,128)S(1)}, bf16[2,144,128]{2,1,0:T(8,128)(2,1)S(1)}, f32[2,144,128]{2,1,0:T(8,128)S(1)}) custom-call(s32[1]{0:T(128)} %bitcast.place_ref, bf16[640,768]{1,0:T(8,128)(2,1)S(1)} %pad_maximum_fusion.mine_ref, bf16[640,768]{1,0:T(8,128)(2,1)S(1)} %pad_maximum_fusion.1.theirs_ref, ...), custom_call_target="tpu_custom_call" | custom-call | tf_op jit(solution)/shard_map/pallas_call | solution.py:152
  98.7 2.0 %collective-permute-start.20 = (bf16[2,144,128]{2,1,0:T(8,128)(2,1)S(1)}, bf16[2,144,128]{2,1,0:T(8,128)(2,1)S(1)}, u32[]{:S(2)}, u32[]{:S(2)}) collective-permute-start(bf16[2,144,128]{2,1,0:T(8,128)(2,1)S(1)} %get-tuple-element.60), channel_id=1, source_target_pairs={{0,16},{16,32},{32,48},{48,0},{1,17},{17,33},{33,49},{49,1},{2,18}... | collective-permute-start | bytes 221192 | tf_op jit(solution)/shard_map/ppermute | solution.py:282
  100.7 1.5 %collective-permute-start.21 = (bf16[2,144,128]{2,1,0:T(8,128)(2,1)S(1)}, bf16[2,144,128]{2,1,0:T(8,128)(2,1)S(1)}, u32[]{:S(2)}, u32[]{:S(2)}) collective-permute-start(bf16[2,144,128]{2,1,0:T(8,128)(2,1)S(1)} %get-tuple-element.60), channel_id=1, source_target_pairs={{0,32},{16,48},{32,0},{48,16},{1,33},{17,49},{33,1},{49,17},{2,34}... | collective-permute-start | bytes 221192 | tf_op jit(solution)/shard_map/ppermute | solution.py:282
  102.2 2.2 %collective-permute-start.22 = (bf16[2,144,128]{2,1,0:T(8,128)(2,1)S(1)}, bf16[2,144,128]{2,1,0:T(8,128)(2,1)S(1)}, u32[]{:S(2)}, u32[]{:S(2)}) collective-permute-start(bf16[2,144,128]{2,1,0:T(8,128)(2,1)S(1)} %get-tuple-element.60), channel_id=1, source_target_pairs={{0,48},{16,0},{32,16},{48,32},{1,49},{17,1},{33,17},{49,33},{2,50}... | collective-permute-start | bytes 221192 | tf_op jit(solution)/shard_map/ppermute | solution.py:282
  104.5 4.8 %shard_map.49 = (bf16[2,640,256]{2,1,0:T(8,128)(2,1)S(1)}, f32[2,640,256]{2,1,0:T(8,128)S(1)}) custom-call(s32[1]{0:T(128)} %bitcast.place_ref, bf16[640,768]{1,0:T(8,128)(2,1)S(1)} %pad_maximum_fusion.mine_ref, bf16[640,768]{1,0:T(8,128)(2,1)S(1)} %pad_maximum_fusion.1.theirs_ref, bf16[1152,256]{1,0:T(8,128)(2,1)S(1)} %collective-permute-done.17.b_ref, ...), custom_call_target="tpu_custom_call" | custom-call | tf_op jit(solution)/shard_map/pallas_call | solution.py:152
  109.3 0.1 shard_map.50
  109.5 3.3 %collective-permute-start.24 = (bf16[2,144,128]{2,1,0:T(8,128)(2,1)S(1)}, bf16[2,144,128]{2,1,0:T(8,128)(2,1)S(1)}, u32[]{:S(2)}, u32[]{:S(2)}) collective-permute-start(bf16[2,144,128]{2,1,0:T(8,128)(2,1)S(1)} %get-tuple-element.69), channel_id=1, source_target_pairs={{0,128},{64,192},{128,0},{192,64},{1,129},{65,193},{129,1},{193,65... | collective-permute-start | bytes 221192 | tf_op jit(solution)/shard_map/ppermute | solution.py:287
  112.8 1.0 collective-permute-start.25
  113.9 1.1 collective-permute-done.23.back1
  115.1 0.9 collective-permute-done.24.back2
  115.9 1.2 collective-permute-done.25.back3
  117.2 0.7 shard_map.51.state_ref
  117.9 2.2 %shard_map.52 = (f32[2,640,256]{2,1,0:T(8,128)S(1)}, f32[2,8,640]{2,1,0:T(8,128)S(1)}) custom-call(bf16[2,640,256]{2,1,0:T(8,128)(2,1)S(1)} %get-tuple-element.59.q_ref, f32[2,8,640]{2,1,0:T(8,128)S(1)} %pad.4.decay_ref, f32[2,640,256]{2,1,0:T(8,128)S(1)} %get-tuple-element.62.intra_ref, bf16[2,2,384,128]{3,2,1,0:T(8,128)(2,1)S(1)} %shard_map.51.state_ref), custom_call_target="tpu_custom_call" | custom-call | flops 1000000000 | bytes 4000000 | tf_op jit(solution)/shard_map/pallas_call | solution.py:206
  120.1 0.1 collective-permute-start.26
  120.2 0.1 slice_bitcast_fusion.1
  120.3 1.0 collective-permute-done.26
  121.4 0.2 collective-permute-start.27
  121.5 0.2 collective-permute-start.28
  121.8 2.6 %collective-permute-start.29 = (f32[640]{0:T(1024)S(1)}, f32[640]{0:T(1024)S(1)}, u32[]{:S(2)}, u32[]{:S(2)}) collective-permute-start(f32[640]{0:T(1024)S(1)} %add.194), channel_id=1, source_target_pairs={{0,4},{2,6},{4,0},{6,2},{1,5},{3,7},{5,1},{7,3},{8,12},{10,14},{12... | collective-permute-start | bytes 7688 | tf_op jit(solution)/shard_map/ppermute | solution.py:294
  124.3 0.8 collective-permute-done.28
  125.1 1.7 %collective-permute-done.29 = f32[640]{0:T(1024)S(1)} collective-permute-done((f32[640]{0:T(1024)S(1)}, f32[640]{0:T(1024)S(1)}, u32[]{:S(2)}, u32[]{:S(2)}) %collective-permute-start.29) | collective-permute-done | bytes 2592 | tf_op jit(solution)/shard_map/ppermute | solution.py:294
  126.9 2.3 %collective-permute-done.30 = f32[640]{0:T(1024)S(1)} collective-permute-done((f32[640]{0:T(1024)S(1)}, f32[640]{0:T(1024)S(1)}, u32[]{:S(2)}, u32[]{:S(2)}) %collective-permute-start.30) | collective-permute-done | bytes 2592 | tf_op jit(solution)/shard_map/ppermute | solution.py:294
  129.2 5.9 %collective-permute-start.31 = (f32[640]{0:T(1024)S(1)}, f32[640]{0:T(1024)S(1)}, u32[]{:S(2)}, u32[]{:S(2)}) collective-permute-start(f32[640]{0:T(1024)S(1)} %add_add_fusion), channel_id=1, source_target_pairs={{0,1},{1,0},{2,3},{3,2},{4,5},{5,4},{6,7},{7,6},{8,9},{9,8},{10,11... | collective-permute-start | bytes 7688 | tf_op jit(solution)/shard_map/ppermute | solution.py:295
  135.1 1.6 %collective-permute-done.31 = f32[640]{0:T(1024)S(1)} collective-permute-done((f32[640]{0:T(1024)S(1)}, f32[640]{0:T(1024)S(1)}, u32[]{:S(2)}, u32[]{:S(2)}) %collective-permute-start.31) | collective-permute-done | bytes 2592 | tf_op jit(solution)/shard_map/ppermute | solution.py:295
  136.7 1.0 fusion.2
  (62 shorter events, 0.7 us)
Async XLA Ops:
  0.0 21.9 %copy-start.10 = (f32[4,640]{1,0:T(4,128)S(1)}, f32[4,640]{1,0:T(4,128)}, u32[]{:S(2)}) copy-start(f32[4,640]{1,0:T(4,128)} %param.6) | copy-start | bytes 30724
  1.1 1.7 %collective-permute-start = (bf16[3,192,256]{2,1,0:T(8,128)(2,1)S(1)}, bf16[3,192,256]{2,1,0:T(8,128)(2,1)S(1)}, u32[]{:S(2)}, u32[]{:S(2)}) collective-permute-start(bf16[3,192,256]{2,1,0:T(8,128)(2,1)S(1)} %get-tuple-element.82), channel_id=1, source_target_pairs={{0,8},{8,0},{1,9},{9,1},{2,10},{10,2},{3,11},{11,3},{4,12},{12,4},... | collective-permute-start | bytes 884744 | tf_op jit(solution)/shard_map/ppermute | solution.py:231
  3.0 21.0 %copy-start.2 = (bf16[3,384,256]{2,1,0:T(8,128)(2,1)}, bf16[3,384,256]{2,1,0:T(8,128)(2,1)S(1)}, u32[]{:S(2)}) copy-start(bf16[3,384,256]{2,1,0:T(8,128)(2,1)S(1)} %maximum_select_fusion.1) | copy-start | bytes 1769476
  3.1 55.5 %collective-permute-start.13 = (bf16[640,6144]{1,0:T(8,128)(2,1)}, bf16[640,6144]{1,0:T(8,128)(2,1)}, u32[]{:S(2)}, u32[]{:S(2)}) collective-permute-start(bf16[640,6144]{1,0:T(8,128)(2,1)} %refs_5_.3), channel_id=1, source_target_pairs={{0,8},{8,0},{1,9},{9,1},{2,10},{10,2},{3,11},{11,3},{4,12},{12,4},... | collective-permute-start | bytes 23592968 | tf_op jit(solution)/shard_map/ppermute | solution.py:235
  3.3 18.6 %collective-permute-start.5 = (bf16[1152,256]{1,0:T(8,128)(2,1)S(1)}, bf16[1152,256]{1,0:T(8,128)(2,1)}, u32[]{:S(2)}, u32[]{:S(2)}) collective-permute-start(bf16[1152,256]{1,0:T(8,128)(2,1)S(1)} %bitcast.23), channel_id=1, source_target_pairs={{0,16},{16,32},{32,48},{48,0},{1,17},{17,33},{33,49},{49,1},{2,18}... | collective-permute-start | bytes 1769480 | tf_op jit(solution)/shard_map/ppermute | solution.py:244
  5.2 18.1 %collective-permute-start.1 = (bf16[1152,256]{1,0:T(8,128)(2,1)S(1)}, bf16[1152,256]{1,0:T(8,128)(2,1)S(1)}, u32[]{:S(2)}, u32[]{:S(2)}) collective-permute-start(bf16[1152,256]{1,0:T(8,128)(2,1)S(1)} %bitcast.24), channel_id=1, source_target_pairs={{0,64},{64,128},{128,192},{192,0},{1,65},{65,129},{129,193},{193,1... | collective-permute-start | bytes 1769480 | tf_op jit(solution)/shard_map/ppermute | solution.py:247
  6.7 21.2 %collective-permute-start.3 = (bf16[1152,256]{1,0:T(8,128)(2,1)S(1)}, bf16[1152,256]{1,0:T(8,128)(2,1)}, u32[]{:S(2)}, u32[]{:S(2)}) collective-permute-start(bf16[1152,256]{1,0:T(8,128)(2,1)S(1)} %bitcast.25), channel_id=1, source_target_pairs={{0,192},{64,0},{128,64},{192,128},{1,193},{65,1},{129,65},{193,129... | collective-permute-start | bytes 1769480 | tf_op jit(solution)/shard_map/ppermute | solution.py:250
  21.9 17.1 %collective-permute-start.6 = (bf16[1152,256]{1,0:T(8,128)(2,1)}, bf16[1152,256]{1,0:T(8,128)(2,1)}, u32[]{:S(2)}, u32[]{:S(2)}) collective-permute-start(bf16[1152,256]{1,0:T(8,128)(2,1)} %collective-permute-done.5.refs_17_), channel_id=1, source_target_pairs={{0,16},{16,32},{32,48},{48,0},{1,17},{17,33},{33,49},{49,1},{2,18}... | collective-permute-start | bytes 1769480 | tf_op jit(solution)/shard_map/ppermute | solution.py:244
  23.2 3.2 %collective-permute-start.16 = (f32[2,640]{1,0:T(2,128)S(1)}, f32[2,640]{1,0:T(2,128)S(1)}, u32[]{:S(2)}, u32[]{:S(2)}) collective-permute-start(f32[2,640]{1,0:T(2,128)S(1)} %get-tuple-element.45), channel_id=1, source_target_pairs={{0,8},{8,0},{1,9},{9,1},{2,10},{10,2},{3,11},{11,3},{4,12},{12,4},... | collective-permute-start | bytes 15368 | tf_op jit(solution)/shard_map/ppermute | solution.py:234
  23.3 2.4 %copy-start.3 = (bf16[1152,256]{1,0:T(8,128)(2,1)}, bf16[1152,256]{1,0:T(8,128)(2,1)S(1)}, u32[]{:S(2)}) copy-start(bf16[1152,256]{1,0:T(8,128)(2,1)S(1)} %collective-permute-done.1.refs_18_) | copy-start | bytes 1769476
  24.1 17.6 %collective-permute-start.2 = (bf16[576,256]{1,0:T(8,128)(2,1)}, bf16[576,256]{1,0:T(8,128)(2,1)S(1)}, u32[]{:S(2)}, u32[]{:S(2)}) collective-permute-start(bf16[576,256]{1,0:T(8,128)(2,1)} %slice.45), channel_id=1, source_target_pairs={{0,64},{64,128},{128,192},{192,0},{1,65},{65,129},{129,193},{193,1... | collective-permute-start | bytes 884744 | tf_op jit(solution)/shard_map/ppermute | solution.py:247
  26.4 24.8 %collective-permute-start.8 = (bf16[1152,256]{1,0:T(8,128)(2,1)}, bf16[1152,256]{1,0:T(8,128)(2,1)S(1)}, u32[]{:S(2)}, u32[]{:S(2)}) collective-permute-start(bf16[1152,256]{1,0:T(8,128)(2,1)} %collective-permute-done.5.refs_17_), channel_id=1, source_target_pairs={{0,64},{64,128},{128,192},{192,0},{1,65},{65,129},{129,193},{193,1... | collective-permute-start | bytes 1769480 | tf_op jit(solution)/shard_map/ppermute | solution.py:247
  27.9 25.9 %collective-permute-start.9 = (bf16[1152,256]{1,0:T(8,128)(2,1)}, bf16[1152,256]{1,0:T(8,128)(2,1)S(1)}, u32[]{:S(2)}, u32[]{:S(2)}) collective-permute-start(bf16[1152,256]{1,0:T(8,128)(2,1)} %collective-permute-done.5.refs_17_), channel_id=1, source_target_pairs={{0,192},{64,0},{128,64},{192,128},{1,193},{65,1},{129,65},{193,129... | collective-permute-start | bytes 1769480 | tf_op jit(solution)/shard_map/ppermute | solution.py:250
  39.0 16.3 %collective-permute-start.7 = (bf16[1152,256]{1,0:T(8,128)(2,1)}, bf16[1152,256]{1,0:T(8,128)(2,1)}, u32[]{:S(2)}, u32[]{:S(2)}) collective-permute-start(bf16[1152,256]{1,0:T(8,128)(2,1)} %collective-permute-done.6.refs_20_), channel_id=1, source_target_pairs={{0,16},{16,32},{32,48},{48,0},{1,17},{17,33},{33,49},{49,1},{2,18}... | collective-permute-start | bytes 1769480 | tf_op jit(solution)/shard_map/ppermute | solution.py:244
  41.7 8.2 %collective-permute-start.4 = (bf16[576,256]{1,0:T(8,128)(2,1)S(1)}, bf16[576,256]{1,0:T(8,128)(2,1)S(1)}, u32[]{:S(2)}, u32[]{:S(2)}) collective-permute-start(bf16[576,256]{1,0:T(8,128)(2,1)S(1)} %slice.46), channel_id=1, source_target_pairs={{0,192},{64,0},{128,64},{192,128},{1,193},{65,1},{129,65},{193,129... | collective-permute-start | bytes 884744 | tf_op jit(solution)/shard_map/ppermute | solution.py:250
  49.9 10.0 %copy-start.4 = (bf16[1152,256]{1,0:T(8,128)(2,1)}, bf16[1152,256]{1,0:T(8,128)(2,1)S(1)}, u32[]{:S(2)}) copy-start(bf16[1152,256]{1,0:T(8,128)(2,1)S(1)} %constant_dynamic-update-slice_fusion.refs_23_) | copy-start | bytes 1769476
  49.9 22.6 %collective-permute-start.14 = (bf16[1152,256]{1,0:T(8,128)(2,1)}, bf16[1152,256]{1,0:T(8,128)(2,1)S(1)}, u32[]{:S(2)}, u32[]{:S(2)}) collective-permute-start(bf16[1152,256]{1,0:T(8,128)(2,1)} %collective-permute-done.6.refs_20_), channel_id=1, source_target_pairs={{0,64},{64,128},{128,192},{192,0},{1,65},{65,129},{129,193},{193,1... | collective-permute-start | bytes 1769480 | tf_op jit(solution)/shard_map/ppermute | solution.py:247
  51.2 8.6 %copy-start.6 = (bf16[1152,256]{1,0:T(8,128)(2,1)}, bf16[1152,256]{1,0:T(8,128)(2,1)S(1)}, u32[]{:S(2)}) copy-start(bf16[1152,256]{1,0:T(8,128)(2,1)S(1)} %collective-permute-done.8.refs_21_) | copy-start | bytes 1769476
  51.2 21.3 %collective-permute-start.15 = (bf16[1152,256]{1,0:T(8,128)(2,1)}, bf16[1152,256]{1,0:T(8,128)(2,1)S(1)}, u32[]{:S(2)}, u32[]{:S(2)}) collective-permute-start(bf16[1152,256]{1,0:T(8,128)(2,1)} %collective-permute-done.6.refs_20_), channel_id=1, source_target_pairs={{0,192},{64,0},{128,64},{192,128},{1,193},{65,1},{129,65},{193,129... | collective-permute-start | bytes 1769480 | tf_op jit(solution)/shard_map/ppermute | solution.py:250
  53.8 6.1 %copy-start.7 = (bf16[1152,256]{1,0:T(8,128)(2,1)}, bf16[1152,256]{1,0:T(8,128)(2,1)S(1)}, u32[]{:S(2)}) copy-start(bf16[1152,256]{1,0:T(8,128)(2,1)S(1)} %collective-permute-done.9.refs_22_) | copy-start | bytes 1769476
  55.3 22.8 %collective-permute-start.11 = (bf16[1152,256]{1,0:T(8,128)(2,1)}, bf16[1152,256]{1,0:T(8,128)(2,1)S(1)}, u32[]{:S(2)}, u32[]{:S(2)}) collective-permute-start(bf16[1152,256]{1,0:T(8,128)(2,1)} %collective-permute-done.7.refs_12_), channel_id=1, source_target_pairs={{0,64},{64,128},{128,192},{192,0},{1,65},{65,129},{129,193},{193,1... | collective-permute-start | bytes 1769480 | tf_op jit(solution)/shard_map/ppermute | solution.py:247
  56.8 21.4 %collective-permute-start.12 = (bf16[1152,256]{1,0:T(8,128)(2,1)}, bf16[1152,256]{1,0:T(8,128)(2,1)}, u32[]{:S(2)}, u32[]{:S(2)}) collective-permute-start(bf16[1152,256]{1,0:T(8,128)(2,1)} %collective-permute-done.7.refs_12_), channel_id=1, source_target_pairs={{0,192},{64,0},{128,64},{192,128},{1,193},{65,1},{129,65},{193,129... | collective-permute-start | bytes 1769480 | tf_op jit(solution)/shard_map/ppermute | solution.py:250
  58.5 14.6 %collective-permute-start.10 = (bf16[1152,256]{1,0:T(8,128)(2,1)S(1)}, bf16[1152,256]{1,0:T(8,128)(2,1)}, u32[]{:S(2)}, u32[]{:S(2)}) collective-permute-start(bf16[1152,256]{1,0:T(8,128)(2,1)S(1)} %constant_dynamic-update-slice_fusion.refs_23_), channel_id=1, source_target_pairs={{0,16},{16,32},{32,48},{48,0},{1,17},{17,33},{33,49},{49,1},{2,18}... | collective-permute-start | bytes 1769480 | tf_op jit(solution)/shard_map/ppermute | solution.py:244
  72.5 5.7 %copy-start.8 = (bf16[1152,256]{1,0:T(8,128)(2,1)}, bf16[1152,256]{1,0:T(8,128)(2,1)S(1)}, u32[]{:S(2)}) copy-start(bf16[1152,256]{1,0:T(8,128)(2,1)S(1)} %collective-permute-done.14.refs_13_) | copy-start | bytes 1769476
  72.5 5.6 %copy-start.9 = (bf16[1152,256]{1,0:T(8,128)(2,1)}, bf16[1152,256]{1,0:T(8,128)(2,1)S(1)}, u32[]{:S(2)}) copy-start(bf16[1152,256]{1,0:T(8,128)(2,1)S(1)} %collective-permute-done.15.refs_14_) | copy-start | bytes 1769476
  78.1 6.1 %copy-start.5 = (bf16[1152,256]{1,0:T(8,128)(2,1)}, bf16[1152,256]{1,0:T(8,128)(2,1)S(1)}, u32[]{:S(2)}) copy-start(bf16[1152,256]{1,0:T(8,128)(2,1)S(1)} %collective-permute-done.11.refs_16_) | copy-start | bytes 1769476
  78.1 17.0 %collective-permute-start.17 = (bf16[1152,256]{1,0:T(8,128)(2,1)}, bf16[1152,256]{1,0:T(8,128)(2,1)S(1)}, u32[]{:S(2)}, u32[]{:S(2)}) collective-permute-start(bf16[1152,256]{1,0:T(8,128)(2,1)} %collective-permute-done.10.refs_15_), channel_id=1, source_target_pairs={{0,16},{16,32},{32,48},{48,0},{1,17},{17,33},{33,49},{49,1},{2,18}... | collective-permute-start | bytes 1769480 | tf_op jit(solution)/shard_map/ppermute | solution.py:244
  79.8 15.3 %collective-permute-start.18 = (bf16[576,256]{1,0:T(8,128)(2,1)S(1)}, bf16[576,256]{1,0:T(8,128)(2,1)S(1)}, u32[]{:S(2)}, u32[]{:S(2)}) collective-permute-start(bf16[576,256]{1,0:T(8,128)(2,1)S(1)} %slice.39), channel_id=1, source_target_pairs={{0,64},{64,128},{128,192},{192,0},{1,65},{65,129},{129,193},{193,1... | collective-permute-start | bytes 884744 | tf_op jit(solution)/shard_map/ppermute | solution.py:247
  81.9 13.2 %collective-permute-start.19 = (bf16[576,256]{1,0:T(8,128)(2,1)S(1)}, bf16[576,256]{1,0:T(8,128)(2,1)S(1)}, u32[]{:S(2)}, u32[]{:S(2)}) collective-permute-start(bf16[576,256]{1,0:T(8,128)(2,1)S(1)} %slice.40), channel_id=1, source_target_pairs={{0,192},{64,0},{128,64},{192,128},{1,193},{65,1},{129,65},{193,129... | collective-permute-start | bytes 884744 | tf_op jit(solution)/shard_map/ppermute | solution.py:250
  95.2 1.7 %copy-start = (f32[2,2,640,256]{3,2,1,0:T(8,128)S(1)}, f32[2,2,640,256]{3,2,1,0:T(8,128)}, u32[]{:S(2)}) copy-start(f32[2,2,640,256]{3,2,1,0:T(8,128)} %get-tuple-element.57.acc_ref) | copy-start | bytes 7864324
  96.9 7.6 %copy-start.1 = (f32[2,1,640,256]{3,2,1,0:T(8,128)S(1)}, f32[2,1,640,256]{3,2,1,0:T(8,128)}, u32[]{:S(2)}) copy-start(f32[2,1,640,256]{3,2,1,0:T(8,128)} %get-tuple-element.55.acc_ref) | copy-start | bytes 3932164
  98.7 10.5 %collective-permute-start.20 = (bf16[2,144,128]{2,1,0:T(8,128)(2,1)S(1)}, bf16[2,144,128]{2,1,0:T(8,128)(2,1)S(1)}, u32[]{:S(2)}, u32[]{:S(2)}) collective-permute-start(bf16[2,144,128]{2,1,0:T(8,128)(2,1)S(1)} %get-tuple-element.60), channel_id=1, source_target_pairs={{0,16},{16,32},{32,48},{48,0},{1,17},{17,33},{33,49},{49,1},{2,18}... | collective-permute-start | bytes 221192 | tf_op jit(solution)/shard_map/ppermute | solution.py:282
  100.7 8.5 %collective-permute-start.21 = (bf16[2,144,128]{2,1,0:T(8,128)(2,1)S(1)}, bf16[2,144,128]{2,1,0:T(8,128)(2,1)S(1)}, u32[]{:S(2)}, u32[]{:S(2)}) collective-permute-start(bf16[2,144,128]{2,1,0:T(8,128)(2,1)S(1)} %get-tuple-element.60), channel_id=1, source_target_pairs={{0,32},{16,48},{32,0},{48,16},{1,33},{17,49},{33,1},{49,17},{2,34}... | collective-permute-start | bytes 221192 | tf_op jit(solution)/shard_map/ppermute | solution.py:282
  102.2 7.0 %collective-permute-start.22 = (bf16[2,144,128]{2,1,0:T(8,128)(2,1)S(1)}, bf16[2,144,128]{2,1,0:T(8,128)(2,1)S(1)}, u32[]{:S(2)}, u32[]{:S(2)}) collective-permute-start(bf16[2,144,128]{2,1,0:T(8,128)(2,1)S(1)} %get-tuple-element.60), channel_id=1, source_target_pairs={{0,48},{16,0},{32,16},{48,32},{1,49},{17,1},{33,17},{49,33},{2,50}... | collective-permute-start | bytes 221192 | tf_op jit(solution)/shard_map/ppermute | solution.py:282
  109.4 5.6 %collective-permute-start.23 = (bf16[2,144,128]{2,1,0:T(8,128)(2,1)S(1)}, bf16[2,144,128]{2,1,0:T(8,128)(2,1)S(1)}, u32[]{:S(2)}, u32[]{:S(2)}) collective-permute-start(bf16[2,144,128]{2,1,0:T(8,128)(2,1)S(1)} %get-tuple-element.69), channel_id=1, source_target_pairs={{0,64},{64,128},{128,192},{192,0},{1,65},{65,129},{129,193},{193,1... | collective-permute-start | bytes 221192 | tf_op jit(solution)/shard_map/ppermute | solution.py:287
  109.5 6.4 %collective-permute-start.24 = (bf16[2,144,128]{2,1,0:T(8,128)(2,1)S(1)}, bf16[2,144,128]{2,1,0:T(8,128)(2,1)S(1)}, u32[]{:S(2)}, u32[]{:S(2)}) collective-permute-start(bf16[2,144,128]{2,1,0:T(8,128)(2,1)S(1)} %get-tuple-element.69), channel_id=1, source_target_pairs={{0,128},{64,192},{128,0},{192,64},{1,129},{65,193},{129,1},{193,65... | collective-permute-start | bytes 221192 | tf_op jit(solution)/shard_map/ppermute | solution.py:287
  112.8 4.4 %collective-permute-start.25 = (bf16[2,144,128]{2,1,0:T(8,128)(2,1)S(1)}, bf16[2,144,128]{2,1,0:T(8,128)(2,1)S(1)}, u32[]{:S(2)}, u32[]{:S(2)}) collective-permute-start(bf16[2,144,128]{2,1,0:T(8,128)(2,1)S(1)} %get-tuple-element.69), channel_id=1, source_target_pairs={{0,192},{64,0},{128,64},{192,128},{1,193},{65,1},{129,65},{193,129... | collective-permute-start | bytes 221192 | tf_op jit(solution)/shard_map/ppermute | solution.py:287
  120.1 1.3 collective-permute-start.26
  120.2 16.5 %copy-start.11 = (f32[512]{0:T(512)S(1)}, f32[512]{0:T(512)}, u32[]{:S(2)}) copy-start(f32[512]{0:T(512)} %param.7) | copy-start | bytes 6148
  121.4 15.3 %collective-permute-start.27 = (f32[640,256]{1,0:T(8,128)S(1)}, f32[640,256]{1,0:T(8,128)S(1)}, u32[]{:S(2)}, u32[]{:S(2)}) collective-permute-start(f32[640,256]{1,0:T(8,128)S(1)} %get-tuple-element.72), channel_id=1, source_target_pairs={{0,8},{8,0},{1,9},{9,1},{2,10},{10,2},{3,11},{11,3},{4,12},{12,4},... | collective-permute-start | bytes 1966088 | tf_op jit(solution)/shard_map/ppermute | solution.py:293
  121.5 3.6 %collective-permute-start.28 = (f32[640]{0:T(1024)S(1)}, f32[640]{0:T(1024)S(1)}, u32[]{:S(2)}, u32[]{:S(2)}) collective-permute-start(f32[640]{0:T(1024)S(1)} %add.194), channel_id=1, source_target_pairs={{0,2},{2,4},{4,6},{6,0},{1,3},{3,5},{5,7},{7,1},{8,10},{10,12},{12... | collective-permute-start | bytes 7688 | tf_op jit(solution)/shard_map/ppermute | solution.py:294
  121.8 5.1 %collective-permute-start.29 = (f32[640]{0:T(1024)S(1)}, f32[640]{0:T(1024)S(1)}, u32[]{:S(2)}, u32[]{:S(2)}) collective-permute-start(f32[640]{0:T(1024)S(1)} %add.194), channel_id=1, source_target_pairs={{0,4},{2,6},{4,0},{6,2},{1,5},{3,7},{5,1},{7,3},{8,12},{10,14},{12... | collective-permute-start | bytes 7688 | tf_op jit(solution)/shard_map/ppermute | solution.py:294
  124.3 4.8 %collective-permute-start.30 = (f32[640]{0:T(1024)S(1)}, f32[640]{0:T(1024)S(1)}, u32[]{:S(2)}, u32[]{:S(2)}) collective-permute-start(f32[640]{0:T(1024)S(1)} %add.194), channel_id=1, source_target_pairs={{0,6},{2,0},{4,2},{6,4},{1,7},{3,1},{5,3},{7,5},{8,14},{10,8},{12,... | collective-permute-start | bytes 7688 | tf_op jit(solution)/shard_map/ppermute | solution.py:294
  129.2 7.5 %collective-permute-start.31 = (f32[640]{0:T(1024)S(1)}, f32[640]{0:T(1024)S(1)}, u32[]{:S(2)}, u32[]{:S(2)}) collective-permute-start(f32[640]{0:T(1024)S(1)} %add_add_fusion), channel_id=1, source_target_pairs={{0,1},{1,0},{2,3},{3,2},{4,5},{5,4},{6,7},{7,6},{8,9},{9,8},{10,11... | collective-permute-start | bytes 7688 | tf_op jit(solution)/shard_map/ppermute | solution.py:295

commit v3 on v2

--- a/solution.py
+++ b/solution.py
@@ -260,11 +260,11 @@
 
     a2, r1, l1, f0, g0 = along_z(a1), to_right(a1), to_left(a1), to_right(r0[:half]), to_left(l0[half:])
 
-    held = tied(a2, a1, r0, l0)
+    held = tied(a2, r1, l1, f0, g0)
     a3, r2, l2 = along_z(held), to_right(held), to_left(held)
 
     far0 = jnp.concatenate([f0, g0])
-    sent_z, sent_x = tied((far0, a3), a2, r1, l1, f0, g0)
+    sent_z, sent_x = tied((far0, a3), r2, l2)
     b1, r3, l3 = along_z(sent_z), to_right(sent_x), to_left(sent_x)
     chunks = [own_x[0], own_x[1], right_x[0], left_x[0], own_x[2], right_x[1], left_x[1], far_x[0]]
     acc = project(chunks, tokens, other_tokens, [own, a1, r0, l0, a2, r1, l1, far0], None)

time: 138 us -> 142 us (1.029)
  waiting for transfers between devices: 47.4 us -> 55.5 us
  starting transfers between devices: 43.9 us -> 39.5 us
    ppermute x6, waiting for transfers between devices: 5.04 us -> 24 us  [to_right(): return lax.ppermute(part, 'x', NEXT)]
    ppermute x5, waiting for transfers between devices: 24.8 us -> 6.06 us  [along_z(): return lax.ppermute(part, 'zl', NEXT)]
    ppermute x6, waiting for transfers between devices: 5.24 us -> 12 us  [to_left(): return lax.ppermute(part, 'x', LAST)]
    ppermute x6, starting transfers between devices: 8.49 us -> 4.72 us  [to_right(): return lax.ppermute(part, 'x', NEXT)]
  transfers between devices with their start and end apart: 32 -> 32, of which waited for: 15 -> 14; matrix products, arithmetic and copies ran while one was open for 6% -> 6% of each run, Pallas kernels for 20% -> 20%
where the time goes in v3:
time: 142 us; the launch traced here: 141 us
  waiting for transfers between devices  55.5 us (39%)
  starting transfers between devices  39.5 us (28%)
  Pallas kernels  33 us (23%)
  local copies, waits for them, and re-layouts  9.79 us (7%)
  other arithmetic  3.11 us (2%)
    ppermute x6, waiting for transfers between devices, to_right(): return lax.ppermute(part, 'x', NEXT)  24 us
    pallas_call x2, Pallas kernels, project(): pl.pallas_call(functools.partial(project_body, groups, chunks, accs is no...  23.5 us
    ppermute x6, starting transfers between devices, to_left(): return lax.ppermute(part, 'x', LAST)  12.4 us
    ppermute x6, waiting for transfers between devices, to_left(): return lax.ppermute(part, 'x', LAST)  12 us
    pallas_call x4, Pallas kernels, small_kernel(): pl.pallas_call(body, out_shape=[jax.ShapeDtypeStruct(*out) for out in out...  7.39 us
    ppermute x3, starting transfers between devices, on_device(): lax.ppermute(sent, 'zl', [(i, (i + j) % 4) for i in range(4)])  6.95 us
    ppermute x5, waiting for transfers between devices, along_z(): return lax.ppermute(part, 'zl', NEXT)  6.06 us
    ppermute x1, starting transfers between devices, on_device(): summed = summed + lax.ppermute(summed, 'zh', SWAP)  5.47 us
  transfers between devices with their start and end apart: 32, of which 14 were waited for; matrix products, arithmetic and copies ran while one was open for 6% of the time, Pallas kernels for 20%

profile of v3, /device:TPU:24, one launch (start us, length us, event | category | flops | bytes accessed | tf_op | source)
XLA Modules:
  0.0 141.3 jit_solution(2366340068662544038)
XLA Ops:
  0.0 1.1 constant_dynamic-slice_fusion.7
  1.1 0.1 collective-permute-start
  1.2 1.6 %collective-permute-done = bf16[3,192,256]{2,1,0:T(8,128)(2,1)S(1)} collective-permute-done((bf16[3,192,256]{2,1,0:T(8,128)(2,1)S(1)}, bf16[3,192,256]{2,1,0:T(8,128)(2,1)S(1)}, u32[]{:S(2)}, u32[]{:S(2)}) %collective-permute-start) | collective-permute-done | bytes 294944 | tf_op jit(solution)/shard_map/ppermute | solution.py:231
  2.8 0.3 maximum_select_fusion.1
  3.0 0.2 collective-permute-start.15
  3.3 1.5 %collective-permute-start.1 = (bf16[1152,256]{1,0:T(8,128)(2,1)S(1)}, bf16[1152,256]{1,0:T(8,128)(2,1)S(1)}, u32[]{:S(2)}, u32[]{:S(2)}) collective-permute-start(bf16[1152,256]{1,0:T(8,128)(2,1)S(1)} %bitcast.23), channel_id=1, source_target_pairs={{0,64},{64,128},{128,192},{192,0},{1,65},{65,129},{129,193},{193,1... | collective-permute-start | bytes 1769480 | tf_op jit(solution)/shard_map/ppermute | solution.py:247
  4.8 1.9 %collective-permute-start.5 = (bf16[1152,256]{1,0:T(8,128)(2,1)S(1)}, bf16[1152,256]{1,0:T(8,128)(2,1)}, u32[]{:S(2)}, u32[]{:S(2)}) collective-permute-start(bf16[1152,256]{1,0:T(8,128)(2,1)S(1)} %bitcast.24), channel_id=1, source_target_pairs={{0,16},{16,32},{32,48},{48,0},{1,17},{17,33},{33,49},{49,1},{2,18}... | collective-permute-start | bytes 1769480 | tf_op jit(solution)/shard_map/ppermute | solution.py:244
  6.7 1.7 %collective-permute-start.3 = (bf16[1152,256]{1,0:T(8,128)(2,1)S(1)}, bf16[1152,256]{1,0:T(8,128)(2,1)S(1)}, u32[]{:S(2)}, u32[]{:S(2)}) collective-permute-start(bf16[1152,256]{1,0:T(8,128)(2,1)S(1)} %bitcast.25), channel_id=1, source_target_pairs={{0,192},{64,0},{128,64},{192,128},{1,193},{65,1},{129,65},{193,129... | collective-permute-start | bytes 1769480 | tf_op jit(solution)/shard_map/ppermute | solution.py:250
  8.5 0.1 collective-permute-start.16
  8.6 11.5 %collective-permute-done.1.refs_18_ = bf16[1152,256]{1,0:T(8,128)(2,1)S(1)} collective-permute-done((bf16[1152,256]{1,0:T(8,128)(2,1)S(1)}, bf16[1152,256]{1,0:T(8,128)(2,1)S(1)}, u32[]{:S(2)}, u32[]{:S(2)}) %collective-permute-start.1) | collective-permute-done | bytes 589856 | tf_op jit(solution)/shard_map/ppermute | solution.py:247
  20.1 0.4 collective-permute-start.2
  20.5 2.6 %collective-permute-done.5.refs_17_ = bf16[1152,256]{1,0:T(8,128)(2,1)} collective-permute-done((bf16[1152,256]{1,0:T(8,128)(2,1)S(1)}, bf16[1152,256]{1,0:T(8,128)(2,1)}, u32[]{:S(2)}, u32[]{:S(2)}) %collective-permute-start.5) | collective-permute-done | bytes 589856 | tf_op jit(solution)/shard_map/ppermute | solution.py:244
  23.1 1.5 %collective-permute-start.7 = (bf16[1152,256]{1,0:T(8,128)(2,1)}, bf16[1152,256]{1,0:T(8,128)(2,1)}, u32[]{:S(2)}, u32[]{:S(2)}) collective-permute-start(bf16[1152,256]{1,0:T(8,128)(2,1)} %collective-permute-done.5.refs_17_), channel_id=1, source_target_pairs={{0,64},{64,128},{128,192},{192,0},{1,65},{65,129},{129,193},{193,1... | collective-permute-start | bytes 1769480 | tf_op jit(solution)/shard_map/ppermute | solution.py:247
  24.6 1.7 %collective-permute-start.8 = (bf16[1152,256]{1,0:T(8,128)(2,1)}, bf16[1152,256]{1,0:T(8,128)(2,1)}, u32[]{:S(2)}, u32[]{:S(2)}) collective-permute-start(bf16[1152,256]{1,0:T(8,128)(2,1)} %collective-permute-done.5.refs_17_), channel_id=1, source_target_pairs={{0,192},{64,0},{128,64},{192,128},{1,193},{65,1},{129,65},{193,129... | collective-permute-start | bytes 1769480 | tf_op jit(solution)/shard_map/ppermute | solution.py:250
  26.3 0.7 slice.46
  27.1 4.3 %collective-permute-done.2 = bf16[576,256]{1,0:T(8,128)(2,1)S(1)} collective-permute-done((bf16[576,256]{1,0:T(8,128)(2,1)S(1)}, bf16[576,256]{1,0:T(8,128)(2,1)S(1)}, u32[]{:S(2)}, u32[]{:S(2)}) %collective-permute-start.2) | collective-permute-done | bytes 294944 | tf_op jit(solution)/shard_map/ppermute | solution.py:247
  31.3 0.3 collective-permute-start.4
  31.7 0.6 stack.72.index_ref
  32.3 1.3 constant_dynamic-slice_fusion.5
  33.7 12.0 %collective-permute-done.4 = bf16[576,256]{1,0:T(8,128)(2,1)} collective-permute-done((bf16[576,256]{1,0:T(8,128)(2,1)}, bf16[576,256]{1,0:T(8,128)(2,1)}, u32[]{:S(2)}, u32[]{:S(2)}) %collective-permute-start.4) | collective-permute-done | bytes 294944 | tf_op jit(solution)/shard_map/ppermute | solution.py:250
  45.7 1.3 collective-permute-start.10
  47.0 2.0 %collective-permute-start.11 = (bf16[1152,256]{1,0:T(8,128)(2,1)}, bf16[1152,256]{1,0:T(8,128)(2,1)S(1)}, u32[]{:S(2)}, u32[]{:S(2)}) collective-permute-start(bf16[1152,256]{1,0:T(8,128)(2,1)} %collective-permute-done.6.refs_20_), channel_id=1, source_target_pairs={{0,192},{64,0},{128,64},{192,128},{1,193},{65,1},{129,65},{193,129... | collective-permute-start | bytes 1769480 | tf_op jit(solution)/shard_map/ppermute | solution.py:250
  49.1 0.8 collective-permute-start.9
  49.8 1.1 reduce-window.6
  51.0 0.2 slice_reduce_fusion
  51.1 0.3 reduce-window.9
  51.6 1.0 constant_dynamic-update-slice_fusion.refs_23_
  52.6 8.2 %collective-permute-done.10.refs_13_ = bf16[1152,256]{1,0:T(8,128)(2,1)S(1)} collective-permute-done((bf16[1152,256]{1,0:T(8,128)(2,1)}, bf16[1152,256]{1,0:T(8,128)(2,1)S(1)}, u32[]{:S(2)}, u32[]{:S(2)}) %collective-permute-start.10) | collective-permute-done | bytes 589856 | tf_op jit(solution)/shard_map/ppermute | solution.py:247
  60.8 3.4 %collective-permute-done.9.refs_12_ = bf16[1152,256]{1,0:T(8,128)(2,1)} collective-permute-done((bf16[1152,256]{1,0:T(8,128)(2,1)}, bf16[1152,256]{1,0:T(8,128)(2,1)}, u32[]{:S(2)}, u32[]{:S(2)}) %collective-permute-start.9) | collective-permute-done | bytes 589856 | tf_op jit(solution)/shard_map/ppermute | solution.py:244
  64.3 3.2 %collective-permute-start.14 = (bf16[1152,256]{1,0:T(8,128)(2,1)}, bf16[1152,256]{1,0:T(8,128)(2,1)}, u32[]{:S(2)}, u32[]{:S(2)}) collective-permute-start(bf16[1152,256]{1,0:T(8,128)(2,1)} %collective-permute-done.9.refs_12_), channel_id=1, source_target_pairs={{0,192},{64,0},{128,64},{192,128},{1,193},{65,1},{129,65},{193,129... | collective-permute-start | bytes 1769480 | tf_op jit(solution)/shard_map/ppermute | solution.py:250
  67.5 1.3 constant_dynamic-slice_fusion.3
  68.9 12.5 %shard_map.46 = (f32[2,1,640,256]{3,2,1,0:T(8,128)}, f32[2,2,640,256]{3,2,1,0:T(8,128)}) custom-call(s32[8]{0:T(128)} %stack.72.index_ref, bf16[640,6144]{1,0:T(8,128)(2,1)} %refs_5_.3, bf16[640,6144]{1,0:T(8,128)(2,1)} %refs_5_.3, bf16[640,6144]{1,0:T(8,128)(2,1)} %refs_5_.3, bf16[640,6144]{1,0:T(8,128)(2,1)} %refs_5_.3, bf16[640,6144]{1,0:T(8,128)(2,1)} %refs_5_.3, ...), custom_call_target="tpu_custom_call" | custom-call | flops 6039797760 | bytes 7864320 | tf_op jit(solution)/shard_map/pallas_call | solution.py:52
  81.5 0.5 collective-permute-start.17
  82.0 0.6 stack.82.index_ref
  82.6 0.1 collective-permute-start.18
  82.7 1.0 slice.40
  83.7 3.3 %collective-permute-start.19 = (bf16[576,256]{1,0:T(8,128)(2,1)S(1)}, bf16[576,256]{1,0:T(8,128)(2,1)S(1)}, u32[]{:S(2)}, u32[]{:S(2)}) collective-permute-start(bf16[576,256]{1,0:T(8,128)(2,1)S(1)} %slice.40), channel_id=1, source_target_pairs={{0,192},{64,0},{128,64},{192,128},{1,193},{65,1},{129,65},{193,129... | collective-permute-start | bytes 884744 | tf_op jit(solution)/shard_map/ppermute | solution.py:250
  87.0 11.0 %shard_map.47 = (f32[2,1,640,256]{3,2,1,0:T(8,128)}, f32[2,2,640,256]{3,2,1,0:T(8,128)}) custom-call(s32[6]{0:T(128)} %stack.82.index_ref, bf16[640,6144]{1,0:T(8,128)(2,1)} %refs_5_.3, bf16[640,6144]{1,0:T(8,128)(2,1)} %refs_5_.3, bf16[640,6144]{1,0:T(8,128)(2,1)} %refs_5_.3, bf16[640,6144]{1,0:T(8,128)(2,1)} %refs_5_.3, bf16[640,6144]{1,0:T(8,128)(2,1)} %refs_5_.3, ...), custom_call_target="tpu_custom_call" | custom-call | flops 4529848320 | bytes 5898240 | tf_op jit(solution)/shard_map/pallas_call | solution.py:52
  98.0 1.7 %copy-done = f32[2,2,640,256]{3,2,1,0:T(8,128)S(1)} copy-done((f32[2,2,640,256]{3,2,1,0:T(8,128)S(1)}, f32[2,2,640,256]{3,2,1,0:T(8,128)}, u32[]{:S(2)}) %copy-start) | copy-done | bytes 2621464
  99.8 1.8 %shard_map.48 = (bf16[2,2,640,256]{3,2,1,0:T(8,128)(2,1)S(1)}, f32[2,144,128]{2,1,0:T(8,128)S(1)}, bf16[2,144,128]{2,1,0:T(8,128)(2,1)S(1)}, f32[2,144,128]{2,1,0:T(8,128)S(1)}) custom-call(s32[1]{0:T(128)} %bitcast.place_ref, bf16[640,768]{1,0:T(8,128)(2,1)S(1)} %pad_maximum_fusion.mine_ref, bf16[640,768]{1,0:T(8,128)(2,1)S(1)} %pad_maximum_fusion.1.theirs_ref, ...), custom_call_target="tpu_custom_call" | custom-call | tf_op jit(solution)/shard_map/pallas_call | solution.py:152
  101.6 2.2 %collective-permute-start.20 = (bf16[2,144,128]{2,1,0:T(8,128)(2,1)S(1)}, bf16[2,144,128]{2,1,0:T(8,128)(2,1)S(1)}, u32[]{:S(2)}, u32[]{:S(2)}) collective-permute-start(bf16[2,144,128]{2,1,0:T(8,128)(2,1)S(1)} %get-tuple-element.60), channel_id=1, source_target_pairs={{0,16},{16,32},{32,48},{48,0},{1,17},{17,33},{33,49},{49,1},{2,18}... | collective-permute-start | bytes 221192 | tf_op jit(solution)/shard_map/ppermute | solution.py:282
  103.8 1.9 %collective-permute-start.21 = (bf16[2,144,128]{2,1,0:T(8,128)(2,1)S(1)}, bf16[2,144,128]{2,1,0:T(8,128)(2,1)S(1)}, u32[]{:S(2)}, u32[]{:S(2)}) collective-permute-start(bf16[2,144,128]{2,1,0:T(8,128)(2,1)S(1)} %get-tuple-element.60), channel_id=1, source_target_pairs={{0,32},{16,48},{32,0},{48,16},{1,33},{17,49},{33,1},{49,17},{2,34}... | collective-permute-start | bytes 221192 | tf_op jit(solution)/shard_map/ppermute | solution.py:282
  105.7 2.8 %collective-permute-start.22 = (bf16[2,144,128]{2,1,0:T(8,128)(2,1)S(1)}, bf16[2,144,128]{2,1,0:T(8,128)(2,1)S(1)}, u32[]{:S(2)}, u32[]{:S(2)}) collective-permute-start(bf16[2,144,128]{2,1,0:T(8,128)(2,1)S(1)} %get-tuple-element.60), channel_id=1, source_target_pairs={{0,48},{16,0},{32,16},{48,32},{1,49},{17,1},{33,17},{49,33},{2,50}... | collective-permute-start | bytes 221192 | tf_op jit(solution)/shard_map/ppermute | solution.py:282
  108.5 4.8 %shard_map.49 = (bf16[2,640,256]{2,1,0:T(8,128)(2,1)S(1)}, f32[2,640,256]{2,1,0:T(8,128)S(1)}) custom-call(s32[1]{0:T(128)} %bitcast.place_ref, bf16[640,768]{1,0:T(8,128)(2,1)S(1)} %pad_maximum_fusion.mine_ref, bf16[640,768]{1,0:T(8,128)(2,1)S(1)} %pad_maximum_fusion.1.theirs_ref, bf16[1152,256]{1,0:T(8,128)(2,1)S(1)} %collective-permute-done.17.b_ref, ...), custom_call_target="tpu_custom_call" | custom-call | tf_op jit(solution)/shard_map/pallas_call | solution.py:152
  113.3 0.1 shard_map.50
  113.5 0.1 collective-permute-start.23
  113.6 1.5 %collective-permute-start.24 = (bf16[2,144,128]{2,1,0:T(8,128)(2,1)S(1)}, bf16[2,144,128]{2,1,0:T(8,128)(2,1)S(1)}, u32[]{:S(2)}, u32[]{:S(2)}) collective-permute-start(bf16[2,144,128]{2,1,0:T(8,128)(2,1)S(1)} %get-tuple-element.69), channel_id=1, source_target_pairs={{0,128},{64,192},{128,0},{192,64},{1,129},{65,193},{129,1},{193,65... | collective-permute-start | bytes 221192 | tf_op jit(solution)/shard_map/ppermute | solution.py:287
  115.1 1.7 %collective-permute-start.25 = (bf16[2,144,128]{2,1,0:T(8,128)(2,1)S(1)}, bf16[2,144,128]{2,1,0:T(8,128)(2,1)S(1)}, u32[]{:S(2)}, u32[]{:S(2)}) collective-permute-start(bf16[2,144,128]{2,1,0:T(8,128)(2,1)S(1)} %get-tuple-element.69), channel_id=1, source_target_pairs={{0,192},{64,0},{128,64},{192,128},{1,193},{65,1},{129,65},{193,129... | collective-permute-start | bytes 221192 | tf_op jit(solution)/shard_map/ppermute | solution.py:287
  116.9 3.0 %collective-permute-done.23.back1 = bf16[2,144,128]{2,1,0:T(8,128)(2,1)S(1)} collective-permute-done((bf16[2,144,128]{2,1,0:T(8,128)(2,1)S(1)}, bf16[2,144,128]{2,1,0:T(8,128)(2,1)S(1)}, u32[]{:S(2)}, u32[]{:S(2)}) %collective-permute-start.23) | collective-permute-done | bytes 73760 | tf_op jit(solution)/shard_map/ppermute | solution.py:287
  119.9 0.9 collective-permute-done.25.back3
  120.8 0.7 shard_map.51.state_ref
  121.5 2.2 %shard_map.52 = (f32[2,640,256]{2,1,0:T(8,128)S(1)}, f32[2,8,640]{2,1,0:T(8,128)S(1)}) custom-call(bf16[2,640,256]{2,1,0:T(8,128)(2,1)S(1)} %get-tuple-element.59.q_ref, f32[2,8,640]{2,1,0:T(8,128)S(1)} %pad.4.decay_ref, f32[2,640,256]{2,1,0:T(8,128)S(1)} %get-tuple-element.62.intra_ref, bf16[2,2,384,128]{3,2,1,0:T(8,128)(2,1)S(1)} %shard_map.51.state_ref), custom_call_target="tpu_custom_call" | custom-call | flops 1000000000 | bytes 4000000 | tf_op jit(solution)/shard_map/pallas_call | solution.py:206
  123.7 0.1 collective-permute-start.26
  123.8 0.1 slice_bitcast_fusion.1
  123.9 1.0 collective-permute-done.26
  125.0 0.2 collective-permute-start.27
  125.1 0.2 collective-permute-start.28
  125.3 2.6 %collective-permute-start.29 = (f32[640]{0:T(1024)S(1)}, f32[640]{0:T(1024)S(1)}, u32[]{:S(2)}, u32[]{:S(2)}) collective-permute-start(f32[640]{0:T(1024)S(1)} %add.194), channel_id=1, source_target_pairs={{0,4},{2,6},{4,0},{6,2},{1,5},{3,7},{5,1},{7,3},{8,12},{10,14},{12... | collective-permute-start | bytes 7688 | tf_op jit(solution)/shard_map/ppermute | solution.py:294
  127.9 0.8 collective-permute-done.28
  128.7 1.7 %collective-permute-done.29 = f32[640]{0:T(1024)S(1)} collective-permute-done((f32[640]{0:T(1024)S(1)}, f32[640]{0:T(1024)S(1)}, u32[]{:S(2)}, u32[]{:S(2)}) %collective-permute-start.29) | collective-permute-done | bytes 2592 | tf_op jit(solution)/shard_map/ppermute | solution.py:294
  130.5 2.3 %collective-permute-done.30 = f32[640]{0:T(1024)S(1)} collective-permute-done((f32[640]{0:T(1024)S(1)}, f32[640]{0:T(1024)S(1)}, u32[]{:S(2)}, u32[]{:S(2)}) %collective-permute-start.30) | collective-permute-done | bytes 2592 | tf_op jit(solution)/shard_map/ppermute | solution.py:294
  132.8 5.5 %collective-permute-start.31 = (f32[640]{0:T(1024)S(1)}, f32[640]{0:T(1024)S(1)}, u32[]{:S(2)}, u32[]{:S(2)}) collective-permute-start(f32[640]{0:T(1024)S(1)} %add_add_fusion), channel_id=1, source_target_pairs={{0,1},{1,0},{2,3},{3,2},{4,5},{5,4},{6,7},{7,6},{8,9},{9,8},{10,11... | collective-permute-start | bytes 7688 | tf_op jit(solution)/shard_map/ppermute | solution.py:295
  138.2 2.0 %collective-permute-done.31 = f32[640]{0:T(1024)S(1)} collective-permute-done((f32[640]{0:T(1024)S(1)}, f32[640]{0:T(1024)S(1)}, u32[]{:S(2)}, u32[]{:S(2)}) %collective-permute-start.31) | collective-permute-done | bytes 2592 | tf_op jit(solution)/shard_map/ppermute | solution.py:295
  140.3 1.0 fusion.2
  (60 shorter events, 0.6 us)
Async XLA Ops:
  0.0 8.4 %copy-start.9 = (f32[4,640]{1,0:T(4,128)S(1)}, f32[4,640]{1,0:T(4,128)}, u32[]{:S(2)}) copy-start(f32[4,640]{1,0:T(4,128)} %param.6) | copy-start | bytes 30724
  1.1 1.7 %collective-permute-start = (bf16[3,192,256]{2,1,0:T(8,128)(2,1)S(1)}, bf16[3,192,256]{2,1,0:T(8,128)(2,1)S(1)}, u32[]{:S(2)}, u32[]{:S(2)}) collective-permute-start(bf16[3,192,256]{2,1,0:T(8,128)(2,1)S(1)} %get-tuple-element.82), channel_id=1, source_target_pairs={{0,8},{8,0},{1,9},{9,1},{2,10},{10,2},{3,11},{11,3},{4,12},{12,4},... | collective-permute-start | bytes 884744 | tf_op jit(solution)/shard_map/ppermute | solution.py:231
  3.0 30.5 %copy-start.2 = (bf16[3,384,256]{2,1,0:T(8,128)(2,1)}, bf16[3,384,256]{2,1,0:T(8,128)(2,1)S(1)}, u32[]{:S(2)}) copy-start(bf16[3,384,256]{2,1,0:T(8,128)(2,1)S(1)} %maximum_select_fusion.1) | copy-start | bytes 1769476
  3.0 64.5 %collective-permute-start.15 = (bf16[640,6144]{1,0:T(8,128)(2,1)}, bf16[640,6144]{1,0:T(8,128)(2,1)}, u32[]{:S(2)}, u32[]{:S(2)}) collective-permute-start(bf16[640,6144]{1,0:T(8,128)(2,1)} %refs_5_.3), channel_id=1, source_target_pairs={{0,8},{8,0},{1,9},{9,1},{2,10},{10,2},{3,11},{11,3},{4,12},{12,4},... | collective-permute-start | bytes 23592968 | tf_op jit(solution)/shard_map/ppermute | solution.py:235
  3.3 16.8 %collective-permute-start.1 = (bf16[1152,256]{1,0:T(8,128)(2,1)S(1)}, bf16[1152,256]{1,0:T(8,128)(2,1)S(1)}, u32[]{:S(2)}, u32[]{:S(2)}) collective-permute-start(bf16[1152,256]{1,0:T(8,128)(2,1)S(1)} %bitcast.23), channel_id=1, source_target_pairs={{0,64},{64,128},{128,192},{192,0},{1,65},{65,129},{129,193},{193,1... | collective-permute-start | bytes 1769480 | tf_op jit(solution)/shard_map/ppermute | solution.py:247
  4.8 18.3 %collective-permute-start.5 = (bf16[1152,256]{1,0:T(8,128)(2,1)S(1)}, bf16[1152,256]{1,0:T(8,128)(2,1)}, u32[]{:S(2)}, u32[]{:S(2)}) collective-permute-start(bf16[1152,256]{1,0:T(8,128)(2,1)S(1)} %bitcast.24), channel_id=1, source_target_pairs={{0,16},{16,32},{32,48},{48,0},{1,17},{17,33},{33,49},{49,1},{2,18}... | collective-permute-start | bytes 1769480 | tf_op jit(solution)/shard_map/ppermute | solution.py:244
  6.7 17.9 %collective-permute-start.3 = (bf16[1152,256]{1,0:T(8,128)(2,1)S(1)}, bf16[1152,256]{1,0:T(8,128)(2,1)S(1)}, u32[]{:S(2)}, u32[]{:S(2)}) collective-permute-start(bf16[1152,256]{1,0:T(8,128)(2,1)S(1)} %bitcast.25), channel_id=1, source_target_pairs={{0,192},{64,0},{128,64},{192,128},{1,193},{65,1},{129,65},{193,129... | collective-permute-start | bytes 1769480 | tf_op jit(solution)/shard_map/ppermute | solution.py:250
  8.5 14.6 %collective-permute-start.16 = (f32[2,640]{1,0:T(2,128)S(1)}, f32[2,640]{1,0:T(2,128)S(1)}, u32[]{:S(2)}, u32[]{:S(2)}) collective-permute-start(f32[2,640]{1,0:T(2,128)S(1)} %get-tuple-element.45), channel_id=1, source_target_pairs={{0,8},{8,0},{1,9},{9,1},{2,10},{10,2},{3,11},{11,3},{4,12},{12,4},... | collective-permute-start | bytes 15368 | tf_op jit(solution)/shard_map/ppermute | solution.py:234
  20.1 13.5 %copy-start.3 = (bf16[1152,256]{1,0:T(8,128)(2,1)}, bf16[1152,256]{1,0:T(8,128)(2,1)S(1)}, u32[]{:S(2)}) copy-start(bf16[1152,256]{1,0:T(8,128)(2,1)S(1)} %collective-permute-done.1.refs_18_) | copy-start | bytes 1769476
  20.1 11.2 %collective-permute-start.2 = (bf16[576,256]{1,0:T(8,128)(2,1)S(1)}, bf16[576,256]{1,0:T(8,128)(2,1)S(1)}, u32[]{:S(2)}, u32[]{:S(2)}) collective-permute-start(bf16[576,256]{1,0:T(8,128)(2,1)S(1)} %slice.45), channel_id=1, source_target_pairs={{0,64},{64,128},{128,192},{192,0},{1,65},{65,129},{129,193},{193,1... | collective-permute-start | bytes 884744 | tf_op jit(solution)/shard_map/ppermute | solution.py:247
  23.1 22.7 %collective-permute-start.6 = (bf16[1152,256]{1,0:T(8,128)(2,1)}, bf16[1152,256]{1,0:T(8,128)(2,1)}, u32[]{:S(2)}, u32[]{:S(2)}) collective-permute-start(bf16[1152,256]{1,0:T(8,128)(2,1)} %collective-permute-done.5.refs_17_), channel_id=1, source_target_pairs={{0,16},{16,32},{32,48},{48,0},{1,17},{17,33},{33,49},{49,1},{2,18}... | collective-permute-start | bytes 1769480 | tf_op jit(solution)/shard_map/ppermute | solution.py:244
  23.1 22.6 %collective-permute-start.7 = (bf16[1152,256]{1,0:T(8,128)(2,1)}, bf16[1152,256]{1,0:T(8,128)(2,1)}, u32[]{:S(2)}, u32[]{:S(2)}) collective-permute-start(bf16[1152,256]{1,0:T(8,128)(2,1)} %collective-permute-done.5.refs_17_), channel_id=1, source_target_pairs={{0,64},{64,128},{128,192},{192,0},{1,65},{65,129},{129,193},{193,1... | collective-permute-start | bytes 1769480 | tf_op jit(solution)/shard_map/ppermute | solution.py:247
  24.6 9.0 %copy-start.4 = (bf16[1152,256]{1,0:T(8,128)(2,1)}, bf16[1152,256]{1,0:T(8,128)(2,1)S(1)}, u32[]{:S(2)}) copy-start(bf16[1152,256]{1,0:T(8,128)(2,1)S(1)} %collective-permute-done.3.refs_19_) | copy-start | bytes 1769476
  24.6 21.2 %collective-permute-start.8 = (bf16[1152,256]{1,0:T(8,128)(2,1)}, bf16[1152,256]{1,0:T(8,128)(2,1)}, u32[]{:S(2)}, u32[]{:S(2)}) collective-permute-start(bf16[1152,256]{1,0:T(8,128)(2,1)} %collective-permute-done.5.refs_17_), channel_id=1, source_target_pairs={{0,192},{64,0},{128,64},{192,128},{1,193},{65,1},{129,65},{193,129... | collective-permute-start | bytes 1769480 | tf_op jit(solution)/shard_map/ppermute | solution.py:250
  31.3 14.4 %collective-permute-start.4 = (bf16[576,256]{1,0:T(8,128)(2,1)}, bf16[576,256]{1,0:T(8,128)(2,1)}, u32[]{:S(2)}, u32[]{:S(2)}) collective-permute-start(bf16[576,256]{1,0:T(8,128)(2,1)} %slice.46), channel_id=1, source_target_pairs={{0,192},{64,0},{128,64},{192,128},{1,193},{65,1},{129,65},{193,129... | collective-permute-start | bytes 884744 | tf_op jit(solution)/shard_map/ppermute | solution.py:250
  45.7 15.1 %collective-permute-start.10 = (bf16[1152,256]{1,0:T(8,128)(2,1)}, bf16[1152,256]{1,0:T(8,128)(2,1)S(1)}, u32[]{:S(2)}, u32[]{:S(2)}) collective-permute-start(bf16[1152,256]{1,0:T(8,128)(2,1)} %collective-permute-done.6.refs_20_), channel_id=1, source_target_pairs={{0,64},{64,128},{128,192},{192,0},{1,65},{65,129},{129,193},{193,1... | collective-permute-start | bytes 1769480 | tf_op jit(solution)/shard_map/ppermute | solution.py:247
  47.0 13.8 %collective-permute-start.11 = (bf16[1152,256]{1,0:T(8,128)(2,1)}, bf16[1152,256]{1,0:T(8,128)(2,1)S(1)}, u32[]{:S(2)}, u32[]{:S(2)}) collective-permute-start(bf16[1152,256]{1,0:T(8,128)(2,1)} %collective-permute-done.6.refs_20_), channel_id=1, source_target_pairs={{0,192},{64,0},{128,64},{192,128},{1,193},{65,1},{129,65},{193,129... | collective-permute-start | bytes 1769480 | tf_op jit(solution)/shard_map/ppermute | solution.py:250
  49.1 15.2 %collective-permute-start.9 = (bf16[1152,256]{1,0:T(8,128)(2,1)}, bf16[1152,256]{1,0:T(8,128)(2,1)}, u32[]{:S(2)}, u32[]{:S(2)}) collective-permute-start(bf16[1152,256]{1,0:T(8,128)(2,1)} %collective-permute-done.6.refs_20_), channel_id=1, source_target_pairs={{0,16},{16,32},{32,48},{48,0},{1,17},{17,33},{33,49},{49,1},{2,18}... | collective-permute-start | bytes 1769480 | tf_op jit(solution)/shard_map/ppermute | solution.py:244
  52.6 16.3 %copy-start.5 = (bf16[1152,256]{1,0:T(8,128)(2,1)}, bf16[1152,256]{1,0:T(8,128)(2,1)S(1)}, u32[]{:S(2)}) copy-start(bf16[1152,256]{1,0:T(8,128)(2,1)S(1)} %constant_dynamic-update-slice_fusion.refs_23_) | copy-start | bytes 1769476
  60.8 8.0 %copy-start.7 = (bf16[1152,256]{1,0:T(8,128)(2,1)}, bf16[1152,256]{1,0:T(8,128)(2,1)S(1)}, u32[]{:S(2)}) copy-start(bf16[1152,256]{1,0:T(8,128)(2,1)S(1)} %collective-permute-done.10.refs_13_) | copy-start | bytes 1769476
  60.8 8.0 %copy-start.8 = (bf16[1152,256]{1,0:T(8,128)(2,1)}, bf16[1152,256]{1,0:T(8,128)(2,1)S(1)}, u32[]{:S(2)}) copy-start(bf16[1152,256]{1,0:T(8,128)(2,1)S(1)} %collective-permute-done.11.refs_14_) | copy-start | bytes 1769476
  64.3 17.1 %collective-permute-start.13 = (bf16[1152,256]{1,0:T(8,128)(2,1)}, bf16[1152,256]{1,0:T(8,128)(2,1)S(1)}, u32[]{:S(2)}, u32[]{:S(2)}) collective-permute-start(bf16[1152,256]{1,0:T(8,128)(2,1)} %collective-permute-done.9.refs_12_), channel_id=1, source_target_pairs={{0,64},{64,128},{128,192},{192,0},{1,65},{65,129},{129,193},{193,1... | collective-permute-start | bytes 1769480 | tf_op jit(solution)/shard_map/ppermute | solution.py:247
  64.3 17.2 %collective-permute-start.14 = (bf16[1152,256]{1,0:T(8,128)(2,1)}, bf16[1152,256]{1,0:T(8,128)(2,1)}, u32[]{:S(2)}, u32[]{:S(2)}) collective-permute-start(bf16[1152,256]{1,0:T(8,128)(2,1)} %collective-permute-done.9.refs_12_), channel_id=1, source_target_pairs={{0,192},{64,0},{128,64},{192,128},{1,193},{65,1},{129,65},{193,129... | collective-permute-start | bytes 1769480 | tf_op jit(solution)/shard_map/ppermute | solution.py:250
  67.5 13.9 %collective-permute-start.12 = (bf16[1152,256]{1,0:T(8,128)(2,1)S(1)}, bf16[1152,256]{1,0:T(8,128)(2,1)}, u32[]{:S(2)}, u32[]{:S(2)}) collective-permute-start(bf16[1152,256]{1,0:T(8,128)(2,1)S(1)} %constant_dynamic-update-slice_fusion.refs_23_), channel_id=1, source_target_pairs={{0,16},{16,32},{32,48},{48,0},{1,17},{17,33},{33,49},{49,1},{2,18}... | collective-permute-start | bytes 1769480 | tf_op jit(solution)/shard_map/ppermute | solution.py:244
  81.4 5.6 %copy-start.6 = (bf16[1152,256]{1,0:T(8,128)(2,1)}, bf16[1152,256]{1,0:T(8,128)(2,1)S(1)}, u32[]{:S(2)}) copy-start(bf16[1152,256]{1,0:T(8,128)(2,1)S(1)} %collective-permute-done.13.refs_16_) | copy-start | bytes 1769476
  81.5 16.6 %collective-permute-start.17 = (bf16[1152,256]{1,0:T(8,128)(2,1)}, bf16[1152,256]{1,0:T(8,128)(2,1)S(1)}, u32[]{:S(2)}, u32[]{:S(2)}) collective-permute-start(bf16[1152,256]{1,0:T(8,128)(2,1)} %collective-permute-done.12.refs_15_), channel_id=1, source_target_pairs={{0,16},{16,32},{32,48},{48,0},{1,17},{17,33},{33,49},{49,1},{2,18}... | collective-permute-start | bytes 1769480 | tf_op jit(solution)/shard_map/ppermute | solution.py:244
  82.6 15.4 %collective-permute-start.18 = (bf16[576,256]{1,0:T(8,128)(2,1)S(1)}, bf16[576,256]{1,0:T(8,128)(2,1)S(1)}, u32[]{:S(2)}, u32[]{:S(2)}) collective-permute-start(bf16[576,256]{1,0:T(8,128)(2,1)S(1)} %slice.39), channel_id=1, source_target_pairs={{0,64},{64,128},{128,192},{192,0},{1,65},{65,129},{129,193},{193,1... | collective-permute-start | bytes 884744 | tf_op jit(solution)/shard_map/ppermute | solution.py:247
  83.7 14.3 %collective-permute-start.19 = (bf16[576,256]{1,0:T(8,128)(2,1)S(1)}, bf16[576,256]{1,0:T(8,128)(2,1)S(1)}, u32[]{:S(2)}, u32[]{:S(2)}) collective-permute-start(bf16[576,256]{1,0:T(8,128)(2,1)S(1)} %slice.40), channel_id=1, source_target_pairs={{0,192},{64,0},{128,64},{192,128},{1,193},{65,1},{129,65},{193,129... | collective-permute-start | bytes 884744 | tf_op jit(solution)/shard_map/ppermute | solution.py:250
  98.0 1.7 %copy-start = (f32[2,2,640,256]{3,2,1,0:T(8,128)S(1)}, f32[2,2,640,256]{3,2,1,0:T(8,128)}, u32[]{:S(2)}) copy-start(f32[2,2,640,256]{3,2,1,0:T(8,128)} %get-tuple-element.57.acc_ref) | copy-start | bytes 7864324
  99.8 8.8 %copy-start.1 = (f32[2,1,640,256]{3,2,1,0:T(8,128)S(1)}, f32[2,1,640,256]{3,2,1,0:T(8,128)}, u32[]{:S(2)}) copy-start(f32[2,1,640,256]{3,2,1,0:T(8,128)} %get-tuple-element.55.acc_ref) | copy-start | bytes 3932164
  101.6 11.7 %collective-permute-start.20 = (bf16[2,144,128]{2,1,0:T(8,128)(2,1)S(1)}, bf16[2,144,128]{2,1,0:T(8,128)(2,1)S(1)}, u32[]{:S(2)}, u32[]{:S(2)}) collective-permute-start(bf16[2,144,128]{2,1,0:T(8,128)(2,1)S(1)} %get-tuple-element.60), channel_id=1, source_target_pairs={{0,16},{16,32},{32,48},{48,0},{1,17},{17,33},{33,49},{49,1},{2,18}... | collective-permute-start | bytes 221192 | tf_op jit(solution)/shard_map/ppermute | solution.py:282
  103.8 9.5 %collective-permute-start.21 = (bf16[2,144,128]{2,1,0:T(8,128)(2,1)S(1)}, bf16[2,144,128]{2,1,0:T(8,128)(2,1)S(1)}, u32[]{:S(2)}, u32[]{:S(2)}) collective-permute-start(bf16[2,144,128]{2,1,0:T(8,128)(2,1)S(1)} %get-tuple-element.60), channel_id=1, source_target_pairs={{0,32},{16,48},{32,0},{48,16},{1,33},{17,49},{33,1},{49,17},{2,34}... | collective-permute-start | bytes 221192 | tf_op jit(solution)/shard_map/ppermute | solution.py:282
  105.7 7.6 %collective-permute-start.22 = (bf16[2,144,128]{2,1,0:T(8,128)(2,1)S(1)}, bf16[2,144,128]{2,1,0:T(8,128)(2,1)S(1)}, u32[]{:S(2)}, u32[]{:S(2)}) collective-permute-start(bf16[2,144,128]{2,1,0:T(8,128)(2,1)S(1)} %get-tuple-element.60), channel_id=1, source_target_pairs={{0,48},{16,0},{32,16},{48,32},{1,49},{17,1},{33,17},{49,33},{2,50}... | collective-permute-start | bytes 221192 | tf_op jit(solution)/shard_map/ppermute | solution.py:282
  113.5 6.4 %collective-permute-start.23 = (bf16[2,144,128]{2,1,0:T(8,128)(2,1)S(1)}, bf16[2,144,128]{2,1,0:T(8,128)(2,1)S(1)}, u32[]{:S(2)}, u32[]{:S(2)}) collective-permute-start(bf16[2,144,128]{2,1,0:T(8,128)(2,1)S(1)} %get-tuple-element.69), channel_id=1, source_target_pairs={{0,64},{64,128},{128,192},{192,0},{1,65},{65,129},{129,193},{193,1... | collective-permute-start | bytes 221192 | tf_op jit(solution)/shard_map/ppermute | solution.py:287
  113.6 6.3 %collective-permute-start.24 = (bf16[2,144,128]{2,1,0:T(8,128)(2,1)S(1)}, bf16[2,144,128]{2,1,0:T(8,128)(2,1)S(1)}, u32[]{:S(2)}, u32[]{:S(2)}) collective-permute-start(bf16[2,144,128]{2,1,0:T(8,128)(2,1)S(1)} %get-tuple-element.69), channel_id=1, source_target_pairs={{0,128},{64,192},{128,0},{192,64},{1,129},{65,193},{129,1},{193,65... | collective-permute-start | bytes 221192 | tf_op jit(solution)/shard_map/ppermute | solution.py:287
  115.1 5.7 %collective-permute-start.25 = (bf16[2,144,128]{2,1,0:T(8,128)(2,1)S(1)}, bf16[2,144,128]{2,1,0:T(8,128)(2,1)S(1)}, u32[]{:S(2)}, u32[]{:S(2)}) collective-permute-start(bf16[2,144,128]{2,1,0:T(8,128)(2,1)S(1)} %get-tuple-element.69), channel_id=1, source_target_pairs={{0,192},{64,0},{128,64},{192,128},{1,193},{65,1},{129,65},{193,129... | collective-permute-start | bytes 221192 | tf_op jit(solution)/shard_map/ppermute | solution.py:287
  123.7 1.3 collective-permute-start.26
  123.8 16.5 %copy-start.10 = (f32[512]{0:T(512)S(1)}, f32[512]{0:T(512)}, u32[]{:S(2)}) copy-start(f32[512]{0:T(512)} %param.7) | copy-start | bytes 6148
  125.0 15.3 %collective-permute-start.27 = (f32[640,256]{1,0:T(8,128)S(1)}, f32[640,256]{1,0:T(8,128)S(1)}, u32[]{:S(2)}, u32[]{:S(2)}) collective-permute-start(f32[640,256]{1,0:T(8,128)S(1)} %get-tuple-element.72), channel_id=1, source_target_pairs={{0,8},{8,0},{1,9},{9,1},{2,10},{10,2},{3,11},{11,3},{4,12},{12,4},... | collective-permute-start | bytes 1966088 | tf_op jit(solution)/shard_map/ppermute | solution.py:293
  125.1 3.6 %collective-permute-start.28 = (f32[640]{0:T(1024)S(1)}, f32[640]{0:T(1024)S(1)}, u32[]{:S(2)}, u32[]{:S(2)}) collective-permute-start(f32[640]{0:T(1024)S(1)} %add.194), channel_id=1, source_target_pairs={{0,2},{2,4},{4,6},{6,0},{1,3},{3,5},{5,7},{7,1},{8,10},{10,12},{12... | collective-permute-start | bytes 7688 | tf_op jit(solution)/shard_map/ppermute | solution.py:294
  125.3 5.1 %collective-permute-start.29 = (f32[640]{0:T(1024)S(1)}, f32[640]{0:T(1024)S(1)}, u32[]{:S(2)}, u32[]{:S(2)}) collective-permute-start(f32[640]{0:T(1024)S(1)} %add.194), channel_id=1, source_target_pairs={{0,4},{2,6},{4,0},{6,2},{1,5},{3,7},{5,1},{7,3},{8,12},{10,14},{12... | collective-permute-start | bytes 7688 | tf_op jit(solution)/shard_map/ppermute | solution.py:294
  127.9 4.8 %collective-permute-start.30 = (f32[640]{0:T(1024)S(1)}, f32[640]{0:T(1024)S(1)}, u32[]{:S(2)}, u32[]{:S(2)}) collective-permute-start(f32[640]{0:T(1024)S(1)} %add.194), channel_id=1, source_target_pairs={{0,6},{2,0},{4,2},{6,4},{1,7},{3,1},{5,3},{7,5},{8,14},{10,8},{12,... | collective-permute-start | bytes 7688 | tf_op jit(solution)/shard_map/ppermute | solution.py:294
  132.8 7.5 %collective-permute-start.31 = (f32[640]{0:T(1024)S(1)}, f32[640]{0:T(1024)S(1)}, u32[]{:S(2)}, u32[]{:S(2)}) collective-permute-start(f32[640]{0:T(1024)S(1)} %add_add_fusion), channel_id=1, source_target_pairs={{0,1},{1,0},{2,3},{3,2},{4,5},{5,4},{6,7},{7,6},{8,9},{9,8},{10,11... | collective-permute-start | bytes 7688 | tf_op jit(solution)/shard_map/ppermute | solution.py:295
